TPU v7x, 128 devices: a whole 4x4x4 slice. The times are simulated.
128 devices in a mesh: row: 32 (over y, x, core), col: 4 (over z).
Axes of the slice: x: 4, y: 4, z: 4, core: 2. Of those that a mesh axis runs over, the one named last changes fastest.
Arguments:
- integrals: bfloat16 [32768, 4096], P('row', 'col'), may hold values from -6 to 6
- amplitudes: bfloat16 [4096, 6144], P('row', 'col'), may hold values from -0.25 to 0.25
- screen: int32 [32, 48], P('row', 'col'), may hold values from 0 to 1, as said below
- next_owner: int32 [256], replicated, may hold values from 0 to 31, as said below
Outputs:
- regrouped: bfloat16 [32768, 6144], P('row', 'col')
Inputs may be any that keep to these rules, and one draw needn't show every extreme that they name: In each aligned block of 1 x 12 tiles of screen (one device's block), between 1 and 2 entries are 1; some block holds exactly 2. next_owner[p * 8 + s] equals p XOR m_s, where m_s (0 to 31) depends only on s.
All inputs are finite; a program needn't handle non-finite values.
Results may differ from a plain program's by a relative error of at most 0.001.
Values may be sent and summed in bfloat16 or wider, within the bound.
No kernel may reach another device: no remote copies, remote signals or barrier semaphores. Data moves between devices by JAX's collectives and lax.ppermute only.
A program may use at most 128 MiB of HBM per device.

v0:
```python
import jax
import jax.numpy as jnp
from jax import lax
from jax.sharding import PartitionSpec as P

TILE = 128


def swapped(value, axis, bit):
    mask = 2**bit
    pairs = [(source, source ^ mask) for source in range(lax.axis_size(axis))]
    return lax.ppermute(value, axis, pairs)


def body(integrals, amplitudes, screen, next_owner):
    row_count = integrals.shape[0]
    depth_local = screen.shape[0]
    width_local = screen.shape[1]
    col_width = width_local * TILE
    rows_local = row_count // TILE
    moves = next_owner[:rows_local]
    bit_count = lax.axis_size("row").bit_length() - 1
    gathered = lax.all_gather(integrals, "col", axis=1, tiled=True)
    tile_flags = screen.astype(jnp.bfloat16)
    blocked = (
        amplitudes.reshape(depth_local, TILE, width_local, TILE) * tile_flags[:, None, :, None]
    )
    masked = blocked.reshape(depth_local * TILE, col_width)
    product = jnp.dot(
        gathered,
        lax.all_gather(masked, "row", axis=0, tiled=True),
        preferred_element_type=jnp.float32,
    )
    residual = product.astype(jnp.bfloat16)
    holding = residual.reshape(rows_local, TILE, col_width)
    for place_bit in range(bit_count):
        partner = swapped(holding, "row", place_bit)
        flipped = moves >> place_bit & 1 == 1
        holding = jnp.where(flipped[:, None, None], partner, holding)
    residual = holding.reshape(row_count, col_width)
    return residual


def solution(mesh):
    placed = (P("row", "col"), P("row", "col"), P("row", "col"), P())
    return jax.shard_map(
        body, mesh=mesh, in_specs=placed, out_specs=P("row", "col"), check_vma=False
    )
```

profile of v0, /device:TPU:0, one launch (start us, length us, event | category | flops | bytes accessed | tf_op | source)
XLA Modules:
  0.0 474.5 jit_solution(4046517192232543873)
XLA Ops:
  6.5 0.0 all-gather.5.cloned.1.call-start
  6.5 0.7 all-gather.5.cloned.1.call-update
  7.3 0.0 all-gather.3.cloned.1.call-start
  7.3 0.7 convert_bitcast_fusion
  8.0 0.1 broadcast_bitcast_fusion
  8.0 1.8 broadcast_multiply_fusion
  9.8 0.0 all-gather.3.cloned.1.call-update
  9.8 0.0 copy-start
  9.8 85.0 %all-gather.5.cloned.1.call-done = bf16[1024,4096]{1,0:T(8,128)(2,1)} async-done(((bf16[1024,1024]{1,0:T(8,128)(2,1)}), bf16[1024,4096]{1,0:T(8,128)(2,1)}) %all-gather.5.cloned.1.call-update) | async-done | bytes 8388624 | tf_op jit(solution)/shard_map/all_gather | solution.py:23
  94.8 65.9 %all-gather.3.cloned.1.call-done = bf16[4096,1536]{1,0:T(8,128)(2,1)} async-done(((bf16[128,1536]{1,0:T(8,128)(2,1)}), bf16[4096,1536]{1,0:T(8,128)(2,1)}) %all-gather.3.cloned.1.call-update) | async-done | bytes 12582928 | tf_op jit(solution)/shard_map/all_gather | solution.py:31
  160.7 18.2 %convolution_convert_fusion = bf16[1536,1024]{0,1:T(8,128)(2,1)S(1)} fusion(bf16[1024,4096]{1,0:T(8,128)(2,1)} %all-gather.5.cloned.1.call-done, bf16[4096,1536]{1,0:T(8,128)(2,1)} %all-gather.3.cloned.1.call-done), kind=kOutput, calls=%fused_computation | convolution fusion | flops 12886474752 | bytes 24117248 | tf_op jit(solution)/shard_map/dot_general | solution.py:29
  178.9 0.4 collective-permute-start
  179.3 0.0 copy-done
  179.3 5.3 %collective-permute-done = bf16[8,128,1536]{2,1,0:T(8,128)(2,1)S(1)} collective-permute-done((bf16[8,128,1536]{2,1,0:T(8,128)(2,1)S(1)}, bf16[8,128,1536]{2,1,0:T(8,128)(2,1)S(1)}, u32[]{:S(2)}, u32[]{:S(2)}) %collective-permute-start) | collective-permute-done | bytes 3145760 | tf_op jit(solution)/shard_map/ppermute | solution.py:12
  184.6 0.4 broadcast_select_fusion
  185.0 1.5 collective-permute-start.1
  186.6 68.8 %collective-permute-done.1 = bf16[8,128,1536]{2,1,0:T(8,128)(2,1)S(1)} collective-permute-done((bf16[8,128,1536]{2,1,0:T(8,128)(2,1)S(1)}, bf16[8,128,1536]{2,1,0:T(8,128)(2,1)S(1)}, u32[]{:S(2)}, u32[]{:S(2)}) %collective-permute-start.1) | collective-permute-done | bytes 3145760 | tf_op jit(solution)/shard_map/ppermute | solution.py:12
  255.4 0.4 broadcast_select_fusion.1
  255.8 3.1 collective-permute-start.2
  258.9 68.0 %collective-permute-done.2 = bf16[8,128,1536]{2,1,0:T(8,128)(2,1)S(1)} collective-permute-done((bf16[8,128,1536]{2,1,0:T(8,128)(2,1)S(1)}, bf16[8,128,1536]{2,1,0:T(8,128)(2,1)S(1)}, u32[]{:S(2)}, u32[]{:S(2)}) %collective-permute-start.2) | collective-permute-done | bytes 3145760 | tf_op jit(solution)/shard_map/ppermute | solution.py:12
  326.9 0.4 broadcast_select_fusion.2
  327.3 1.2 collective-permute-start.3
  328.4 67.5 %collective-permute-done.3 = bf16[8,128,1536]{2,1,0:T(8,128)(2,1)S(1)} collective-permute-done((bf16[8,128,1536]{2,1,0:T(8,128)(2,1)S(1)}, bf16[8,128,1536]{2,1,0:T(8,128)(2,1)S(1)}, u32[]{:S(2)}, u32[]{:S(2)}) %collective-permute-start.3) | collective-permute-done | bytes 3145760 | tf_op jit(solution)/shard_map/ppermute | solution.py:12
  395.9 0.4 broadcast_select_fusion.3
  396.3 2.7 collective-permute-start.4
  399.0 66.6 %collective-permute-done.4 = bf16[8,128,1536]{2,1,0:T(8,128)(2,1)S(1)} collective-permute-done((bf16[8,128,1536]{2,1,0:T(8,128)(2,1)S(1)}, bf16[8,128,1536]{2,1,0:T(8,128)(2,1)S(1)}, u32[]{:S(2)}, u32[]{:S(2)}) %collective-permute-start.4) | collective-permute-done | bytes 3145760 | tf_op jit(solution)/shard_map/ppermute | solution.py:12
  465.6 2.0 broadcast_select_fusion.4
  (1 shorter events, 0.0 us)
Async XLA Ops:
  6.5 88.3 %all-gather.5.cloned.1.call-start = ((), (), s32[]{:S(2)}) async-start(), calls=%async_computation.1 | async-start | bytes 10485760 | tf_op jit(solution)/shard_map/all_gather | solution.py:23
  7.3 153.5 %all-gather.3.cloned.1.call-start = ((), (), s32[]{:S(2)}) async-start(), calls=%async_computation | async-start | bytes 12976128 | tf_op jit(solution)/shard_map/all_gather | solution.py:31
  9.8 169.5 %copy-start = (s32[256]{0:T(256)S(1)}, s32[256]{0:T(256)}, u32[]{:S(2)}) copy-start(s32[256]{0:T(256)} %param.7) | copy-start | bytes 3076
  178.9 5.7 %collective-permute-start = (bf16[8,128,1536]{2,1,0:T(8,128)(2,1)S(1)}, bf16[8,128,1536]{2,1,0:T(8,128)(2,1)S(1)}, u32[]{:S(2)}, u32[]{:S(2)}) collective-permute-start(bf16[8,128,1536]{2,1,0:T(8,128)(2,1)S(1)} %bitcast.10), channel_id=1, source_target_pairs={{0,4},{4,0},{8,12},{12,8},{16,20},{20,16},{24,28},{28,24},{32,36},... | collective-permute-start | bytes 9437192 | tf_op jit(solution)/shard_map/ppermute | solution.py:12
  185.0 70.4 %collective-permute-start.1 = (bf16[8,128,1536]{2,1,0:T(8,128)(2,1)S(1)}, bf16[8,128,1536]{2,1,0:T(8,128)(2,1)S(1)}, u32[]{:S(2)}, u32[]{:S(2)}) collective-permute-start(bf16[8,128,1536]{2,1,0:T(8,128)(2,1)S(1)} %broadcast_select_fusion), channel_id=1, source_target_pairs={{0,8},{4,12},{8,0},{12,4},{16,24},{20,28},{24,16},{28,20},{32,40},... | collective-permute-start | bytes 9437192 | tf_op jit(solution)/shard_map/ppermute | solution.py:12
  255.8 71.1 %collective-permute-start.2 = (bf16[8,128,1536]{2,1,0:T(8,128)(2,1)S(1)}, bf16[8,128,1536]{2,1,0:T(8,128)(2,1)S(1)}, u32[]{:S(2)}, u32[]{:S(2)}) collective-permute-start(bf16[8,128,1536]{2,1,0:T(8,128)(2,1)S(1)} %broadcast_select_fusion.1), channel_id=1, source_target_pairs={{0,16},{4,20},{8,24},{12,28},{16,0},{20,4},{24,8},{28,12},{32,48},... | collective-permute-start | bytes 9437192 | tf_op jit(solution)/shard_map/ppermute | solution.py:12
  327.3 68.7 %collective-permute-start.3 = (bf16[8,128,1536]{2,1,0:T(8,128)(2,1)S(1)}, bf16[8,128,1536]{2,1,0:T(8,128)(2,1)S(1)}, u32[]{:S(2)}, u32[]{:S(2)}) collective-permute-start(bf16[8,128,1536]{2,1,0:T(8,128)(2,1)S(1)} %broadcast_select_fusion.2), channel_id=1, source_target_pairs={{0,32},{4,36},{8,40},{12,44},{16,48},{20,52},{24,56},{28,60},{32,0... | collective-permute-start | bytes 9437192 | tf_op jit(solution)/shard_map/ppermute | solution.py:12
  396.3 69.2 %collective-permute-start.4 = (bf16[8,128,1536]{2,1,0:T(8,128)(2,1)S(1)}, bf16[8,128,1536]{2,1,0:T(8,128)(2,1)S(1)}, u32[]{:S(2)}, u32[]{:S(2)}) collective-permute-start(bf16[8,128,1536]{2,1,0:T(8,128)(2,1)S(1)} %broadcast_select_fusion.3), channel_id=1, source_target_pairs={{0,64},{4,68},{8,72},{12,76},{16,80},{20,84},{24,88},{28,92},{32,9... | collective-permute-start | bytes 9437192 | tf_op jit(solution)/shard_map/ppermute | solution.py:12
Sparse Core Ops, SparseCore 0:
  9.0 85.7 all-gather.4
  97.1 63.5 all-gather.2
where the time goes:
time: 475 us; the launch traced here: 474 us
  waiting for transfers between devices  428 us (90%)
  matrix products  18.2 us (4%)
  between operations  13.4 us (3%)
  starting transfers between devices  8.86 us (2%)
  other arithmetic  6.04 us (1%)
    ppermute x5, waiting for transfers between devices, swapped(): return lax.ppermute(value, axis, pairs)  276 us
    all_gather x1, waiting for transfers between devices, body(): gathered = lax.all_gather(integrals, 'col', axis=1, tiled=True)  85 us
    all_gather x1, waiting for transfers between devices, body(): lax.all_gather(masked, 'row', axis=0, tiled=True)  65.9 us
    dot_general x1, matrix products, body(): jnp.dot(gathered, lax.all_gather(masked, 'row', axis=0, tiled=True), pref...  18.2 us
  transfers between devices with their start and end apart: 7, of which 7 were waited for; matrix products, arithmetic and copies ran while one was open for 1% of the time, Pallas kernels for 0%

commit v1 on v0

v1 whole, which is shorter than its diff:
```python
import functools

import jax
import jax.numpy as jnp
from jax import lax
from jax.experimental import pallas as pl
from jax.experimental.pallas import tpu as pltpu
from jax.sharding import PartitionSpec as P

TILE = 128
SLOTS = 8
GROUPS = ((0, 2), (2, 4), (4, 6), (6, 8))
X1, X3, Y1, Y3, CORE = 2, 6, 8, 24, 1
AXES = ("row", "col")


def exchange(value, masks):
    pairs = [(p, p ^ masks[p & 1]) for p in range(lax.axis_size("row"))]
    return lax.ppermute(value, "row", pairs)


def turn(value):
    rows, cols = lax.axis_size("row"), lax.axis_size("col")
    pairs = []
    for p in range(rows):
        step = 1 if p & 1 == 0 else -1
        for c in range(cols):
            pairs.append((p * cols + c, p * cols + (c + step) % cols))
    return lax.ppermute(value, AXES, pairs)


def need(moves, mask):
    if mask == CORE:
        return moves & 1 == 1
    shift = 1 if mask in (X1, X3) else 3
    low, high = moves >> shift & 1, moves >> (shift + 1) & 1
    return (high if mask in (X3, Y3) else low ^ high) == 1


def step(value, moves, masks, core):
    partner = exchange(value, masks)
    if masks[0] == masks[1]:
        flags = need(moves, masks[0])
    else:
        flags = jnp.where(core == 0, need(moves, masks[0]), need(moves, masks[1]))
    return jnp.where(flags[:, None, None], partner, value)


def regroup(value, moves, core):
    value = step(value, moves, (CORE, CORE), core)
    half = value.shape[0] // 2
    parts = [value[:half], value[half:]]
    order_x = [(X1, X3), (X3, X1)]
    order_y = [(Y1, Y3), (Y3, Y1)]
    orders = [order_x + order_y, order_y + order_x]
    cuts = [moves[:half], moves[half:]]
    for at in range(4):
        parts = [step(parts[i], cuts[i], orders[i][at], core) for i in range(2)]
    return jnp.concatenate(parts, axis=0)


def gather_tiles(packed, core):
    held = packed[None]
    for masks in ((X1, X3), (X3, X1), (Y1, Y3), (Y3, Y1)):
        held = jnp.concatenate([held, exchange(held, masks)], axis=0)
    return jnp.concatenate([held, exchange(held, (CORE, CORE))], axis=0)


def tile_order(me):
    k = jnp.arange(32, dtype=jnp.int32)
    delta = k ^ me
    other = delta & 1
    core = k & 1
    bit = [delta >> i & 1 for i in range(5)]
    x1, x3, y1, y3 = bit[1] ^ bit[2], bit[2], bit[3] ^ bit[4], bit[4]
    first = jnp.where(core == 0, x1 + 2 * x3 + 4 * y1 + 8 * y3, x3 + 2 * x1 + 4 * y3 + 8 * y1)
    return (first + 16 * other).astype(jnp.int32)


def product_kernel(at_ref, place_ref, base_ref, x0, x1, x2, x3, tiles_ref, *rest):
    out_ref, total = rest[-2:]
    total[...] = jnp.zeros_like(total)
    for j, x_ref in enumerate((x0, x1, x2, x3)):
        for kk in range(8):
            k = base_ref[j] * 8 + kk
            part = jnp.dot(
                x_ref[:, kk * TILE : (kk + 1) * TILE],
                tiles_ref[at_ref[k], :TILE, :],
                preferred_element_type=jnp.float32,
            )
            for i in range(2):
                where = pl.ds(pl.multiple_of(place_ref[2 * k + i] * TILE, TILE), TILE)
                total[:, where] += part[:, i * TILE : (i + 1) * TILE]
    out_ref[...] = total[...].astype(out_ref.dtype)


def product(blocks, tiles, at, place, base, out, first, rows_all):
    rows = blocks[0].shape[0]
    width = 12 * TILE
    where = first // rows
    in_specs = [pl.BlockSpec((rows, 1024), lambda i, *_: (0, 0))] * 4
    in_specs.append(pl.BlockSpec(tiles.shape, lambda i, *_: (0, 0, 0)))
    args = list(blocks) + [tiles]
    aliases = {}
    if out is not None:
        in_specs.append(pl.BlockSpec(memory_space=pl.ANY))
        args.append(out)
        aliases = {8: 0}
    return pl.pallas_call(
        product_kernel,
        grid_spec=pltpu.PrefetchScalarGridSpec(
            num_scalar_prefetch=3,
            grid=(1,),
            in_specs=in_specs,
            out_specs=pl.BlockSpec((rows, width), lambda i, *_: (where, 0)),
            scratch_shapes=[pltpu.VMEM((rows, width), jnp.float32)],
        ),
        out_shape=jax.ShapeDtypeStruct((rows_all, width), jnp.bfloat16),
        input_output_aliases=aliases,
        compiler_params=pltpu.CompilerParams(vmem_limit_bytes=40 * 2**20),
        cost_estimate=pl.CostEstimate(
            flops=rows * 4096 * 256 * 4, bytes_accessed=rows * 11264 + 2**21, transcendentals=0
        ),
    )(at, place, base, *args)


def body(integrals, amplitudes, screen, next_owner):
    me = lax.axis_index("row").astype(jnp.int32)
    col = lax.axis_index("col").astype(jnp.int32)
    core = me & 1
    moves = next_owner[:SLOTS]

    flags = screen[0] == 1
    spots = jnp.arange(12, dtype=jnp.int32)
    first = jnp.min(jnp.where(flags, spots, 11))
    second = jnp.max(jnp.where(flags, spots, 0))
    both = first != second
    one = lax.dynamic_slice(amplitudes, (0, first * TILE), (TILE, TILE))
    two = lax.dynamic_slice(amplitudes, (0, second * TILE), (TILE, TILE))
    two = jnp.where(both, two, jnp.zeros_like(two))
    live = jnp.concatenate([one, two], axis=1)
    spot = jnp.concatenate(
        [jnp.full((16, TILE), first, jnp.int32), jnp.full((16, TILE), second, jnp.int32)], axis=1
    ).astype(jnp.bfloat16)
    tiles = gather_tiles(jnp.concatenate([live, spot], axis=0), core)
    at = tile_order(me)
    place = tiles[:, TILE, :].reshape(32, 2, TILE)[:, :, 0].astype(jnp.int32)
    place = place[at].reshape(64)
    sign = 1 - 2 * core
    base = (col - sign * jnp.arange(4, dtype=jnp.int32)) & 3

    slots = integrals.reshape(SLOTS, TILE, 1024)
    out = None
    for low, high in GROUPS:
        held = regroup(slots[low:high], moves[low:high], core).reshape((high - low) * TILE, 1024)
        blocks = [held]
        for _ in range(3):
            blocks.append(turn(blocks[-1]))
        out = product(blocks, tiles, at, place, base, out, low * TILE, 1024)
    return out


def solution(mesh):
    placed = (P("row", "col"), P("row", "col"), P("row", "col"), P())
    return jax.shard_map(
        body, mesh=mesh, in_specs=placed, out_specs=P("row", "col"), check_vma=False
    )
```

time: 475 us -> 189 us (0.40)
  waiting for transfers between devices: 428 us -> 65.3 us
  starting transfers between devices: 8.86 us -> 57.1 us
  Pallas kernels: 0 us -> 20.1 us
  matrix products: 18.2 us -> 0 us
  local copies, waits for them, and re-layouts: 0.08 us -> 11.5 us
  between operations: 13.4 us -> 23.9 us
    ppermute x5 -> x53, waiting for transfers between devices: 276 us -> 65.3 us  [the longest x12 46.3 us: turn(): return lax.ppermute(value, AXES, pairs)]
    all_gather x2 -> x0, waiting for transfers between devices: 151 us -> none  [the longest x1 85 us: body(): gathered = lax.all_gather(integrals, 'col', axis=1, tiled=True)]
    ppermute x5 -> x53, starting transfers between devices: 8.82 us -> 57.1 us  [the longest x41 49 us: exchange(): return lax.ppermute(value, 'row', pairs)]
    pallas_call x0 -> x4, Pallas kernels: none -> 20.1 us  [product(): pl.pallas_call(product_kernel, grid_spec=pltpu.PrefetchScalarGridSpec(num...]
    dot_general x1 -> x0, matrix products: 18.2 us -> none  [body(): jnp.dot(gathered, lax.all_gather(masked, 'row', axis=0, tiled=True), pref...]
    unnamed x2 -> x26, local copies, waits for them, and re-layouts: 0.01 us -> 4.86 us
  transfers between devices with their start and end apart: 7 -> 53, of which waited for: 7 -> 28; matrix products, arithmetic and copies ran while one was open for 1% -> 10% of each run, Pallas kernels for 0% -> 8%
where the time goes in v1:
time: 189 us; the launch traced here: 188 us
  waiting for transfers between devices  65.3 us (35%)
  starting transfers between devices  57.1 us (30%)
  between operations  23.9 us (13%)
  Pallas kernels  20.1 us (11%)
  local copies, waits for them, and re-layouts  11.5 us (6%)
  other arithmetic  9.64 us (5%)
    ppermute x41, starting transfers between devices, exchange(): return lax.ppermute(value, 'row', pairs)  49 us
    ppermute x12, waiting for transfers between devices, turn(): return lax.ppermute(value, AXES, pairs)  46.3 us
    pallas_call x4, Pallas kernels, product(): pl.pallas_call(product_kernel, grid_spec=pltpu.PrefetchScalarGridSpec(num...  20.1 us
    ppermute x41, waiting for transfers between devices, exchange(): return lax.ppermute(value, 'row', pairs)  19 us
    ppermute x12, starting transfers between devices, turn(): return lax.ppermute(value, AXES, pairs)  8.13 us
    unnamed x26, local copies, waits for them, and re-layouts  4.86 us
    select_n x30, other arithmetic, step(): return jnp.where(flags[:, None, None], partner, value)  4.11 us
  transfers between devices with their start and end apart: 53, of which 28 were waited for; matrix products, arithmetic and copies ran while one was open for 10% of the time, Pallas kernels for 8%

profile of v1, /device:TPU:0, one launch (start us, length us, event | category | flops | bytes accessed | tf_op | source)
XLA Modules:
  0.0 187.6 jit_solution(14859358285776843233)
XLA Ops:
  5.9 1.6 collective-permute-start
  7.5 2.8 %fusion.5 = (bf16[256,1024]{1,0:T(8,128)(2,1)}, bf16[256,1024]{1,0:T(8,128)(2,1)S(1)}, bf16[256,1024]{1,0:T(8,128)(2,1)S(1)}, bf16[256,1024]{1,0:T(8,128)(2,1)}) fusion(bf16[1024,1024]{1,0:T(8,128)(2,1)} %param.4), kind=kLoop, calls=%fused_computation.76 | loop fusion | bytes 4194304 | tf_op jit(solution)/shard_map/slice | solution.py:155
  11.7 1.9 collective-permute-start.1
  14.8 3.3 %collective-permute-done.1 = bf16[2,144,256]{2,1,0:T(8,128)(2,1)S(1)} collective-permute-done((bf16[2,144,256]{2,1,0:T(8,128)(2,1)S(1)}, bf16[2,144,256]{2,1,0:T(8,128)(2,1)S(1)}, u32[]{:S(2)}, u32[]{:S(2)}) %collective-permute-start.1) | collective-permute-done | bytes 147488 | tf_op jit(solution)/shard_map/ppermute | solution.py:19
  18.9 1.6 collective-permute-start.2
  40.8 1.5 constant_dynamic-update-slice_fusion.3
  44.1 2.2 %collective-permute-start.3 = (bf16[8,144,256]{2,1,0:T(8,128)(2,1)S(1)}, bf16[8,144,256]{2,1,0:T(8,128)(2,1)S(1)}, u32[]{:S(2)}, u32[]{:S(2)}) collective-permute-start(bf16[8,144,256]{2,1,0:T(8,128)(2,1)S(1)} %pad_maximum_fusion), channel_id=1, source_target_pairs={{0,96},{4,36},{8,104},{12,44},{16,112},{20,52},{24,120},{28,60},{3... | collective-permute-start | bytes 1769480 | tf_op jit(solution)/shard_map/ppermute | solution.py:19
  46.3 1.7 constant_dynamic-update-slice_fusion.1
  48.1 1.7 broadcast_select_fusion
  50.7 2.0 %collective-permute-start.30 = (bf16[1,128,1024]{2,1,0:T(8,128)(2,1)S(1)}, bf16[1,128,1024]{2,1,0:T(8,128)(2,1)S(1)}, u32[]{:S(2)}, u32[]{:S(2)}) collective-permute-start(bf16[1,128,1024]{2,1,0:T(8,128)(2,1)S(1)} %get-tuple-element.19), channel_id=1, source_target_pairs={{0,8},{4,28},{8,0},{12,20},{16,24},{20,12},{24,16},{28,4},{32,40},... | collective-permute-start | bytes 786440 | tf_op jit(solution)/shard_map/ppermute | solution.py:19
  54.1 1.4 broadcast_select_fusion.2
  57.1 2.0 %collective-permute-done.30 = bf16[1,128,1024]{2,1,0:T(8,128)(2,1)S(1)} collective-permute-done((bf16[1,128,1024]{2,1,0:T(8,128)(2,1)S(1)}, bf16[1,128,1024]{2,1,0:T(8,128)(2,1)S(1)}, u32[]{:S(2)}, u32[]{:S(2)}) %collective-permute-start.30) | collective-permute-done | bytes 262176 | tf_op jit(solution)/shard_map/ppermute | solution.py:19
  61.2 1.5 collective-permute-done.18
  62.7 1.8 collective-permute-start.43
  65.6 1.7 collective-permute-start.31
  67.3 2.0 %collective-permute-start.35 = (bf16[1,128,1024]{2,1,0:T(8,128)(2,1)S(1)}, bf16[1,128,1024]{2,1,0:T(8,128)(2,1)S(1)}, u32[]{:S(2)}, u32[]{:S(2)}) collective-permute-start(bf16[1,128,1024]{2,1,0:T(8,128)(2,1)S(1)} %get-tuple-element.18), channel_id=1, source_target_pairs={{0,96},{4,36},{8,104},{12,44},{16,112},{20,52},{24,120},{28,60},{3... | collective-permute-start | bytes 786440 | tf_op jit(solution)/shard_map/ppermute | solution.py:19
  70.2 1.8 collective-permute-start.19
  72.1 2.1 %collective-permute-start.23 = (bf16[1,128,1024]{2,1,0:T(8,128)(2,1)S(1)}, bf16[1,128,1024]{2,1,0:T(8,128)(2,1)S(1)}, u32[]{:S(2)}, u32[]{:S(2)}) collective-permute-start(bf16[1,128,1024]{2,1,0:T(8,128)(2,1)S(1)} %get-tuple-element.22), channel_id=1, source_target_pairs={{0,96},{4,36},{8,104},{12,44},{16,112},{20,52},{24,120},{28,60},{3... | collective-permute-start | bytes 786440 | tf_op jit(solution)/shard_map/ppermute | solution.py:19
  74.2 1.5 collective-permute-start.7
  78.5 1.8 collective-permute-done.23
  80.6 2.5 %collective-permute-done.7 = bf16[1,128,1024]{2,1,0:T(8,128)(2,1)S(1)} collective-permute-done((bf16[1,128,1024]{2,1,0:T(8,128)(2,1)S(1)}, bf16[1,128,1024]{2,1,0:T(8,128)(2,1)S(1)}, u32[]{:S(2)}, u32[]{:S(2)}) %collective-permute-start.7) | collective-permute-done | bytes 262176 | tf_op jit(solution)/shard_map/ppermute | solution.py:19
  83.2 3.2 %collective-permute-done.11 = bf16[1,128,1024]{2,1,0:T(8,128)(2,1)S(1)} collective-permute-done((bf16[1,128,1024]{2,1,0:T(8,128)(2,1)S(1)}, bf16[1,128,1024]{2,1,0:T(8,128)(2,1)S(1)}, u32[]{:S(2)}, u32[]{:S(2)}) %collective-permute-start.11) | collective-permute-done | bytes 262176 | tf_op jit(solution)/shard_map/ppermute | solution.py:19
  86.4 1.5 collective-permute-start.36
  89.5 2.1 %collective-permute-start.8 = (bf16[1,128,1024]{2,1,0:T(8,128)(2,1)S(1)}, bf16[1,128,1024]{2,1,0:T(8,128)(2,1)S(1)}, u32[]{:S(2)}, u32[]{:S(2)}) collective-permute-start(bf16[1,128,1024]{2,1,0:T(8,128)(2,1)S(1)} %broadcast_select_fusion.33), channel_id=1, source_target_pairs={{0,32},{4,100},{8,40},{12,108},{16,48},{20,116},{24,56},{28,124},{... | collective-permute-start | bytes 786440 | tf_op jit(solution)/shard_map/ppermute | solution.py:19
  91.6 1.6 collective-permute-start.12
  95.5 1.8 collective-permute-start.49
  97.7 2.3 %collective-permute-start.33 = (bf16[1,128,1024]{2,1,0:T(8,128)(2,1)S(1)}, bf16[1,128,1024]{2,1,0:T(8,128)(2,1)S(1)}, u32[]{:S(2)}, u32[]{:S(2)}) collective-permute-start(bf16[1,128,1024]{2,1,0:T(8,128)(2,1)S(1)} %broadcast_select_fusion.18), channel_id=1, source_target_pairs={{0,96},{4,36},{8,104},{12,44},{16,112},{20,52},{24,120},{28,60},{3... | collective-permute-start | bytes 786440 | tf_op jit(solution)/shard_map/ppermute | solution.py:19
  100.0 1.4 collective-permute-start.37
  101.9 1.6 collective-permute-start.21
  103.6 2.2 %collective-permute-start.25 = (bf16[1,128,1024]{2,1,0:T(8,128)(2,1)S(1)}, bf16[1,128,1024]{2,1,0:T(8,128)(2,1)S(1)}, u32[]{:S(2)}, u32[]{:S(2)}) collective-permute-start(bf16[1,128,1024]{2,1,0:T(8,128)(2,1)S(1)} %broadcast_select_fusion.22), channel_id=1, source_target_pairs={{0,24},{4,12},{8,16},{12,4},{16,8},{20,28},{24,0},{28,20},{32,56},... | collective-permute-start | bytes 786440 | tf_op jit(solution)/shard_map/ppermute | solution.py:19
  105.8 1.8 collective-permute-start.9
  109.5 2.0 %collective-permute-start.50 = (bf16[256,1024]{1,0:T(8,128)(2,1)S(1)}, bf16[256,1024]{1,0:T(8,128)(2,1)}, u32[]{:S(2)}, u32[]{:S(2)}) collective-permute-start(bf16[256,1024]{1,0:T(8,128)(2,1)S(1)} %bitcast.62), channel_id=1, source_target_pairs={{0,1},{1,2},{2,3},{3,0},{4,7},{5,4},{6,5},{7,6},{8,9},{9,10},{10,1... | collective-permute-start | bytes 1572872 | tf_op jit(solution)/shard_map/ppermute | solution.py:29
  111.6 2.0 %collective-permute-start.38 = (bf16[256,1024]{1,0:T(8,128)(2,1)S(1)}, bf16[256,1024]{1,0:T(8,128)(2,1)}, u32[]{:S(2)}, u32[]{:S(2)}) collective-permute-start(bf16[256,1024]{1,0:T(8,128)(2,1)S(1)} %bitcast.60), channel_id=1, source_target_pairs={{0,1},{1,2},{2,3},{3,0},{4,7},{5,4},{6,5},{7,6},{8,9},{9,10},{10,1... | collective-permute-start | bytes 1572872 | tf_op jit(solution)/shard_map/ppermute | solution.py:29
  113.7 1.6 collective-permute-start.26
  115.5 1.9 %collective-permute-start.14 = (bf16[256,1024]{1,0:T(8,128)(2,1)S(1)}, bf16[256,1024]{1,0:T(8,128)(2,1)}, u32[]{:S(2)}, u32[]{:S(2)}) collective-permute-start(bf16[256,1024]{1,0:T(8,128)(2,1)S(1)} %bitcast.66), channel_id=1, source_target_pairs={{0,1},{1,2},{2,3},{3,0},{4,7},{5,4},{6,5},{7,6},{8,9},{9,10},{10,1... | collective-permute-start | bytes 1572872 | tf_op jit(solution)/shard_map/ppermute | solution.py:29
  118.2 2.5 %collective-permute-done.50.x1 = bf16[256,1024]{1,0:T(8,128)(2,1)} collective-permute-done((bf16[256,1024]{1,0:T(8,128)(2,1)S(1)}, bf16[256,1024]{1,0:T(8,128)(2,1)}, u32[]{:S(2)}, u32[]{:S(2)}) %collective-permute-start.50) | collective-permute-done | bytes 524320 | tf_op jit(solution)/shard_map/ppermute | solution.py:29
  120.8 5.6 %collective-permute-done.38.x1 = bf16[256,1024]{1,0:T(8,128)(2,1)} collective-permute-done((bf16[256,1024]{1,0:T(8,128)(2,1)S(1)}, bf16[256,1024]{1,0:T(8,128)(2,1)}, u32[]{:S(2)}, u32[]{:S(2)}) %collective-permute-start.38) | collective-permute-done | bytes 524320 | tf_op jit(solution)/shard_map/ppermute | solution.py:29
  126.5 5.5 %collective-permute-done.26.x1 = bf16[256,1024]{1,0:T(8,128)(2,1)} collective-permute-done((bf16[256,1024]{1,0:T(8,128)(2,1)S(1)}, bf16[256,1024]{1,0:T(8,128)(2,1)}, u32[]{:S(2)}, u32[]{:S(2)}) %collective-permute-start.26) | collective-permute-done | bytes 524320 | tf_op jit(solution)/shard_map/ppermute | solution.py:29
  132.1 5.5 %collective-permute-done.14.x1 = bf16[256,1024]{1,0:T(8,128)(2,1)} collective-permute-done((bf16[256,1024]{1,0:T(8,128)(2,1)S(1)}, bf16[256,1024]{1,0:T(8,128)(2,1)}, u32[]{:S(2)}, u32[]{:S(2)}) %collective-permute-start.14) | collective-permute-done | bytes 524320 | tf_op jit(solution)/shard_map/ppermute | solution.py:29
  137.7 5.5 %collective-permute-done.51.x2 = bf16[256,1024]{1,0:T(8,128)(2,1)} collective-permute-done((bf16[256,1024]{1,0:T(8,128)(2,1)}, bf16[256,1024]{1,0:T(8,128)(2,1)}, u32[]{:S(2)}, u32[]{:S(2)}) %collective-permute-start.51) | collective-permute-done | bytes 524320 | tf_op jit(solution)/shard_map/ppermute | solution.py:29
  143.3 5.5 %collective-permute-done.39.x2 = bf16[256,1024]{1,0:T(8,128)(2,1)} collective-permute-done((bf16[256,1024]{1,0:T(8,128)(2,1)}, bf16[256,1024]{1,0:T(8,128)(2,1)}, u32[]{:S(2)}, u32[]{:S(2)}) %collective-permute-start.39) | collective-permute-done | bytes 524320 | tf_op jit(solution)/shard_map/ppermute | solution.py:29
  150.3 4.2 %collective-permute-done.27.x2 = bf16[256,1024]{1,0:T(8,128)(2,1)} collective-permute-done((bf16[256,1024]{1,0:T(8,128)(2,1)}, bf16[256,1024]{1,0:T(8,128)(2,1)}, u32[]{:S(2)}, u32[]{:S(2)}) %collective-permute-start.27) | collective-permute-done | bytes 524320 | tf_op jit(solution)/shard_map/ppermute | solution.py:29
  154.7 5.3 %collective-permute-done.15.x2 = bf16[256,1024]{1,0:T(8,128)(2,1)} collective-permute-done((bf16[256,1024]{1,0:T(8,128)(2,1)}, bf16[256,1024]{1,0:T(8,128)(2,1)}, u32[]{:S(2)}, u32[]{:S(2)}) %collective-permute-start.15) | collective-permute-done | bytes 524320 | tf_op jit(solution)/shard_map/ppermute | solution.py:29
  160.9 4.8 %collective-permute-done.52.x3 = bf16[256,1024]{1,0:T(8,128)(2,1)} collective-permute-done((bf16[256,1024]{1,0:T(8,128)(2,1)}, bf16[256,1024]{1,0:T(8,128)(2,1)}, u32[]{:S(2)}, u32[]{:S(2)}) %collective-permute-start.52) | collective-permute-done | bytes 524320 | tf_op jit(solution)/shard_map/ppermute | solution.py:29
  165.7 5.0 %shard_map.46.rest_0_ = bf16[1024,1536]{1,0:T(8,128)(2,1)} custom-call(s32[32]{0:T(128)S(1)} %fusion.at_ref, s32[64]{0:T(128)S(1)} %reshape.228.place_ref, s32[4]{0:T(128)S(1)} %subtract_and_fusion.base_ref, bf16[256,1024]{1,0:T(8,128)(2,1)S(1)} %bitcast.63, bf16[256,1024]{1,0:T(8,128)(2,1)} %collective-permute-done.50.x1, ...), custom_call_target="tpu_custom_call" | custom-call | flops 1073741824 | bytes 4980736 | tf_op jit(solution)/shard_map/pallas_call | solution.py:109
  171.3 5.0 %shard_map.47.rest_0_ = bf16[1024,1536]{1,0:T(8,128)(2,1)} custom-call(s32[32]{0:T(128)S(1)} %fusion.at_ref, s32[64]{0:T(128)S(1)} %reshape.228.place_ref, s32[4]{0:T(128)S(1)} %subtract_and_fusion.base_ref, bf16[256,1024]{1,0:T(8,128)(2,1)S(1)} %bitcast.61, bf16[256,1024]{1,0:T(8,128)(2,1)} %collective-permute-done.38.x1, ...), custom_call_target="tpu_custom_call", output_to_operand_aliasing={{}: (8, {})} | custom-call | flops 1073741824 | bytes 4980736 | tf_op jit(solution)/shard_map/pallas_call | solution.py:109
  176.9 5.0 %shard_map.48.rest_0_ = bf16[1024,1536]{1,0:T(8,128)(2,1)} custom-call(s32[32]{0:T(128)S(1)} %fusion.at_ref, s32[64]{0:T(128)S(1)} %reshape.228.place_ref, s32[4]{0:T(128)S(1)} %subtract_and_fusion.base_ref, bf16[256,1024]{1,0:T(8,128)(2,1)S(1)} %bitcast.65, bf16[256,1024]{1,0:T(8,128)(2,1)} %collective-permute-done.26.x1, ...), custom_call_target="tpu_custom_call", output_to_operand_aliasing={{}: (8, {})} | custom-call | flops 1073741824 | bytes 4980736 | tf_op jit(solution)/shard_map/pallas_call | solution.py:109
  182.6 5.0 %shard_map.49 = bf16[1024,1536]{1,0:T(8,128)(2,1)} custom-call(s32[32]{0:T(128)S(1)} %fusion.at_ref, s32[64]{0:T(128)S(1)} %reshape.228.place_ref, s32[4]{0:T(128)S(1)} %subtract_and_fusion.base_ref, bf16[256,1024]{1,0:T(8,128)(2,1)S(1)} %bitcast.67, bf16[256,1024]{1,0:T(8,128)(2,1)} %collective-permute-done.14.x1, ...), custom_call_target="tpu_custom_call", output_to_operand_aliasing={{}: (8, {})} | custom-call | flops 1073741824 | bytes 4980736 | tf_op jit(solution)/shard_map/pallas_call | solution.py:109
  (151 shorter events, 31.9 us)
Async XLA Ops:
  10.2 37.8 %collective-permute-start.29 = (bf16[2,128,1024]{2,1,0:T(8,128)(2,1)}, bf16[2,128,1024]{2,1,0:T(8,128)(2,1)}, u32[]{:S(2)}, u32[]{:S(2)}) collective-permute-start(bf16[2,128,1024]{2,1,0:T(8,128)(2,1)} %bitcast.29), channel_id=1, source_target_pairs={{0,4},{4,0},{8,12},{12,8},{16,20},{20,16},{24,28},{28,24},{32,36},... | collective-permute-start | bytes 1572872 | tf_op jit(solution)/shard_map/ppermute | solution.py:19
  11.1 36.9 %collective-permute-start.41 = (bf16[2,128,1024]{2,1,0:T(8,128)(2,1)}, bf16[2,128,1024]{2,1,0:T(8,128)(2,1)}, u32[]{:S(2)}, u32[]{:S(2)}) collective-permute-start(bf16[2,128,1024]{2,1,0:T(8,128)(2,1)} %bitcast.39), channel_id=1, source_target_pairs={{0,4},{4,0},{8,12},{12,8},{16,20},{20,16},{24,28},{28,24},{32,36},... | collective-permute-start | bytes 1572872 | tf_op jit(solution)/shard_map/ppermute | solution.py:19
  11.1 39.6 %collective-permute-start.17 = (bf16[2,128,1024]{2,1,0:T(8,128)(2,1)S(1)}, bf16[2,128,1024]{2,1,0:T(8,128)(2,1)}, u32[]{:S(2)}, u32[]{:S(2)}) collective-permute-start(bf16[2,128,1024]{2,1,0:T(8,128)(2,1)S(1)} %bitcast.68), channel_id=1, source_target_pairs={{0,4},{4,0},{8,12},{12,8},{16,20},{20,16},{24,28},{28,24},{32,36},... | collective-permute-start | bytes 1572872 | tf_op jit(solution)/shard_map/ppermute | solution.py:19
  11.6 41.1 %collective-permute-start.5 = (bf16[2,128,1024]{2,1,0:T(8,128)(2,1)S(1)}, bf16[2,128,1024]{2,1,0:T(8,128)(2,1)}, u32[]{:S(2)}, u32[]{:S(2)}) collective-permute-start(bf16[2,128,1024]{2,1,0:T(8,128)(2,1)S(1)} %bitcast.70), channel_id=1, source_target_pairs={{0,4},{4,0},{8,12},{12,8},{16,20},{20,16},{24,28},{28,24},{32,36},... | collective-permute-start | bytes 1572872 | tf_op jit(solution)/shard_map/ppermute | solution.py:19
  18.9 24.2 %collective-permute-start.2 = (bf16[4,144,256]{2,1,0:T(8,128)(2,1)}, bf16[4,144,256]{2,1,0:T(8,128)(2,1)}, u32[]{:S(2)}, u32[]{:S(2)}) collective-permute-start(bf16[4,144,256]{2,1,0:T(8,128)(2,1)} %pad_maximum_fusion.5), channel_id=1, source_target_pairs={{0,32},{4,100},{8,40},{12,108},{16,48},{20,116},{24,56},{28,124},{... | collective-permute-start | bytes 884744 | tf_op jit(solution)/shard_map/ppermute | solution.py:19
  44.1 43.8 %collective-permute-start.3 = (bf16[8,144,256]{2,1,0:T(8,128)(2,1)S(1)}, bf16[8,144,256]{2,1,0:T(8,128)(2,1)S(1)}, u32[]{:S(2)}, u32[]{:S(2)}) collective-permute-start(bf16[8,144,256]{2,1,0:T(8,128)(2,1)S(1)} %pad_maximum_fusion), channel_id=1, source_target_pairs={{0,96},{4,36},{8,104},{12,44},{16,112},{20,52},{24,120},{28,60},{3... | collective-permute-start | bytes 1769480 | tf_op jit(solution)/shard_map/ppermute | solution.py:19
  49.8 6.5 %collective-permute-start.42 = (bf16[1,128,1024]{2,1,0:T(8,128)(2,1)S(1)}, bf16[1,128,1024]{2,1,0:T(8,128)(2,1)S(1)}, u32[]{:S(2)}, u32[]{:S(2)}) collective-permute-start(bf16[1,128,1024]{2,1,0:T(8,128)(2,1)S(1)} %get-tuple-element.15), channel_id=1, source_target_pairs={{0,8},{4,28},{8,0},{12,20},{16,24},{20,12},{24,16},{28,4},{32,40},... | collective-permute-start | bytes 786440 | tf_op jit(solution)/shard_map/ppermute | solution.py:19
  50.7 8.4 %collective-permute-start.30 = (bf16[1,128,1024]{2,1,0:T(8,128)(2,1)S(1)}, bf16[1,128,1024]{2,1,0:T(8,128)(2,1)S(1)}, u32[]{:S(2)}, u32[]{:S(2)}) collective-permute-start(bf16[1,128,1024]{2,1,0:T(8,128)(2,1)S(1)} %get-tuple-element.19), channel_id=1, source_target_pairs={{0,8},{4,28},{8,0},{12,20},{16,24},{20,12},{24,16},{28,4},{32,40},... | collective-permute-start | bytes 786440 | tf_op jit(solution)/shard_map/ppermute | solution.py:19
  52.7 7.0 %collective-permute-start.34 = (bf16[1,128,1024]{2,1,0:T(8,128)(2,1)S(1)}, bf16[1,128,1024]{2,1,0:T(8,128)(2,1)S(1)}, u32[]{:S(2)}, u32[]{:S(2)}) collective-permute-start(bf16[1,128,1024]{2,1,0:T(8,128)(2,1)S(1)} %get-tuple-element.20), channel_id=1, source_target_pairs={{0,32},{4,100},{8,40},{12,108},{16,48},{20,116},{24,56},{28,124},{... | collective-permute-start | bytes 786440 | tf_op jit(solution)/shard_map/ppermute | solution.py:19
  56.4 8.1 %collective-permute-start.22 = (bf16[1,128,1024]{2,1,0:T(8,128)(2,1)S(1)}, bf16[1,128,1024]{2,1,0:T(8,128)(2,1)S(1)}, u32[]{:S(2)}, u32[]{:S(2)}) collective-permute-start(bf16[1,128,1024]{2,1,0:T(8,128)(2,1)S(1)} %get-tuple-element.24), channel_id=1, source_target_pairs={{0,32},{4,100},{8,40},{12,108},{16,48},{20,116},{24,56},{28,124},{... | collective-permute-start | bytes 786440 | tf_op jit(solution)/shard_map/ppermute | solution.py:19
  59.1 6.5 %collective-permute-start.10 = (bf16[1,128,1024]{2,1,0:T(8,128)(2,1)S(1)}, bf16[1,128,1024]{2,1,0:T(8,128)(2,1)S(1)}, u32[]{:S(2)}, u32[]{:S(2)}) collective-permute-start(bf16[1,128,1024]{2,1,0:T(8,128)(2,1)S(1)} %get-tuple-element.28), channel_id=1, source_target_pairs={{0,32},{4,100},{8,40},{12,108},{16,48},{20,116},{24,56},{28,124},{... | collective-permute-start | bytes 786440 | tf_op jit(solution)/shard_map/ppermute | solution.py:19
  59.8 7.6 %collective-permute-start.6 = (bf16[1,128,1024]{2,1,0:T(8,128)(2,1)S(1)}, bf16[1,128,1024]{2,1,0:T(8,128)(2,1)S(1)}, u32[]{:S(2)}, u32[]{:S(2)}) collective-permute-start(bf16[1,128,1024]{2,1,0:T(8,128)(2,1)S(1)} %get-tuple-element.27), channel_id=1, source_target_pairs={{0,8},{4,28},{8,0},{12,20},{16,24},{20,12},{24,16},{28,4},{32,40},... | collective-permute-start | bytes 786440 | tf_op jit(solution)/shard_map/ppermute | solution.py:19
  62.7 7.6 %collective-permute-start.43 = (bf16[1,128,1024]{2,1,0:T(8,128)(2,1)S(1)}, bf16[1,128,1024]{2,1,0:T(8,128)(2,1)S(1)}, u32[]{:S(2)}, u32[]{:S(2)}) collective-permute-start(bf16[1,128,1024]{2,1,0:T(8,128)(2,1)S(1)} %get-tuple-element.13), channel_id=1, source_target_pairs={{0,24},{4,12},{8,16},{12,4},{16,8},{20,28},{24,0},{28,20},{32,56},... | collective-permute-start | bytes 786440 | tf_op jit(solution)/shard_map/ppermute | solution.py:19
  64.4 7.6 %collective-permute-start.47 = (bf16[1,128,1024]{2,1,0:T(8,128)(2,1)S(1)}, bf16[1,128,1024]{2,1,0:T(8,128)(2,1)S(1)}, u32[]{:S(2)}, u32[]{:S(2)}) collective-permute-start(bf16[1,128,1024]{2,1,0:T(8,128)(2,1)S(1)} %get-tuple-element.14), channel_id=1, source_target_pairs={{0,96},{4,36},{8,104},{12,44},{16,112},{20,52},{24,120},{28,60},{3... | collective-permute-start | bytes 786440 | tf_op jit(solution)/shard_map/ppermute | solution.py:19
  65.6 8.6 %collective-permute-start.31 = (bf16[1,128,1024]{2,1,0:T(8,128)(2,1)S(1)}, bf16[1,128,1024]{2,1,0:T(8,128)(2,1)S(1)}, u32[]{:S(2)}, u32[]{:S(2)}) collective-permute-start(bf16[1,128,1024]{2,1,0:T(8,128)(2,1)S(1)} %get-tuple-element.17), channel_id=1, source_target_pairs={{0,24},{4,12},{8,16},{12,4},{16,8},{20,28},{24,0},{28,20},{32,56},... | collective-permute-start | bytes 786440 | tf_op jit(solution)/shard_map/ppermute | solution.py:19
  67.3 8.5 %collective-permute-start.35 = (bf16[1,128,1024]{2,1,0:T(8,128)(2,1)S(1)}, bf16[1,128,1024]{2,1,0:T(8,128)(2,1)S(1)}, u32[]{:S(2)}, u32[]{:S(2)}) collective-permute-start(bf16[1,128,1024]{2,1,0:T(8,128)(2,1)S(1)} %get-tuple-element.18), channel_id=1, source_target_pairs={{0,96},{4,36},{8,104},{12,44},{16,112},{20,52},{24,120},{28,60},{3... | collective-permute-start | bytes 786440 | tf_op jit(solution)/shard_map/ppermute | solution.py:19
  70.2 7.6 %collective-permute-start.19 = (bf16[1,128,1024]{2,1,0:T(8,128)(2,1)S(1)}, bf16[1,128,1024]{2,1,0:T(8,128)(2,1)S(1)}, u32[]{:S(2)}, u32[]{:S(2)}) collective-permute-start(bf16[1,128,1024]{2,1,0:T(8,128)(2,1)S(1)} %get-tuple-element.21), channel_id=1, source_target_pairs={{0,24},{4,12},{8,16},{12,4},{16,8},{20,28},{24,0},{28,20},{32,56},... | collective-permute-start | bytes 786440 | tf_op jit(solution)/shard_map/ppermute | solution.py:19
  72.1 8.2 %collective-permute-start.23 = (bf16[1,128,1024]{2,1,0:T(8,128)(2,1)S(1)}, bf16[1,128,1024]{2,1,0:T(8,128)(2,1)S(1)}, u32[]{:S(2)}, u32[]{:S(2)}) collective-permute-start(bf16[1,128,1024]{2,1,0:T(8,128)(2,1)S(1)} %get-tuple-element.22), channel_id=1, source_target_pairs={{0,96},{4,36},{8,104},{12,44},{16,112},{20,52},{24,120},{28,60},{3... | collective-permute-start | bytes 786440 | tf_op jit(solution)/shard_map/ppermute | solution.py:19
  74.2 8.8 %collective-permute-start.7 = (bf16[1,128,1024]{2,1,0:T(8,128)(2,1)S(1)}, bf16[1,128,1024]{2,1,0:T(8,128)(2,1)S(1)}, u32[]{:S(2)}, u32[]{:S(2)}) collective-permute-start(bf16[1,128,1024]{2,1,0:T(8,128)(2,1)S(1)} %get-tuple-element.25), channel_id=1, source_target_pairs={{0,24},{4,12},{8,16},{12,4},{16,8},{20,28},{24,0},{28,20},{32,56},... | collective-permute-start | bytes 786440 | tf_op jit(solution)/shard_map/ppermute | solution.py:19
  75.8 10.5 %collective-permute-start.11 = (bf16[1,128,1024]{2,1,0:T(8,128)(2,1)S(1)}, bf16[1,128,1024]{2,1,0:T(8,128)(2,1)S(1)}, u32[]{:S(2)}, u32[]{:S(2)}) collective-permute-start(bf16[1,128,1024]{2,1,0:T(8,128)(2,1)S(1)} %get-tuple-element.26), channel_id=1, source_target_pairs={{0,96},{4,36},{8,104},{12,44},{16,112},{20,52},{24,120},{28,60},{3... | collective-permute-start | bytes 786440 | tf_op jit(solution)/shard_map/ppermute | solution.py:19
  77.8 11.1 %collective-permute-start.44 = (bf16[1,128,1024]{2,1,0:T(8,128)(2,1)S(1)}, bf16[1,128,1024]{2,1,0:T(8,128)(2,1)S(1)}, u32[]{:S(2)}, u32[]{:S(2)}) collective-permute-start(bf16[1,128,1024]{2,1,0:T(8,128)(2,1)S(1)} %broadcast_select_fusion.9), channel_id=1, source_target_pairs={{0,32},{4,100},{8,40},{12,108},{16,48},{20,116},{24,56},{28,124},{... | collective-permute-start | bytes 786440 | tf_op jit(solution)/shard_map/ppermute | solution.py:19
  80.3 9.2 %collective-permute-start.48 = (bf16[1,128,1024]{2,1,0:T(8,128)(2,1)S(1)}, bf16[1,128,1024]{2,1,0:T(8,128)(2,1)S(1)}, u32[]{:S(2)}, u32[]{:S(2)}) collective-permute-start(bf16[1,128,1024]{2,1,0:T(8,128)(2,1)S(1)} %broadcast_select_fusion.5), channel_id=1, source_target_pairs={{0,8},{4,28},{8,0},{12,20},{16,24},{20,12},{24,16},{28,4},{32,40},... | collective-permute-start | bytes 786440 | tf_op jit(solution)/shard_map/ppermute | solution.py:19
  83.1 8.5 %collective-permute-start.32 = (bf16[1,128,1024]{2,1,0:T(8,128)(2,1)S(1)}, bf16[1,128,1024]{2,1,0:T(8,128)(2,1)S(1)}, u32[]{:S(2)}, u32[]{:S(2)}) collective-permute-start(bf16[1,128,1024]{2,1,0:T(8,128)(2,1)S(1)} %broadcast_select_fusion.17), channel_id=1, source_target_pairs={{0,32},{4,100},{8,40},{12,108},{16,48},{20,116},{24,56},{28,124},{... | collective-permute-start | bytes 786440 | tf_op jit(solution)/shard_map/ppermute | solution.py:19
  86.4 6.9 %collective-permute-start.36 = (bf16[1,128,1024]{2,1,0:T(8,128)(2,1)S(1)}, bf16[1,128,1024]{2,1,0:T(8,128)(2,1)S(1)}, u32[]{:S(2)}, u32[]{:S(2)}) collective-permute-start(bf16[1,128,1024]{2,1,0:T(8,128)(2,1)S(1)} %broadcast_select_fusion.13), channel_id=1, source_target_pairs={{0,8},{4,28},{8,0},{12,20},{16,24},{20,12},{24,16},{28,4},{32,40},... | collective-permute-start | bytes 786440 | tf_op jit(solution)/shard_map/ppermute | solution.py:19
  88.9 6.6 %collective-permute-start.24 = (bf16[1,128,1024]{2,1,0:T(8,128)(2,1)S(1)}, bf16[1,128,1024]{2,1,0:T(8,128)(2,1)S(1)}, u32[]{:S(2)}, u32[]{:S(2)}) collective-permute-start(bf16[1,128,1024]{2,1,0:T(8,128)(2,1)S(1)} %broadcast_select_fusion.21), channel_id=1, source_target_pairs={{0,8},{4,28},{8,0},{12,20},{16,24},{20,12},{24,16},{28,4},{32,40},... | collective-permute-start | bytes 786440 | tf_op jit(solution)/shard_map/ppermute | solution.py:19
  89.5 8.2 %collective-permute-start.8 = (bf16[1,128,1024]{2,1,0:T(8,128)(2,1)S(1)}, bf16[1,128,1024]{2,1,0:T(8,128)(2,1)S(1)}, u32[]{:S(2)}, u32[]{:S(2)}) collective-permute-start(bf16[1,128,1024]{2,1,0:T(8,128)(2,1)S(1)} %broadcast_select_fusion.33), channel_id=1, source_target_pairs={{0,32},{4,100},{8,40},{12,108},{16,48},{20,116},{24,56},{28,124},{... | collective-permute-start | bytes 786440 | tf_op jit(solution)/shard_map/ppermute | solution.py:19
  91.6 8.4 %collective-permute-start.12 = (bf16[1,128,1024]{2,1,0:T(8,128)(2,1)S(1)}, bf16[1,128,1024]{2,1,0:T(8,128)(2,1)S(1)}, u32[]{:S(2)}, u32[]{:S(2)}) collective-permute-start(bf16[1,128,1024]{2,1,0:T(8,128)(2,1)S(1)} %broadcast_select_fusion.29), channel_id=1, source_target_pairs={{0,8},{4,28},{8,0},{12,20},{16,24},{20,12},{24,16},{28,4},{32,40},... | collective-permute-start | bytes 786440 | tf_op jit(solution)/shard_map/ppermute | solution.py:19
  93.3 55.7 %collective-permute-start.4 = (bf16[16,144,256]{2,1,0:T(8,128)(2,1)}, bf16[16,144,256]{2,1,0:T(8,128)(2,1)}, u32[]{:S(2)}, u32[]{:S(2)}) collective-permute-start(bf16[16,144,256]{2,1,0:T(8,128)(2,1)} %get-tuple-element.11), channel_id=1, source_target_pairs={{0,4},{4,0},{8,12},{12,8},{16,20},{20,16},{24,28},{28,24},{32,36},... | collective-permute-start | bytes 3538952 | tf_op jit(solution)/shard_map/ppermute | solution.py:19
  94.4 7.6 %collective-permute-start.45 = (bf16[1,128,1024]{2,1,0:T(8,128)(2,1)S(1)}, bf16[1,128,1024]{2,1,0:T(8,128)(2,1)S(1)}, u32[]{:S(2)}, u32[]{:S(2)}) collective-permute-start(bf16[1,128,1024]{2,1,0:T(8,128)(2,1)S(1)} %broadcast_select_fusion.10), channel_id=1, source_target_pairs={{0,96},{4,36},{8,104},{12,44},{16,112},{20,52},{24,120},{28,60},{3... | collective-permute-start | bytes 786440 | tf_op jit(solution)/shard_map/ppermute | solution.py:19
  95.5 8.0 %collective-permute-start.49 = (bf16[1,128,1024]{2,1,0:T(8,128)(2,1)S(1)}, bf16[1,128,1024]{2,1,0:T(8,128)(2,1)S(1)}, u32[]{:S(2)}, u32[]{:S(2)}) collective-permute-start(bf16[1,128,1024]{2,1,0:T(8,128)(2,1)S(1)} %broadcast_select_fusion.6), channel_id=1, source_target_pairs={{0,24},{4,12},{8,16},{12,4},{16,8},{20,28},{24,0},{28,20},{32,56},... | collective-permute-start | bytes 786440 | tf_op jit(solution)/shard_map/ppermute | solution.py:19
  97.7 8.1 %collective-permute-start.33 = (bf16[1,128,1024]{2,1,0:T(8,128)(2,1)S(1)}, bf16[1,128,1024]{2,1,0:T(8,128)(2,1)S(1)}, u32[]{:S(2)}, u32[]{:S(2)}) collective-permute-start(bf16[1,128,1024]{2,1,0:T(8,128)(2,1)S(1)} %broadcast_select_fusion.18), channel_id=1, source_target_pairs={{0,96},{4,36},{8,104},{12,44},{16,112},{20,52},{24,120},{28,60},{3... | collective-permute-start | bytes 786440 | tf_op jit(solution)/shard_map/ppermute | solution.py:19
  100.0 7.7 %collective-permute-start.37 = (bf16[1,128,1024]{2,1,0:T(8,128)(2,1)S(1)}, bf16[1,128,1024]{2,1,0:T(8,128)(2,1)S(1)}, u32[]{:S(2)}, u32[]{:S(2)}) collective-permute-start(bf16[1,128,1024]{2,1,0:T(8,128)(2,1)S(1)} %broadcast_select_fusion.14), channel_id=1, source_target_pairs={{0,24},{4,12},{8,16},{12,4},{16,8},{20,28},{24,0},{28,20},{32,56},... | collective-permute-start | bytes 786440 | tf_op jit(solution)/shard_map/ppermute | solution.py:19
  101.9 7.6 %collective-permute-start.21 = (bf16[1,128,1024]{2,1,0:T(8,128)(2,1)S(1)}, bf16[1,128,1024]{2,1,0:T(8,128)(2,1)S(1)}, u32[]{:S(2)}, u32[]{:S(2)}) collective-permute-start(bf16[1,128,1024]{2,1,0:T(8,128)(2,1)S(1)} %broadcast_select_fusion.26), channel_id=1, source_target_pairs={{0,96},{4,36},{8,104},{12,44},{16,112},{20,52},{24,120},{28,60},{3... | collective-permute-start | bytes 786440 | tf_op jit(solution)/shard_map/ppermute | solution.py:19
  103.6 8.0 %collective-permute-start.25 = (bf16[1,128,1024]{2,1,0:T(8,128)(2,1)S(1)}, bf16[1,128,1024]{2,1,0:T(8,128)(2,1)S(1)}, u32[]{:S(2)}, u32[]{:S(2)}) collective-permute-start(bf16[1,128,1024]{2,1,0:T(8,128)(2,1)S(1)} %broadcast_select_fusion.22), channel_id=1, source_target_pairs={{0,24},{4,12},{8,16},{12,4},{16,8},{20,28},{24,0},{28,20},{32,56},... | collective-permute-start | bytes 786440 | tf_op jit(solution)/shard_map/ppermute | solution.py:19
  105.8 7.9 %collective-permute-start.9 = (bf16[1,128,1024]{2,1,0:T(8,128)(2,1)S(1)}, bf16[1,128,1024]{2,1,0:T(8,128)(2,1)S(1)}, u32[]{:S(2)}, u32[]{:S(2)}) collective-permute-start(bf16[1,128,1024]{2,1,0:T(8,128)(2,1)S(1)} %broadcast_select_fusion.34), channel_id=1, source_target_pairs={{0,96},{4,36},{8,104},{12,44},{16,112},{20,52},{24,120},{28,60},{3... | collective-permute-start | bytes 786440 | tf_op jit(solution)/shard_map/ppermute | solution.py:19
  107.7 7.7 %collective-permute-start.13 = (bf16[1,128,1024]{2,1,0:T(8,128)(2,1)S(1)}, bf16[1,128,1024]{2,1,0:T(8,128)(2,1)S(1)}, u32[]{:S(2)}, u32[]{:S(2)}) collective-permute-start(bf16[1,128,1024]{2,1,0:T(8,128)(2,1)S(1)} %broadcast_select_fusion.30), channel_id=1, source_target_pairs={{0,24},{4,12},{8,16},{12,4},{16,8},{20,28},{24,0},{28,20},{32,56},... | collective-permute-start | bytes 786440 | tf_op jit(solution)/shard_map/ppermute | solution.py:19
  109.5 11.2 %collective-permute-start.50 = (bf16[256,1024]{1,0:T(8,128)(2,1)S(1)}, bf16[256,1024]{1,0:T(8,128)(2,1)}, u32[]{:S(2)}, u32[]{:S(2)}) collective-permute-start(bf16[256,1024]{1,0:T(8,128)(2,1)S(1)} %bitcast.62), channel_id=1, source_target_pairs={{0,1},{1,2},{2,3},{3,0},{4,7},{5,4},{6,5},{7,6},{8,9},{9,10},{10,1... | collective-permute-start | bytes 1572872 | tf_op jit(solution)/shard_map/ppermute | solution.py:29
  111.6 14.8 %collective-permute-start.38 = (bf16[256,1024]{1,0:T(8,128)(2,1)S(1)}, bf16[256,1024]{1,0:T(8,128)(2,1)}, u32[]{:S(2)}, u32[]{:S(2)}) collective-permute-start(bf16[256,1024]{1,0:T(8,128)(2,1)S(1)} %bitcast.60), channel_id=1, source_target_pairs={{0,1},{1,2},{2,3},{3,0},{4,7},{5,4},{6,5},{7,6},{8,9},{9,10},{10,1... | collective-permute-start | bytes 1572872 | tf_op jit(solution)/shard_map/ppermute | solution.py:29
  113.7 18.3 %collective-permute-start.26 = (bf16[256,1024]{1,0:T(8,128)(2,1)S(1)}, bf16[256,1024]{1,0:T(8,128)(2,1)}, u32[]{:S(2)}, u32[]{:S(2)}) collective-permute-start(bf16[256,1024]{1,0:T(8,128)(2,1)S(1)} %bitcast.64), channel_id=1, source_target_pairs={{0,1},{1,2},{2,3},{3,0},{4,7},{5,4},{6,5},{7,6},{8,9},{9,10},{10,1... | collective-permute-start | bytes 1572872 | tf_op jit(solution)/shard_map/ppermute | solution.py:29
  115.5 22.1 %collective-permute-start.14 = (bf16[256,1024]{1,0:T(8,128)(2,1)S(1)}, bf16[256,1024]{1,0:T(8,128)(2,1)}, u32[]{:S(2)}, u32[]{:S(2)}) collective-permute-start(bf16[256,1024]{1,0:T(8,128)(2,1)S(1)} %bitcast.66), channel_id=1, source_target_pairs={{0,1},{1,2},{2,3},{3,0},{4,7},{5,4},{6,5},{7,6},{8,9},{9,10},{10,1... | collective-permute-start | bytes 1572872 | tf_op jit(solution)/shard_map/ppermute | solution.py:29
  120.8 22.5 %collective-permute-start.51 = (bf16[256,1024]{1,0:T(8,128)(2,1)}, bf16[256,1024]{1,0:T(8,128)(2,1)}, u32[]{:S(2)}, u32[]{:S(2)}) collective-permute-start(bf16[256,1024]{1,0:T(8,128)(2,1)} %collective-permute-done.50.x1), channel_id=1, source_target_pairs={{0,1},{1,2},{2,3},{3,0},{4,7},{5,4},{6,5},{7,6},{8,9},{9,10},{10,1... | collective-permute-start | bytes 1572872 | tf_op jit(solution)/shard_map/ppermute | solution.py:29
  126.4 22.5 %collective-permute-start.39 = (bf16[256,1024]{1,0:T(8,128)(2,1)}, bf16[256,1024]{1,0:T(8,128)(2,1)}, u32[]{:S(2)}, u32[]{:S(2)}) collective-permute-start(bf16[256,1024]{1,0:T(8,128)(2,1)} %collective-permute-done.38.x1), channel_id=1, source_target_pairs={{0,1},{1,2},{2,3},{3,0},{4,7},{5,4},{6,5},{7,6},{8,9},{9,10},{10,1... | collective-permute-start | bytes 1572872 | tf_op jit(solution)/shard_map/ppermute | solution.py:29
  132.0 22.5 %collective-permute-start.27 = (bf16[256,1024]{1,0:T(8,128)(2,1)}, bf16[256,1024]{1,0:T(8,128)(2,1)}, u32[]{:S(2)}, u32[]{:S(2)}) collective-permute-start(bf16[256,1024]{1,0:T(8,128)(2,1)} %collective-permute-done.26.x1), channel_id=1, source_target_pairs={{0,1},{1,2},{2,3},{3,0},{4,7},{5,4},{6,5},{7,6},{8,9},{9,10},{10,1... | collective-permute-start | bytes 1572872 | tf_op jit(solution)/shard_map/ppermute | solution.py:29
  137.6 22.5 %collective-permute-start.15 = (bf16[256,1024]{1,0:T(8,128)(2,1)}, bf16[256,1024]{1,0:T(8,128)(2,1)}, u32[]{:S(2)}, u32[]{:S(2)}) collective-permute-start(bf16[256,1024]{1,0:T(8,128)(2,1)} %collective-permute-done.14.x1), channel_id=1, source_target_pairs={{0,1},{1,2},{2,3},{3,0},{4,7},{5,4},{6,5},{7,6},{8,9},{9,10},{10,1... | collective-permute-start | bytes 1572872 | tf_op jit(solution)/shard_map/ppermute | solution.py:29
  143.2 22.5 %collective-permute-start.52 = (bf16[256,1024]{1,0:T(8,128)(2,1)}, bf16[256,1024]{1,0:T(8,128)(2,1)}, u32[]{:S(2)}, u32[]{:S(2)}) collective-permute-start(bf16[256,1024]{1,0:T(8,128)(2,1)} %collective-permute-done.51.x2), channel_id=1, source_target_pairs={{0,1},{1,2},{2,3},{3,0},{4,7},{5,4},{6,5},{7,6},{8,9},{9,10},{10,1... | collective-permute-start | bytes 1572872 | tf_op jit(solution)/shard_map/ppermute | solution.py:29
  148.9 22.5 %collective-permute-start.40 = (bf16[256,1024]{1,0:T(8,128)(2,1)}, bf16[256,1024]{1,0:T(8,128)(2,1)}, u32[]{:S(2)}, u32[]{:S(2)}) collective-permute-start(bf16[256,1024]{1,0:T(8,128)(2,1)} %collective-permute-done.39.x2), channel_id=1, source_target_pairs={{0,1},{1,2},{2,3},{3,0},{4,7},{5,4},{6,5},{7,6},{8,9},{9,10},{10,1... | collective-permute-start | bytes 1572872 | tf_op jit(solution)/shard_map/ppermute | solution.py:29
  154.5 22.5 %collective-permute-start.28 = (bf16[256,1024]{1,0:T(8,128)(2,1)}, bf16[256,1024]{1,0:T(8,128)(2,1)}, u32[]{:S(2)}, u32[]{:S(2)}) collective-permute-start(bf16[256,1024]{1,0:T(8,128)(2,1)} %collective-permute-done.27.x2), channel_id=1, source_target_pairs={{0,1},{1,2},{2,3},{3,0},{4,7},{5,4},{6,5},{7,6},{8,9},{9,10},{10,1... | collective-permute-start | bytes 1572872 | tf_op jit(solution)/shard_map/ppermute | solution.py:29
  160.1 22.5 %collective-permute-start.16 = (bf16[256,1024]{1,0:T(8,128)(2,1)}, bf16[256,1024]{1,0:T(8,128)(2,1)}, u32[]{:S(2)}, u32[]{:S(2)}) collective-permute-start(bf16[256,1024]{1,0:T(8,128)(2,1)} %collective-permute-done.15.x2), channel_id=1, source_target_pairs={{0,1},{1,2},{2,3},{3,0},{4,7},{5,4},{6,5},{7,6},{8,9},{9,10},{10,1... | collective-permute-start | bytes 1572872 | tf_op jit(solution)/shard_map/ppermute | solution.py:29
  (16 other events, 149.8 us)

commit v2 on v0

v2 whole, which is shorter than its diff:
```python
import functools

import jax
import jax.numpy as jnp
import numpy as np
from jax import lax
from jax.experimental import pallas as pl
from jax.experimental.pallas import tpu as pltpu
from jax.sharding import PartitionSpec as P

TILE = 128
SLOTS = 8
DEPTH = 1024
WIDTH = 1536
CORE = (1, 1)
X_A, X_B, Y_A, Y_B = (2, 6), (6, 2), (8, 24), (24, 8)
STEPS = (CORE, X_A, X_B, Y_A, Y_B)
FUNCTIONAL = {1: 1, 2: 6, 6: 4, 8: 24, 24: 16}
GATHER = (X_A, X_B, Y_A, Y_B)
AXES = ("row", "col")


def exchange(value, masks):
    pairs = [(p, p ^ masks[p & 1]) for p in range(lax.axis_size("row"))]
    return lax.ppermute(value, "row", pairs)


def turn(value):
    rows, cols = lax.axis_size("row"), lax.axis_size("col")
    pairs = []
    for p in range(rows):
        step = 1 if p & 1 == 0 else -1
        for c in range(cols):
            pairs.append((p * cols + c, p * cols + (c + step) % cols))
    return lax.ppermute(value, AXES, pairs)


def choose(flags, masks, low, high, partner, mine):
    taken = flags[STEPS.index(masks), low:high] == 1
    return jnp.where(taken[:, None, None], partner, mine)


def pack_kernel(screen_ref, amplitudes_ref, out_ref):
    first = jnp.int32(11)
    second = jnp.int32(0)
    for j in range(12):
        live = screen_ref[0, j] == 1
        first = jnp.where(live, jnp.minimum(first, j), first)
        second = jnp.where(live, jnp.maximum(second, j), second)
    one = amplitudes_ref[:, pl.ds(pl.multiple_of(first * TILE, TILE), TILE)]
    two = amplitudes_ref[:, pl.ds(pl.multiple_of(second * TILE, TILE), TILE)]
    out_ref[0, :TILE, :TILE] = one
    out_ref[0, :TILE, TILE:] = jnp.where(first != second, two, jnp.zeros_like(two))
    side = lax.broadcasted_iota(jnp.int32, (16, 2 * TILE), 1) < TILE
    out_ref[0, TILE:, :] = jnp.where(side, first, second).astype(jnp.float32).astype(jnp.bfloat16)


def pack(amplitudes, screen):
    return pl.pallas_call(
        pack_kernel,
        in_specs=[pl.BlockSpec(memory_space=pltpu.SMEM), pl.BlockSpec(memory_space=pltpu.VMEM)],
        out_specs=pl.BlockSpec(memory_space=pltpu.VMEM),
        out_shape=jax.ShapeDtypeStruct((1, TILE + 16, 2 * TILE), jnp.bfloat16),
        cost_estimate=pl.CostEstimate(flops=1, bytes_accessed=1, transcendentals=0),
    )(screen, amplitudes)


def order_table():
    table = np.zeros((32, 32), np.int32)
    for me in range(32):
        for k in range(32):
            delta = k ^ me
            at = 16 * (delta & 1)
            for i, masks in enumerate(GATHER):
                at += (bin(delta & FUNCTIONAL[masks[k & 1]]).count("1") & 1) << i
            table[me, k] = at
    return table


def product_kernel(first, at_ref, place_ref, base_ref, *refs):
    *sources, tiles_hbm = refs[:5]
    out_hbm, x, tiles, total, out, sems = refs[-6:]
    rows = total.shape[0]
    loads = [pltpu.make_async_copy(tiles_hbm, tiles, sems.at[4])]
    loads += [pltpu.make_async_copy(sources[j], x.at[j], sems.at[j]) for j in range(4)]
    for load in loads:
        load.start()
    total[...] = jnp.zeros_like(total)
    loads[0].wait()
    for j in range(4):
        loads[j + 1].wait()

        for kk in range(8):
            at = at_ref[0, base_ref[j] * 8 + kk]
            part = jnp.dot(
                x[j, :, kk * TILE : (kk + 1) * TILE],
                tiles[at, :TILE, :],
                preferred_element_type=jnp.float32,
            )
            for i in range(2):
                where = pl.ds(pl.multiple_of(place_ref[2 * at + i] * TILE, TILE), TILE)
                total[:, where] += part[:, i * TILE : (i + 1) * TILE]

    out[...] = total[...].astype(out.dtype)
    store = pltpu.make_async_copy(out, out_hbm.at[pl.ds(first, rows)], sems.at[5])
    store.start()
    store.wait()


def product(blocks, tiles, at, place, base, out=None, first=0, rows_all=None):
    rows = blocks[0].shape[0]
    rows_all = rows_all or rows
    args = list(blocks) + [tiles]
    aliases = {}
    if out is not None:
        args.append(out)
        aliases = {8: 0}
    return pl.pallas_call(
        functools.partial(product_kernel, first),
        grid_spec=pltpu.PrefetchScalarGridSpec(
            num_scalar_prefetch=3,
            grid=(1,),
            in_specs=[pl.BlockSpec(memory_space=pl.ANY)] * len(args),
            out_specs=pl.BlockSpec(memory_space=pl.ANY),
            scratch_shapes=[
                pltpu.VMEM((4, rows, DEPTH), jnp.bfloat16),
                pltpu.VMEM(tiles.shape, jnp.bfloat16),
                pltpu.VMEM((rows, WIDTH), jnp.float32),
                pltpu.VMEM((rows, WIDTH), jnp.bfloat16),
                pltpu.SemaphoreType.DMA((6,)),
            ],
        ),
        out_shape=jax.ShapeDtypeStruct((rows_all, WIDTH), jnp.bfloat16),
        input_output_aliases=aliases,
        compiler_params=pltpu.CompilerParams(vmem_limit_bytes=24 * 2**20),
        cost_estimate=pl.CostEstimate(flops=1, bytes_accessed=1, transcendentals=0),
    )(at, place, base, *args)


class Sequence:
    def __init__(self, token):
        self.token = token

    def tied(self, *values):
        return lax.optimization_barrier((*values, self.token))[: len(values)]

    def after(self, value):
        return self.tied(value)[0]

    def done(self, value):
        self.token = self.after(value)
        return self.token


PAIRS = ((0, 2), (2, 4), (4, 6), (6, 8))
PATHS = (
    (X_A, X_B, Y_A, Y_B),
    (Y_A, X_A, Y_B, X_B),
    (Y_A, X_A, X_B, Y_B),
    (X_A, Y_A, Y_B, X_B),
)


def body(integrals, amplitudes, screen, next_owner):
    me = lax.axis_index("row").astype(jnp.int32)
    col = lax.axis_index("col").astype(jnp.int32)
    core = me & 1
    slots = integrals.reshape(SLOTS, TILE, DEPTH)

    functional = [jnp.asarray([[FUNCTIONAL[m[c]]] for m in STEPS], jnp.int32) for c in range(2)]
    value = next_owner[None, :SLOTS] & jnp.where(core == 0, functional[0], functional[1])
    value = value ^ value >> 4
    value = value ^ value >> 2
    value = value ^ value >> 1
    flags = value & 1
    at = lax.dynamic_slice(jnp.asarray(order_table()), (me, 0), (1, 32))
    sign = 1 - 2 * core
    base = (col - sign * jnp.arange(4, dtype=jnp.int32)) & 3
    flags, at, base = lax.optimization_barrier((flags, at, base))

    seq = Sequence(next_owner)

    class Moving:
        def __init__(self, value, cut, order):
            self.value, self.cut, self.order, self.at = value, cut, order, 0

        def send(self):
            self.value = seq.after(self.value)
            self.partner = exchange(self.value, self.order[self.at])

        def take(self):
            partner, mine = seq.tied(self.partner, self.value)
            self.value = seq.done(choose(flags, self.order[self.at], *self.cut, partner, mine))
            self.at += 1

    class Ring:
        def __init__(self, value):
            self.blocks = [value]

        def send(self):
            self.blocks.append(turn(seq.after(self.blocks[-1])))

        def take(self):
            self.blocks[-1] = seq.done(self.blocks[-1])

    class Tiles:
        def __init__(self, value):
            self.value, self.at = value, 0

        def send(self):
            self.value = seq.after(self.value)
            self.partner = exchange(self.value, (*GATHER, CORE)[self.at])
            self.at += 1

        def take(self):
            partner, mine = seq.tied(self.partner, self.value)
            self.value = seq.done(jnp.concatenate([mine, partner], axis=0))

    class Swapped:
        def __init__(self):
            self.partner = exchange(slots, CORE)

        def pair(self, low, high):
            other, mine = seq.tied(self.partner, slots)
            return seq.done(choose(flags, CORE, low, high, other[low:high], mine[low:high]))

    def times(ring):
        live = tiles.value
        place = live[:, TILE, :].reshape(32, 2, TILE)[:, :, 0].astype(jnp.int32).reshape(64)
        return product(ring.blocks, live, at, place, base)

    def finish(ring, out, low):
        live = tiles.value
        place = live[:, TILE, :].reshape(32, 2, TILE)[:, :, 0].astype(jnp.int32).reshape(64)
        return product(ring.blocks, live, at, place, base, out, low * TILE, SLOTS * TILE)

    early, late, rings = [None] * 2, [None] * 2, [None] * 4
    swapped = Swapped()
    tiles = Tiles(seq.done(pack(amplitudes, screen)))
    tiles.send()
    rings[3] = Ring(swapped.pair(*PAIRS[3]).reshape(2 * TILE, DEPTH))
    tiles.take()
    rings[3].send()
    tiles.send()
    rings[2] = Ring(swapped.pair(*PAIRS[2]).reshape(2 * TILE, DEPTH))
    early[0] = Moving(swapped.pair(*PAIRS[0]), PAIRS[0], PATHS[0])
    early[0].send()
    rings[2].send()
    early[1] = Moving(swapped.pair(*PAIRS[1]), PAIRS[1], PATHS[1])
    tiles.take()
    tiles.send()
    early[1].send()
    rings[3].take()
    rings[3].send()
    early[0].take()
    early[0].send()
    tiles.take()
    tiles.send()
    rings[2].take()
    rings[2].send()
    early[1].take()
    early[1].send()
    rings[3].take()
    rings[3].send()
    early[0].take()
    early[0].send()
    tiles.take()
    tiles.send()
    rings[2].take()
    rings[2].send()
    early[1].take()
    early[1].send()
    tiles.take()
    rings[3].take()
    value = seq.done(times(rings[3])).reshape(2, TILE, WIDTH)
    late[1] = Moving(value, PAIRS[3], PATHS[3])
    early[0].take()
    early[0].send()
    late[1].send()
    rings[2].take()
    value = seq.done(times(rings[2])).reshape(2, TILE, WIDTH)
    late[0] = Moving(value, PAIRS[2], PATHS[2])
    late[0].send()
    early[1].take()
    early[1].send()
    early[0].take()
    rings[0] = Ring(early[0].value.reshape(2 * TILE, DEPTH))
    rings[0].send()
    late[1].take()
    late[1].send()
    late[0].take()
    late[0].send()
    early[1].take()
    rings[1] = Ring(early[1].value.reshape(2 * TILE, DEPTH))
    rings[1].send()
    rings[0].take()
    rings[0].send()
    late[1].take()
    late[1].send()
    late[0].take()
    late[0].send()
    rings[1].take()
    rings[1].send()
    rings[0].take()
    rings[0].send()
    late[1].take()
    late[1].send()
    rings[1].take()
    rings[1].send()
    late[0].take()
    late[0].send()
    rings[0].take()
    out = seq.done(finish(rings[0], None, PAIRS[0][0]))
    late[1].take()
    rings[1].take()
    out = seq.done(finish(rings[1], out, PAIRS[1][0]))
    late[0].take()

    for part, (low, _) in zip(late, PAIRS[2:]):
        out = lax.dynamic_update_slice(out, part.value.reshape(2 * TILE, WIDTH), (low * TILE, 0))
    return out


def solution(mesh):
    placed = (P("row", "col"), P("row", "col"), P("row", "col"), P())
    return jax.shard_map(
        body, mesh=mesh, in_specs=placed, out_specs=P("row", "col"), check_vma=False
    )
```

time: 475 us -> 146 us (0.31)
  waiting for transfers between devices: 428 us -> 65.1 us
  starting transfers between devices: 8.86 us -> 43.4 us
  matrix products: 18.2 us -> 0 us
  Pallas kernels: 0 us -> 17.7 us
  between operations: 13.4 us -> 0.28 us
  other arithmetic: 6.04 us -> 13.8 us
    ppermute x5 -> x34, waiting for transfers between devices: 276 us -> 65.1 us  [the longest x22 34.1 us: exchange(): return lax.ppermute(value, 'row', pairs)]
    all_gather x2 -> x0, waiting for transfers between devices: 151 us -> none  [the longest x1 85 us: body(): gathered = lax.all_gather(integrals, 'col', axis=1, tiled=True)]
    ppermute x5 -> x34, starting transfers between devices: 8.82 us -> 43.4 us  [the longest x22 33.9 us: exchange(): return lax.ppermute(value, 'row', pairs)]
    dot_general x1 -> x0, matrix products: 18.2 us -> none  [body(): jnp.dot(gathered, lax.all_gather(masked, 'row', axis=0, tiled=True), pref...]
    pallas_call x0 -> x5, Pallas kernels: none -> 17.7 us  [the longest x4 15.9 us: product(): pl.pallas_call(functools.partial(product_kernel, first), grid_spec=pltpu....]
    select_n x5 -> x20, other arithmetic: 3.6 us -> 11 us  [choose(): return jnp.where(taken[:, None, None], partner, mine)]
  transfers between devices with their start and end apart: 7 -> 34, of which waited for: 7 -> 15; matrix products, arithmetic and copies ran while one was open for 1% -> 8% of each run, Pallas kernels for 0% -> 12%
where the time goes in v2:
time: 146 us; the launch traced here: 145 us
  waiting for transfers between devices  65.1 us (45%)
  starting transfers between devices  43.4 us (30%)
  Pallas kernels  17.7 us (12%)
  other arithmetic  13.8 us (9%)
  local copies, waits for them, and re-layouts  4.49 us (3%)
    ppermute x22, waiting for transfers between devices, exchange(): return lax.ppermute(value, 'row', pairs)  34.1 us
    ppermute x22, starting transfers between devices, exchange(): return lax.ppermute(value, 'row', pairs)  33.9 us
    ppermute x12, waiting for transfers between devices, turn(): return lax.ppermute(value, AXES, pairs)  31 us
    pallas_call x4, Pallas kernels, product(): pl.pallas_call(functools.partial(product_kernel, first), grid_spec=pltpu....  15.9 us
    select_n x20, other arithmetic, choose(): return jnp.where(taken[:, None, None], partner, mine)  11 us
    ppermute x12, starting transfers between devices, turn(): return lax.ppermute(value, AXES, pairs)  9.56 us
  transfers between devices with their start and end apart: 34, of which 15 were waited for; matrix products, arithmetic and copies ran while one was open for 8% of the time, Pallas kernels for 12%

profile of v2, /device:TPU:0, one launch (start us, length us, event | category | flops | bytes accessed | tf_op | source)
XLA Modules:
  0.0 144.8 jit_solution(8705259160975348376)
XLA Ops:
  0.0 1.8 %shard_map.73 = bf16[1,144,256]{2,1,0:T(8,128)(2,1)} custom-call(s32[1,12]{1,0:T(1,128)} %screen_ref.1, bf16[128,1536]{1,0:T(8,128)(2,1)} %amplitudes_ref.1), custom_call_target="tpu_custom_call" | custom-call | flops 1 | bytes 1 | tf_op jit(solution)/shard_map/pallas_call | solution.py:59
  1.8 1.6 %collective-permute-start = (bf16[1,144,256]{2,1,0:T(8,128)(2,1)}, bf16[1,144,256]{2,1,0:T(8,128)(2,1)S(1)}, u32[]{:S(2)}, u32[]{:S(2)}) collective-permute-start(bf16[1,144,256]{2,1,0:T(8,128)(2,1)} %shard_map.73), channel_id=1, source_target_pairs={{0,8},{4,28},{8,0},{12,20},{16,24},{20,12},{24,16},{28,4},{32,40},... | collective-permute-start | bytes 221192 | tf_op jit(solution)/shard_map/ppermute | solution.py:25
  5.7 1.3 slice_select_fusion.3
  7.0 0.9 pad_maximum_fusion.4
  8.0 1.2 slice_select_fusion.2
  9.2 1.2 slice_select_fusion.1
  10.4 2.0 %collective-permute-start.5 = (bf16[256,1024]{1,0:T(8,128)(2,1)S(1)}, bf16[256,1024]{1,0:T(8,128)(2,1)S(1)}, u32[]{:S(2)}, u32[]{:S(2)}) collective-permute-start(bf16[256,1024]{1,0:T(8,128)(2,1)S(1)} %bitcast.57), channel_id=1, source_target_pairs={{0,1},{1,2},{2,3},{3,0},{4,7},{5,4},{6,5},{7,6},{8,9},{9,10},{10,1... | collective-permute-start | bytes 1572872 | tf_op jit(solution)/shard_map/ppermute | solution.py:35
  12.3 0.9 collective-permute-start.4
  13.3 1.9 %collective-permute-start.10 = (bf16[256,1024]{1,0:T(8,128)(2,1)S(1)}, bf16[256,1024]{1,0:T(8,128)(2,1)S(1)}, u32[]{:S(2)}, u32[]{:S(2)}) collective-permute-start(bf16[256,1024]{1,0:T(8,128)(2,1)S(1)} %bitcast.55), channel_id=1, source_target_pairs={{0,1},{1,2},{2,3},{3,0},{4,7},{5,4},{6,5},{7,6},{8,9},{9,10},{10,1... | collective-permute-start | bytes 1572872 | tf_op jit(solution)/shard_map/ppermute | solution.py:35
  15.2 2.4 %collective-permute-start.2 = (bf16[2,144,256]{2,1,0:T(8,128)(2,1)S(1)}, bf16[2,144,256]{2,1,0:T(8,128)(2,1)S(1)}, u32[]{:S(2)}, u32[]{:S(2)}) collective-permute-start(bf16[2,144,256]{2,1,0:T(8,128)(2,1)S(1)} %pad_maximum_fusion.4), channel_id=1, source_target_pairs={{0,24},{4,12},{8,16},{12,4},{16,8},{20,28},{24,0},{28,20},{32,56},... | collective-permute-start | bytes 442376 | tf_op jit(solution)/shard_map/ppermute | solution.py:25
  17.5 1.2 slice_select_fusion
  18.7 4.3 %collective-permute-done.2 = bf16[2,144,256]{2,1,0:T(8,128)(2,1)S(1)} collective-permute-done((bf16[2,144,256]{2,1,0:T(8,128)(2,1)S(1)}, bf16[2,144,256]{2,1,0:T(8,128)(2,1)S(1)}, u32[]{:S(2)}, u32[]{:S(2)}) %collective-permute-start.2) | collective-permute-done | bytes 147488 | tf_op jit(solution)/shard_map/ppermute | solution.py:25
  23.1 1.7 %collective-permute-start.3 = (bf16[4,144,256]{2,1,0:T(8,128)(2,1)S(1)}, bf16[4,144,256]{2,1,0:T(8,128)(2,1)S(1)}, u32[]{:S(2)}, u32[]{:S(2)}) collective-permute-start(bf16[4,144,256]{2,1,0:T(8,128)(2,1)S(1)} %pad_maximum_fusion.3), channel_id=1, source_target_pairs={{0,32},{4,100},{8,40},{12,108},{16,48},{20,116},{24,56},{28,124},{... | collective-permute-start | bytes 884744 | tf_op jit(solution)/shard_map/ppermute | solution.py:25
  25.3 1.8 %collective-permute-start.8 = (bf16[256,1024]{1,0:T(8,128)(2,1)S(1)}, bf16[256,1024]{1,0:T(8,128)(2,1)}, u32[]{:S(2)}, u32[]{:S(2)}) collective-permute-start(bf16[256,1024]{1,0:T(8,128)(2,1)S(1)} %collective-permute-done.5.refs_1_), channel_id=1, source_target_pairs={{0,1},{1,2},{2,3},{3,0},{4,7},{5,4},{6,5},{7,6},{8,9},{9,10},{10,1... | collective-permute-start | bytes 1572872 | tf_op jit(solution)/shard_map/ppermute | solution.py:35
  27.1 1.3 collective-permute-start.7
  28.4 1.5 %collective-permute-done.3 = bf16[4,144,256]{2,1,0:T(8,128)(2,1)S(1)} collective-permute-done((bf16[4,144,256]{2,1,0:T(8,128)(2,1)S(1)}, bf16[4,144,256]{2,1,0:T(8,128)(2,1)S(1)}, u32[]{:S(2)}, u32[]{:S(2)}) %collective-permute-start.3) | collective-permute-done | bytes 294944 | tf_op jit(solution)/shard_map/ppermute | solution.py:25
  29.9 3.1 %collective-permute-start.6 = (bf16[8,144,256]{2,1,0:T(8,128)(2,1)S(1)}, bf16[8,144,256]{2,1,0:T(8,128)(2,1)S(1)}, u32[]{:S(2)}, u32[]{:S(2)}) collective-permute-start(bf16[8,144,256]{2,1,0:T(8,128)(2,1)S(1)} %pad_maximum_fusion.2), channel_id=1, source_target_pairs={{0,96},{4,36},{8,104},{12,44},{16,112},{20,52},{24,120},{28,60},{3... | collective-permute-start | bytes 1769480 | tf_op jit(solution)/shard_map/ppermute | solution.py:25
  33.0 5.7 %collective-permute-done.9 = bf16[2,128,1024]{2,1,0:T(8,128)(2,1)S(1)} collective-permute-done((bf16[2,128,1024]{2,1,0:T(8,128)(2,1)S(1)}, bf16[2,128,1024]{2,1,0:T(8,128)(2,1)S(1)}, u32[]{:S(2)}, u32[]{:S(2)}) %collective-permute-start.9) | collective-permute-done | bytes 524320 | tf_op jit(solution)/shard_map/ppermute | solution.py:25
  38.9 0.9 broadcast_select_fusion.14
  39.8 1.8 %collective-permute-done.6 = bf16[8,144,256]{2,1,0:T(8,128)(2,1)S(1)} collective-permute-done((bf16[8,144,256]{2,1,0:T(8,128)(2,1)S(1)}, bf16[8,144,256]{2,1,0:T(8,128)(2,1)S(1)}, u32[]{:S(2)}, u32[]{:S(2)}) %collective-permute-start.6) | collective-permute-done | bytes 589856 | tf_op jit(solution)/shard_map/ppermute | solution.py:25
  41.9 1.6 %collective-permute-start.13 = (bf16[256,1024]{1,0:T(8,128)(2,1)S(1)}, bf16[256,1024]{1,0:T(8,128)(2,1)}, u32[]{:S(2)}, u32[]{:S(2)}) collective-permute-start(bf16[256,1024]{1,0:T(8,128)(2,1)S(1)} %collective-permute-done.10.refs_1_), channel_id=1, source_target_pairs={{0,1},{1,2},{2,3},{3,0},{4,7},{5,4},{6,5},{7,6},{8,9},{9,10},{10,1... | collective-permute-start | bytes 1572872 | tf_op jit(solution)/shard_map/ppermute | solution.py:35
  44.0 2.5 %collective-permute-start.16 = (bf16[2,128,1024]{2,1,0:T(8,128)(2,1)}, bf16[2,128,1024]{2,1,0:T(8,128)(2,1)}, u32[]{:S(2)}, u32[]{:S(2)}) collective-permute-start(bf16[2,128,1024]{2,1,0:T(8,128)(2,1)} %broadcast_select_fusion.14), channel_id=1, source_target_pairs={{0,32},{4,100},{8,40},{12,108},{16,48},{20,116},{24,56},{28,124},{... | collective-permute-start | bytes 1572872 | tf_op jit(solution)/shard_map/ppermute | solution.py:25
  46.5 6.0 %collective-permute-done.13.refs_2_ = bf16[256,1024]{1,0:T(8,128)(2,1)} collective-permute-done((bf16[256,1024]{1,0:T(8,128)(2,1)S(1)}, bf16[256,1024]{1,0:T(8,128)(2,1)}, u32[]{:S(2)}, u32[]{:S(2)}) %collective-permute-start.13) | collective-permute-done | bytes 524320 | tf_op jit(solution)/shard_map/ppermute | solution.py:35
  52.9 0.9 broadcast_select_fusion.12
  53.8 3.0 %collective-permute-start.14 = (bf16[2,128,1024]{2,1,0:T(8,128)(2,1)}, bf16[2,128,1024]{2,1,0:T(8,128)(2,1)}, u32[]{:S(2)}, u32[]{:S(2)}) collective-permute-start(bf16[2,128,1024]{2,1,0:T(8,128)(2,1)} %broadcast_select_fusion.12), channel_id=1, source_target_pairs={{0,96},{4,36},{8,104},{12,44},{16,112},{20,52},{24,120},{28,60},{3... | collective-permute-start | bytes 1572872 | tf_op jit(solution)/shard_map/ppermute | solution.py:25
  58.2 1.0 copy-done.3
  59.2 3.5 %shard_map.74 = bf16[256,1536]{1,0:T(8,128)(2,1)S(1)} custom-call(s32[1,32]{1,0:T(1,128)S(1)} %constant_dynamic-slice_fusion.at_ref, s32[64]{0:T(128)S(1)} %reshape.184.place_ref, s32[4]{0:T(128)S(1)} %subtract_and_fusion.base_ref, bf16[256,1024]{1,0:T(8,128)(2,1)S(1)} %bitcast.58, bf16[256,1024]{1,0:T(8,128)(2,1)S(1)} %copy-done.3, ...), custom_call_target="tpu_custom_call" | custom-call | flops 1 | bytes 1 | tf_op jit(solution)/shard_map/pallas_call | solution.py:118
  62.8 1.3 broadcast_select_fusion.9
  64.1 3.0 %collective-permute-start.21 = (bf16[2,128,1024]{2,1,0:T(8,128)(2,1)S(1)}, bf16[2,128,1024]{2,1,0:T(8,128)(2,1)S(1)}, u32[]{:S(2)}, u32[]{:S(2)}) collective-permute-start(bf16[2,128,1024]{2,1,0:T(8,128)(2,1)S(1)} %broadcast_select_fusion.9), channel_id=1, source_target_pairs={{0,96},{4,36},{8,104},{12,44},{16,112},{20,52},{24,120},{28,60},{3... | collective-permute-start | bytes 1572872 | tf_op jit(solution)/shard_map/ppermute | solution.py:25
  67.4 3.5 %shard_map.75 = bf16[256,1536]{1,0:T(8,128)(2,1)S(1)} custom-call(s32[1,32]{1,0:T(1,128)S(1)} %constant_dynamic-slice_fusion.at_ref, s32[64]{0:T(128)S(1)} %reshape.184.place_ref, s32[4]{0:T(128)S(1)} %subtract_and_fusion.base_ref, bf16[256,1024]{1,0:T(8,128)(2,1)S(1)} %bitcast.56, bf16[256,1024]{1,0:T(8,128)(2,1)S(1)} %copy-done.1, ...), custom_call_target="tpu_custom_call" | custom-call | flops 1 | bytes 1 | tf_op jit(solution)/shard_map/pallas_call | solution.py:118
  70.9 1.3 broadcast_select_fusion.10
  72.3 2.3 %collective-permute-start.18 = (bf16[2,128,1024]{2,1,0:T(8,128)(2,1)S(1)}, bf16[2,128,1024]{2,1,0:T(8,128)(2,1)S(1)}, u32[]{:S(2)}, u32[]{:S(2)}) collective-permute-start(bf16[2,128,1024]{2,1,0:T(8,128)(2,1)S(1)} %broadcast_select_fusion.10), channel_id=1, source_target_pairs={{0,24},{4,12},{8,16},{12,4},{16,8},{20,28},{24,0},{28,20},{32,56},... | collective-permute-start | bytes 1572872 | tf_op jit(solution)/shard_map/ppermute | solution.py:25
  75.1 8.0 %collective-permute-done.20 = bf16[2,128,1536]{2,1,0:T(8,128)(2,1)S(1)} collective-permute-done((bf16[2,128,1536]{2,1,0:T(8,128)(2,1)S(1)}, bf16[2,128,1536]{2,1,0:T(8,128)(2,1)S(1)}, u32[]{:S(2)}, u32[]{:S(2)}) %collective-permute-start.20) | collective-permute-done | bytes 786464 | tf_op jit(solution)/shard_map/ppermute | solution.py:25
  83.3 1.1 collective-permute-done.19
  84.5 1.9 %collective-permute-start.23 = (bf16[2,128,1536]{2,1,0:T(8,128)(2,1)S(1)}, bf16[2,128,1536]{2,1,0:T(8,128)(2,1)S(1)}, u32[]{:S(2)}, u32[]{:S(2)}) collective-permute-start(bf16[2,128,1536]{2,1,0:T(8,128)(2,1)S(1)} %broadcast_select_fusion.7), channel_id=1, source_target_pairs={{0,8},{4,28},{8,0},{12,20},{16,24},{20,12},{24,16},{28,4},{32,40},... | collective-permute-start | bytes 2359304 | tf_op jit(solution)/shard_map/ppermute | solution.py:25
  87.1 9.2 %collective-permute-done.24 = bf16[2,128,1536]{2,1,0:T(8,128)(2,1)S(1)} collective-permute-done((bf16[2,128,1536]{2,1,0:T(8,128)(2,1)S(1)}, bf16[2,128,1536]{2,1,0:T(8,128)(2,1)S(1)}, u32[]{:S(2)}, u32[]{:S(2)}) %collective-permute-start.24) | collective-permute-done | bytes 786464 | tf_op jit(solution)/shard_map/ppermute | solution.py:25
  97.4 2.5 %collective-permute-start.32 = (bf16[2,128,1536]{2,1,0:T(8,128)(2,1)S(1)}, bf16[2,128,1536]{2,1,0:T(8,128)(2,1)S(1)}, u32[]{:S(2)}, u32[]{:S(2)}) collective-permute-start(bf16[2,128,1536]{2,1,0:T(8,128)(2,1)S(1)} %broadcast_select_fusion.5), channel_id=1, source_target_pairs={{0,24},{4,12},{8,16},{12,4},{16,8},{20,28},{24,0},{28,20},{32,56},... | collective-permute-start | bytes 2359304 | tf_op jit(solution)/shard_map/ppermute | solution.py:25
  99.9 7.4 %collective-permute-done.28.refs_2_ = bf16[256,1024]{1,0:T(8,128)(2,1)S(1)} collective-permute-done((bf16[256,1024]{1,0:T(8,128)(2,1)S(1)}, bf16[256,1024]{1,0:T(8,128)(2,1)S(1)}, u32[]{:S(2)}, u32[]{:S(2)}) %collective-permute-start.28) | collective-permute-done | bytes 524320 | tf_op jit(solution)/shard_map/ppermute | solution.py:35
  107.4 2.3 %collective-permute-done.27 = bf16[2,128,1536]{2,1,0:T(8,128)(2,1)S(1)} collective-permute-done((bf16[2,128,1536]{2,1,0:T(8,128)(2,1)S(1)}, bf16[2,128,1536]{2,1,0:T(8,128)(2,1)S(1)}, u32[]{:S(2)}, u32[]{:S(2)}) %collective-permute-start.27) | collective-permute-done | bytes 786464 | tf_op jit(solution)/shard_map/ppermute | solution.py:25
  109.9 3.1 %collective-permute-start.30 = (bf16[2,128,1536]{2,1,0:T(8,128)(2,1)S(1)}, bf16[2,128,1536]{2,1,0:T(8,128)(2,1)S(1)}, u32[]{:S(2)}, u32[]{:S(2)}) collective-permute-start(bf16[2,128,1536]{2,1,0:T(8,128)(2,1)S(1)} %broadcast_select_fusion.3), channel_id=1, source_target_pairs={{0,24},{4,12},{8,16},{12,4},{16,8},{20,28},{24,0},{28,20},{32,56},... | collective-permute-start | bytes 2359304 | tf_op jit(solution)/shard_map/ppermute | solution.py:25
  113.0 4.7 %collective-permute-done.26.refs_2_ = bf16[256,1024]{1,0:T(8,128)(2,1)S(1)} collective-permute-done((bf16[256,1024]{1,0:T(8,128)(2,1)S(1)}, bf16[256,1024]{1,0:T(8,128)(2,1)S(1)}, u32[]{:S(2)}, u32[]{:S(2)}) %collective-permute-start.26) | collective-permute-done | bytes 524320 | tf_op jit(solution)/shard_map/ppermute | solution.py:35
  117.8 3.0 %collective-permute-start.33 = (bf16[2,128,1536]{2,1,0:T(8,128)(2,1)S(1)}, bf16[2,128,1536]{2,1,0:T(8,128)(2,1)S(1)}, u32[]{:S(2)}, u32[]{:S(2)}) collective-permute-start(bf16[2,128,1536]{2,1,0:T(8,128)(2,1)S(1)} %broadcast_select_fusion.1), channel_id=1, source_target_pairs={{0,96},{4,36},{8,104},{12,44},{16,112},{20,52},{24,120},{28,60},{3... | collective-permute-start | bytes 2359304 | tf_op jit(solution)/shard_map/ppermute | solution.py:25
  120.8 2.4 %collective-permute-done.31.refs_3_ = bf16[256,1024]{1,0:T(8,128)(2,1)S(1)} collective-permute-done((bf16[256,1024]{1,0:T(8,128)(2,1)S(1)}, bf16[256,1024]{1,0:T(8,128)(2,1)S(1)}, u32[]{:S(2)}, u32[]{:S(2)}) %collective-permute-start.31) | collective-permute-done | bytes 524320 | tf_op jit(solution)/shard_map/ppermute | solution.py:35
  123.2 4.4 %shard_map.76.refs_5_ = bf16[1024,1536]{1,0:T(8,128)(2,1)} custom-call(s32[1,32]{1,0:T(1,128)S(1)} %constant_dynamic-slice_fusion.at_ref, s32[64]{0:T(128)S(1)} %reshape.184.place_ref, s32[4]{0:T(128)S(1)} %subtract_and_fusion.base_ref, bf16[256,1024]{1,0:T(8,128)(2,1)S(1)} %bitcast.60, bf16[256,1024]{1,0:T(8,128)(2,1)S(1)} %collective-permute-done.25.refs_1_, ...), custom_call_target="tpu_custom_call" | custom-call | flops 1 | bytes 1 | tf_op jit(solution)/shard_map/pallas_call | solution.py:118
  128.1 10.2 %collective-permute-done.29.refs_3_ = bf16[256,1024]{1,0:T(8,128)(2,1)S(1)} collective-permute-done((bf16[256,1024]{1,0:T(8,128)(2,1)S(1)}, bf16[256,1024]{1,0:T(8,128)(2,1)S(1)}, u32[]{:S(2)}, u32[]{:S(2)}) %collective-permute-start.29) | collective-permute-done | bytes 524320 | tf_op jit(solution)/shard_map/ppermute | solution.py:35
  138.3 4.4 %shard_map.77 = bf16[1024,1536]{1,0:T(8,128)(2,1)} custom-call(s32[1,32]{1,0:T(1,128)S(1)} %constant_dynamic-slice_fusion.at_ref, s32[64]{0:T(128)S(1)} %reshape.184.place_ref, s32[4]{0:T(128)S(1)} %subtract_and_fusion.base_ref, bf16[256,1024]{1,0:T(8,128)(2,1)S(1)} %bitcast.62, ...), custom_call_target="tpu_custom_call", output_to_operand_aliasing={{}: (8, {})} | custom-call | flops 1 | bytes 1 | tf_op jit(solution)/shard_map/pallas_call | solution.py:118
  142.9 0.9 constant_dynamic-update-slice_fusion.1
  143.9 0.9 constant_dynamic-update-slice_fusion
  (73 shorter events, 9.5 us)
Async XLA Ops:
  0.0 8.0 %copy-start.4 = (bf16[1024,1024]{1,0:T(8,128)(2,1)S(1)}, bf16[1024,1024]{1,0:T(8,128)(2,1)}, u32[]{:S(2)}) copy-start(bf16[1024,1024]{1,0:T(8,128)(2,1)} %param.7) | copy-start | bytes 6291460
  0.0 5.7 %collective-permute-start.1 = (bf16[8,128,1024]{2,1,0:T(8,128)(2,1)}, bf16[8,128,1024]{2,1,0:T(8,128)(2,1)}, u32[]{:S(2)}, u32[]{:S(2)}) collective-permute-start(bf16[8,128,1024]{2,1,0:T(8,128)(2,1)} %bitcast.65), channel_id=1, source_target_pairs={{0,4},{4,0},{8,12},{12,8},{16,20},{20,16},{24,28},{28,24},{32,36},... | collective-permute-start | bytes 6291464 | tf_op jit(solution)/shard_map/ppermute | solution.py:25
  1.8 5.2 %collective-permute-start = (bf16[1,144,256]{2,1,0:T(8,128)(2,1)}, bf16[1,144,256]{2,1,0:T(8,128)(2,1)S(1)}, u32[]{:S(2)}, u32[]{:S(2)}) collective-permute-start(bf16[1,144,256]{2,1,0:T(8,128)(2,1)} %shard_map.73), channel_id=1, source_target_pairs={{0,8},{4,28},{8,0},{12,20},{16,24},{20,12},{24,16},{28,4},{32,40},... | collective-permute-start | bytes 221192 | tf_op jit(solution)/shard_map/ppermute | solution.py:25
  10.4 14.8 %collective-permute-start.5 = (bf16[256,1024]{1,0:T(8,128)(2,1)S(1)}, bf16[256,1024]{1,0:T(8,128)(2,1)S(1)}, u32[]{:S(2)}, u32[]{:S(2)}) collective-permute-start(bf16[256,1024]{1,0:T(8,128)(2,1)S(1)} %bitcast.57), channel_id=1, source_target_pairs={{0,1},{1,2},{2,3},{3,0},{4,7},{5,4},{6,5},{7,6},{8,9},{9,10},{10,1... | collective-permute-start | bytes 1572872 | tf_op jit(solution)/shard_map/ppermute | solution.py:35
  12.3 12.9 %collective-permute-start.4 = (bf16[2,128,1024]{2,1,0:T(8,128)(2,1)S(1)}, bf16[2,128,1024]{2,1,0:T(8,128)(2,1)S(1)}, u32[]{:S(2)}, u32[]{:S(2)}) collective-permute-start(bf16[2,128,1024]{2,1,0:T(8,128)(2,1)S(1)} %slice_select_fusion.1), channel_id=1, source_target_pairs={{0,8},{4,28},{8,0},{12,20},{16,24},{20,12},{24,16},{28,4},{32,40},... | collective-permute-start | bytes 1572872 | tf_op jit(solution)/shard_map/ppermute | solution.py:25
  13.3 19.8 %collective-permute-start.10 = (bf16[256,1024]{1,0:T(8,128)(2,1)S(1)}, bf16[256,1024]{1,0:T(8,128)(2,1)S(1)}, u32[]{:S(2)}, u32[]{:S(2)}) collective-permute-start(bf16[256,1024]{1,0:T(8,128)(2,1)S(1)} %bitcast.55), channel_id=1, source_target_pairs={{0,1},{1,2},{2,3},{3,0},{4,7},{5,4},{6,5},{7,6},{8,9},{9,10},{10,1... | collective-permute-start | bytes 1572872 | tf_op jit(solution)/shard_map/ppermute | solution.py:35
  15.2 7.9 %collective-permute-start.2 = (bf16[2,144,256]{2,1,0:T(8,128)(2,1)S(1)}, bf16[2,144,256]{2,1,0:T(8,128)(2,1)S(1)}, u32[]{:S(2)}, u32[]{:S(2)}) collective-permute-start(bf16[2,144,256]{2,1,0:T(8,128)(2,1)S(1)} %pad_maximum_fusion.4), channel_id=1, source_target_pairs={{0,24},{4,12},{8,16},{12,4},{16,8},{20,28},{24,0},{28,20},{32,56},... | collective-permute-start | bytes 442376 | tf_op jit(solution)/shard_map/ppermute | solution.py:25
  23.1 6.8 %collective-permute-start.3 = (bf16[4,144,256]{2,1,0:T(8,128)(2,1)S(1)}, bf16[4,144,256]{2,1,0:T(8,128)(2,1)S(1)}, u32[]{:S(2)}, u32[]{:S(2)}) collective-permute-start(bf16[4,144,256]{2,1,0:T(8,128)(2,1)S(1)} %pad_maximum_fusion.3), channel_id=1, source_target_pairs={{0,32},{4,100},{8,40},{12,108},{16,48},{20,116},{24,56},{28,124},{... | collective-permute-start | bytes 884744 | tf_op jit(solution)/shard_map/ppermute | solution.py:25
  24.7 14.0 %collective-permute-start.9 = (bf16[2,128,1024]{2,1,0:T(8,128)(2,1)S(1)}, bf16[2,128,1024]{2,1,0:T(8,128)(2,1)S(1)}, u32[]{:S(2)}, u32[]{:S(2)}) collective-permute-start(bf16[2,128,1024]{2,1,0:T(8,128)(2,1)S(1)} %slice_select_fusion), channel_id=1, source_target_pairs={{0,32},{4,100},{8,40},{12,108},{16,48},{20,116},{24,56},{28,124},{... | collective-permute-start | bytes 1572872 | tf_op jit(solution)/shard_map/ppermute | solution.py:25
  25.2 13.7 %copy-start.2 = (bf16[256,1024]{1,0:T(8,128)(2,1)}, bf16[256,1024]{1,0:T(8,128)(2,1)S(1)}, u32[]{:S(2)}) copy-start(bf16[256,1024]{1,0:T(8,128)(2,1)S(1)} %collective-permute-done.5.refs_1_) | copy-start | bytes 1572868
  25.3 13.6 %collective-permute-start.8 = (bf16[256,1024]{1,0:T(8,128)(2,1)S(1)}, bf16[256,1024]{1,0:T(8,128)(2,1)}, u32[]{:S(2)}, u32[]{:S(2)}) collective-permute-start(bf16[256,1024]{1,0:T(8,128)(2,1)S(1)} %collective-permute-done.5.refs_1_), channel_id=1, source_target_pairs={{0,1},{1,2},{2,3},{3,0},{4,7},{5,4},{6,5},{7,6},{8,9},{9,10},{10,1... | collective-permute-start | bytes 1572872 | tf_op jit(solution)/shard_map/ppermute | solution.py:35
  27.1 11.8 %collective-permute-start.7 = (bf16[2,128,1024]{2,1,0:T(8,128)(2,1)S(1)}, bf16[2,128,1024]{2,1,0:T(8,128)(2,1)S(1)}, u32[]{:S(2)}, u32[]{:S(2)}) collective-permute-start(bf16[2,128,1024]{2,1,0:T(8,128)(2,1)S(1)} %broadcast_select_fusion.15), channel_id=1, source_target_pairs={{0,24},{4,12},{8,16},{12,4},{16,8},{20,28},{24,0},{28,20},{32,56},... | collective-permute-start | bytes 1572872 | tf_op jit(solution)/shard_map/ppermute | solution.py:25
  29.9 11.7 %collective-permute-start.6 = (bf16[8,144,256]{2,1,0:T(8,128)(2,1)S(1)}, bf16[8,144,256]{2,1,0:T(8,128)(2,1)S(1)}, u32[]{:S(2)}, u32[]{:S(2)}) collective-permute-start(bf16[8,144,256]{2,1,0:T(8,128)(2,1)S(1)} %pad_maximum_fusion.2), channel_id=1, source_target_pairs={{0,96},{4,36},{8,104},{12,44},{16,112},{20,52},{24,120},{28,60},{3... | collective-permute-start | bytes 1769480 | tf_op jit(solution)/shard_map/ppermute | solution.py:25
  33.0 8.9 %copy-start = (bf16[256,1024]{1,0:T(8,128)(2,1)}, bf16[256,1024]{1,0:T(8,128)(2,1)S(1)}, u32[]{:S(2)}) copy-start(bf16[256,1024]{1,0:T(8,128)(2,1)S(1)} %collective-permute-done.10.refs_1_) | copy-start | bytes 1572868
  41.7 15.0 %collective-permute-start.11 = (bf16[16,144,256]{2,1,0:T(8,128)(2,1)S(1)}, bf16[16,144,256]{2,1,0:T(8,128)(2,1)S(1)}, u32[]{:S(2)}, u32[]{:S(2)}) collective-permute-start(bf16[16,144,256]{2,1,0:T(8,128)(2,1)S(1)} %pad_maximum_fusion.1), channel_id=1, source_target_pairs={{0,4},{4,0},{8,12},{12,8},{16,20},{20,16},{24,28},{28,24},{32,36},... | collective-permute-start | bytes 3538952 | tf_op jit(solution)/shard_map/ppermute | solution.py:25
  41.9 10.5 %collective-permute-start.13 = (bf16[256,1024]{1,0:T(8,128)(2,1)S(1)}, bf16[256,1024]{1,0:T(8,128)(2,1)}, u32[]{:S(2)}, u32[]{:S(2)}) collective-permute-start(bf16[256,1024]{1,0:T(8,128)(2,1)S(1)} %collective-permute-done.10.refs_1_), channel_id=1, source_target_pairs={{0,1},{1,2},{2,3},{3,0},{4,7},{5,4},{6,5},{7,6},{8,9},{9,10},{10,1... | collective-permute-start | bytes 1572872 | tf_op jit(solution)/shard_map/ppermute | solution.py:35
  43.6 9.3 %collective-permute-start.12 = (bf16[2,128,1024]{2,1,0:T(8,128)(2,1)S(1)}, bf16[2,128,1024]{2,1,0:T(8,128)(2,1)S(1)}, u32[]{:S(2)}, u32[]{:S(2)}) collective-permute-start(bf16[2,128,1024]{2,1,0:T(8,128)(2,1)S(1)} %broadcast_select_fusion.13), channel_id=1, source_target_pairs={{0,8},{4,28},{8,0},{12,20},{16,24},{20,12},{24,16},{28,4},{32,40},... | collective-permute-start | bytes 1572872 | tf_op jit(solution)/shard_map/ppermute | solution.py:25
  43.8 14.2 %collective-permute-start.17 = (bf16[256,1024]{1,0:T(8,128)(2,1)}, bf16[256,1024]{1,0:T(8,128)(2,1)}, u32[]{:S(2)}, u32[]{:S(2)}) collective-permute-start(bf16[256,1024]{1,0:T(8,128)(2,1)} %collective-permute-done.8.refs_2_), channel_id=1, source_target_pairs={{0,1},{1,2},{2,3},{3,0},{4,7},{5,4},{6,5},{7,6},{8,9},{9,10},{10,1... | collective-permute-start | bytes 1572872 | tf_op jit(solution)/shard_map/ppermute | solution.py:35
  44.0 18.8 %collective-permute-start.16 = (bf16[2,128,1024]{2,1,0:T(8,128)(2,1)}, bf16[2,128,1024]{2,1,0:T(8,128)(2,1)}, u32[]{:S(2)}, u32[]{:S(2)}) collective-permute-start(bf16[2,128,1024]{2,1,0:T(8,128)(2,1)} %broadcast_select_fusion.14), channel_id=1, source_target_pairs={{0,32},{4,100},{8,40},{12,108},{16,48},{20,116},{24,56},{28,124},{... | collective-permute-start | bytes 1572872 | tf_op jit(solution)/shard_map/ppermute | solution.py:25
  52.4 14.9 %collective-permute-start.15 = (bf16[256,1024]{1,0:T(8,128)(2,1)}, bf16[256,1024]{1,0:T(8,128)(2,1)}, u32[]{:S(2)}, u32[]{:S(2)}) collective-permute-start(bf16[256,1024]{1,0:T(8,128)(2,1)} %collective-permute-done.13.refs_2_), channel_id=1, source_target_pairs={{0,1},{1,2},{2,3},{3,0},{4,7},{5,4},{6,5},{7,6},{8,9},{9,10},{10,1... | collective-permute-start | bytes 1572872 | tf_op jit(solution)/shard_map/ppermute | solution.py:35
  53.8 17.1 %collective-permute-start.14 = (bf16[2,128,1024]{2,1,0:T(8,128)(2,1)}, bf16[2,128,1024]{2,1,0:T(8,128)(2,1)}, u32[]{:S(2)}, u32[]{:S(2)}) collective-permute-start(bf16[2,128,1024]{2,1,0:T(8,128)(2,1)} %broadcast_select_fusion.12), channel_id=1, source_target_pairs={{0,96},{4,36},{8,104},{12,44},{16,112},{20,52},{24,120},{28,60},{3... | collective-permute-start | bytes 1572872 | tf_op jit(solution)/shard_map/ppermute | solution.py:25
  58.2 1.0 copy-start.3
  59.2 8.2 %copy-start.1 = (bf16[256,1024]{1,0:T(8,128)(2,1)S(1)}, bf16[256,1024]{1,0:T(8,128)(2,1)}, u32[]{:S(2)}) copy-start(bf16[256,1024]{1,0:T(8,128)(2,1)} %copy-done) | copy-start | bytes 1572868
  64.1 10.7 %collective-permute-start.21 = (bf16[2,128,1024]{2,1,0:T(8,128)(2,1)S(1)}, bf16[2,128,1024]{2,1,0:T(8,128)(2,1)S(1)}, u32[]{:S(2)}, u32[]{:S(2)}) collective-permute-start(bf16[2,128,1024]{2,1,0:T(8,128)(2,1)S(1)} %broadcast_select_fusion.9), channel_id=1, source_target_pairs={{0,96},{4,36},{8,104},{12,44},{16,112},{20,52},{24,120},{28,60},{3... | collective-permute-start | bytes 1572872 | tf_op jit(solution)/shard_map/ppermute | solution.py:25
  67.1 16.0 %collective-permute-start.20 = (bf16[2,128,1536]{2,1,0:T(8,128)(2,1)S(1)}, bf16[2,128,1536]{2,1,0:T(8,128)(2,1)S(1)}, u32[]{:S(2)}, u32[]{:S(2)}) collective-permute-start(bf16[2,128,1536]{2,1,0:T(8,128)(2,1)S(1)} %bitcast.51), channel_id=1, source_target_pairs={{0,8},{4,28},{8,0},{12,20},{16,24},{20,12},{24,16},{28,4},{32,40},... | collective-permute-start | bytes 2359304 | tf_op jit(solution)/shard_map/ppermute | solution.py:25
  72.2 12.1 %collective-permute-start.19 = (bf16[2,128,1536]{2,1,0:T(8,128)(2,1)S(1)}, bf16[2,128,1536]{2,1,0:T(8,128)(2,1)S(1)}, u32[]{:S(2)}, u32[]{:S(2)}) collective-permute-start(bf16[2,128,1536]{2,1,0:T(8,128)(2,1)S(1)} %bitcast.53), channel_id=1, source_target_pairs={{0,32},{4,100},{8,40},{12,108},{16,48},{20,116},{24,56},{28,124},{... | collective-permute-start | bytes 2359304 | tf_op jit(solution)/shard_map/ppermute | solution.py:25
  72.3 12.1 %collective-permute-start.18 = (bf16[2,128,1024]{2,1,0:T(8,128)(2,1)S(1)}, bf16[2,128,1024]{2,1,0:T(8,128)(2,1)S(1)}, u32[]{:S(2)}, u32[]{:S(2)}) collective-permute-start(bf16[2,128,1024]{2,1,0:T(8,128)(2,1)S(1)} %broadcast_select_fusion.10), channel_id=1, source_target_pairs={{0,24},{4,12},{8,16},{12,4},{16,8},{20,28},{24,0},{28,20},{32,56},... | collective-permute-start | bytes 1572872 | tf_op jit(solution)/shard_map/ppermute | solution.py:25
  74.9 12.3 %collective-permute-start.25 = (bf16[256,1024]{1,0:T(8,128)(2,1)S(1)}, bf16[256,1024]{1,0:T(8,128)(2,1)S(1)}, u32[]{:S(2)}, u32[]{:S(2)}) collective-permute-start(bf16[256,1024]{1,0:T(8,128)(2,1)S(1)} %bitcast.59), channel_id=1, source_target_pairs={{0,1},{1,2},{2,3},{3,0},{4,7},{5,4},{6,5},{7,6},{8,9},{9,10},{10,1... | collective-permute-start | bytes 1572872 | tf_op jit(solution)/shard_map/ppermute | solution.py:35
  84.3 12.0 %collective-permute-start.24 = (bf16[2,128,1536]{2,1,0:T(8,128)(2,1)S(1)}, bf16[2,128,1536]{2,1,0:T(8,128)(2,1)S(1)}, u32[]{:S(2)}, u32[]{:S(2)}) collective-permute-start(bf16[2,128,1536]{2,1,0:T(8,128)(2,1)S(1)} %broadcast_select_fusion.6), channel_id=1, source_target_pairs={{0,32},{4,100},{8,40},{12,108},{16,48},{20,116},{24,56},{28,124},{... | collective-permute-start | bytes 2359304 | tf_op jit(solution)/shard_map/ppermute | solution.py:25
  84.5 12.7 %collective-permute-start.23 = (bf16[2,128,1536]{2,1,0:T(8,128)(2,1)S(1)}, bf16[2,128,1536]{2,1,0:T(8,128)(2,1)S(1)}, u32[]{:S(2)}, u32[]{:S(2)}) collective-permute-start(bf16[2,128,1536]{2,1,0:T(8,128)(2,1)S(1)} %broadcast_select_fusion.7), channel_id=1, source_target_pairs={{0,8},{4,28},{8,0},{12,20},{16,24},{20,12},{24,16},{28,4},{32,40},... | collective-permute-start | bytes 2359304 | tf_op jit(solution)/shard_map/ppermute | solution.py:25
  86.5 13.3 %collective-permute-start.22 = (bf16[256,1024]{1,0:T(8,128)(2,1)S(1)}, bf16[256,1024]{1,0:T(8,128)(2,1)S(1)}, u32[]{:S(2)}, u32[]{:S(2)}) collective-permute-start(bf16[256,1024]{1,0:T(8,128)(2,1)S(1)} %bitcast.61), channel_id=1, source_target_pairs={{0,1},{1,2},{2,3},{3,0},{4,7},{5,4},{6,5},{7,6},{8,9},{9,10},{10,1... | collective-permute-start | bytes 1572872 | tf_op jit(solution)/shard_map/ppermute | solution.py:35
  96.5 13.3 %collective-permute-start.27 = (bf16[2,128,1536]{2,1,0:T(8,128)(2,1)S(1)}, bf16[2,128,1536]{2,1,0:T(8,128)(2,1)S(1)}, u32[]{:S(2)}, u32[]{:S(2)}) collective-permute-start(bf16[2,128,1536]{2,1,0:T(8,128)(2,1)S(1)} %broadcast_select_fusion.4), channel_id=1, source_target_pairs={{0,96},{4,36},{8,104},{12,44},{16,112},{20,52},{24,120},{28,60},{3... | collective-permute-start | bytes 2359304 | tf_op jit(solution)/shard_map/ppermute | solution.py:25
  96.8 10.4 %collective-permute-start.28 = (bf16[256,1024]{1,0:T(8,128)(2,1)S(1)}, bf16[256,1024]{1,0:T(8,128)(2,1)S(1)}, u32[]{:S(2)}, u32[]{:S(2)}) collective-permute-start(bf16[256,1024]{1,0:T(8,128)(2,1)S(1)} %collective-permute-done.25.refs_1_), channel_id=1, source_target_pairs={{0,1},{1,2},{2,3},{3,0},{4,7},{5,4},{6,5},{7,6},{8,9},{9,10},{10,1... | collective-permute-start | bytes 1572872 | tf_op jit(solution)/shard_map/ppermute | solution.py:35
  97.4 20.3 %collective-permute-start.32 = (bf16[2,128,1536]{2,1,0:T(8,128)(2,1)S(1)}, bf16[2,128,1536]{2,1,0:T(8,128)(2,1)S(1)}, u32[]{:S(2)}, u32[]{:S(2)}) collective-permute-start(bf16[2,128,1536]{2,1,0:T(8,128)(2,1)S(1)} %broadcast_select_fusion.5), channel_id=1, source_target_pairs={{0,24},{4,12},{8,16},{12,4},{16,8},{20,28},{24,0},{28,20},{32,56},... | collective-permute-start | bytes 2359304 | tf_op jit(solution)/shard_map/ppermute | solution.py:25
  107.2 10.4 %collective-permute-start.26 = (bf16[256,1024]{1,0:T(8,128)(2,1)S(1)}, bf16[256,1024]{1,0:T(8,128)(2,1)S(1)}, u32[]{:S(2)}, u32[]{:S(2)}) collective-permute-start(bf16[256,1024]{1,0:T(8,128)(2,1)S(1)} %collective-permute-done.22.refs_1_), channel_id=1, source_target_pairs={{0,1},{1,2},{2,3},{3,0},{4,7},{5,4},{6,5},{7,6},{8,9},{9,10},{10,1... | collective-permute-start | bytes 1572872 | tf_op jit(solution)/shard_map/ppermute | solution.py:35
  107.2 16.0 %collective-permute-start.31 = (bf16[256,1024]{1,0:T(8,128)(2,1)S(1)}, bf16[256,1024]{1,0:T(8,128)(2,1)S(1)}, u32[]{:S(2)}, u32[]{:S(2)}) collective-permute-start(bf16[256,1024]{1,0:T(8,128)(2,1)S(1)} %collective-permute-done.28.refs_2_), channel_id=1, source_target_pairs={{0,1},{1,2},{2,3},{3,0},{4,7},{5,4},{6,5},{7,6},{8,9},{9,10},{10,1... | collective-permute-start | bytes 1572872 | tf_op jit(solution)/shard_map/ppermute | solution.py:35
  109.9 18.1 %collective-permute-start.30 = (bf16[2,128,1536]{2,1,0:T(8,128)(2,1)S(1)}, bf16[2,128,1536]{2,1,0:T(8,128)(2,1)S(1)}, u32[]{:S(2)}, u32[]{:S(2)}) collective-permute-start(bf16[2,128,1536]{2,1,0:T(8,128)(2,1)S(1)} %broadcast_select_fusion.3), channel_id=1, source_target_pairs={{0,24},{4,12},{8,16},{12,4},{16,8},{20,28},{24,0},{28,20},{32,56},... | collective-permute-start | bytes 2359304 | tf_op jit(solution)/shard_map/ppermute | solution.py:25
  117.8 25.0 %collective-permute-start.33 = (bf16[2,128,1536]{2,1,0:T(8,128)(2,1)S(1)}, bf16[2,128,1536]{2,1,0:T(8,128)(2,1)S(1)}, u32[]{:S(2)}, u32[]{:S(2)}) collective-permute-start(bf16[2,128,1536]{2,1,0:T(8,128)(2,1)S(1)} %broadcast_select_fusion.1), channel_id=1, source_target_pairs={{0,96},{4,36},{8,104},{12,44},{16,112},{20,52},{24,120},{28,60},{3... | collective-permute-start | bytes 2359304 | tf_op jit(solution)/shard_map/ppermute | solution.py:25
  127.7 10.7 %collective-permute-start.29 = (bf16[256,1024]{1,0:T(8,128)(2,1)S(1)}, bf16[256,1024]{1,0:T(8,128)(2,1)S(1)}, u32[]{:S(2)}, u32[]{:S(2)}) collective-permute-start(bf16[256,1024]{1,0:T(8,128)(2,1)S(1)} %collective-permute-done.26.refs_2_), channel_id=1, source_target_pairs={{0,1},{1,2},{2,3},{3,0},{4,7},{5,4},{6,5},{7,6},{8,9},{9,10},{10,1... | collective-permute-start | bytes 1572872 | tf_op jit(solution)/shard_map/ppermute | solution.py:35

commit v3 on v2

--- a/solution.py
+++ b/solution.py
@@ -132,7 +132,7 @@
         ),
         out_shape=jax.ShapeDtypeStruct((rows_all, WIDTH), jnp.bfloat16),
         input_output_aliases=aliases,
-        compiler_params=pltpu.CompilerParams(vmem_limit_bytes=24 * 2**20),
+        compiler_params=pltpu.CompilerParams(vmem_limit_bytes=16 * 2**20),
         cost_estimate=pl.CostEstimate(flops=1, bytes_accessed=1, transcendentals=0),
     )(at, place, base, *args)
 
@@ -152,12 +152,12 @@
         return self.token
 
 
-PAIRS = ((0, 2), (2, 4), (4, 6), (6, 8))
+SPANS = ((0, 2), (2, 4), (4, 6), (6, 8))
 PATHS = (
+    (Y_A, Y_B, X_A, X_B),
     (X_A, X_B, Y_A, Y_B),
-    (Y_A, X_A, Y_B, X_B),
-    (Y_A, X_A, X_B, Y_B),
     (X_A, Y_A, Y_B, X_B),
+    (Y_A, Y_B, X_A, X_B),
 )
 
 
@@ -216,108 +216,110 @@
             partner, mine = seq.tied(self.partner, self.value)
             self.value = seq.done(jnp.concatenate([mine, partner], axis=0))
 
-    class Swapped:
-        def __init__(self):
-            self.partner = exchange(slots, CORE)
-
-        def pair(self, low, high):
-            other, mine = seq.tied(self.partner, slots)
-            return seq.done(choose(flags, CORE, low, high, other[low:high], mine[low:high]))
-
-    def times(ring):
+    swapped = exchange(slots, CORE)
+
+    def group(number):
+        low, high = SPANS[number]
+        other, mine = seq.tied(swapped, slots)
+        value = seq.done(choose(flags, CORE, low, high, other[low:high], mine[low:high]))
+        return Moving(value, SPANS[number], PATHS[number])
+
+    def ring(moving):
+        return Ring(moving.value.reshape(-1, DEPTH))
+
+    def times(blocks, *place_in):
         live = tiles.value
         place = live[:, TILE, :].reshape(32, 2, TILE)[:, :, 0].astype(jnp.int32).reshape(64)
-        return product(ring.blocks, live, at, place, base)
-
-    def finish(ring, out, low):
-        live = tiles.value
-        place = live[:, TILE, :].reshape(32, 2, TILE)[:, :, 0].astype(jnp.int32).reshape(64)
-        return product(ring.blocks, live, at, place, base, out, low * TILE, SLOTS * TILE)
-
-    early, late, rings = [None] * 2, [None] * 2, [None] * 4
-    swapped = Swapped()
+        return seq.done(product(blocks, live, at, place, base, *place_in))
+
+    def onward(moving, blocks):
+        value = times(blocks).reshape(-1, TILE, WIDTH)
+        later = Moving(value, moving.cut, moving.order)
+        later.at = moving.at
+        return later
+
+    moving, rings = [None] * 4, [None] * 4
     tiles = Tiles(seq.done(pack(amplitudes, screen)))
     tiles.send()
-    rings[3] = Ring(swapped.pair(*PAIRS[3]).reshape(2 * TILE, DEPTH))
-    tiles.take()
+    moving[0] = group(0)
+    moving[3] = group(3)
+    moving[3].send()
+    tiles.take()
+    tiles.send()
+    moving[1] = group(1)
+    moving[1].send()
+    rings[0] = ring(moving[0])
+    rings[0].send()
+    moving[2] = group(2)
+    moving[2].send()
+    tiles.take()
+    tiles.send()
+    moving[3].take()
+    moving[3].send()
+    moving[1].take()
+    moving[1].send()
+    rings[0].take()
+    rings[0].send()
+    tiles.take()
+    tiles.send()
+    moving[2].take()
+    moving[2].send()
+    moving[3].take()
+    moving[3].send()
+    moving[1].take()
+    rings[0].take()
+    rings[0].send()
+    rings[1] = ring(moving[1])
+    rings[1].send()
+    tiles.take()
+    tiles.send()
+    moving[3].take()
+    moving[3].send()
+    tiles.take()
+    moving[2].take()
+    moving[2].send()
+    rings[0].take()
+    rings[1].take()
+    moving[0] = onward(moving[0], rings[0].blocks)
+    moving[0].send()
+    rings[1].send()
+    moving[3].take()
+    rings[3] = ring(moving[3])
     rings[3].send()
-    tiles.send()
-    rings[2] = Ring(swapped.pair(*PAIRS[2]).reshape(2 * TILE, DEPTH))
-    early[0] = Moving(swapped.pair(*PAIRS[0]), PAIRS[0], PATHS[0])
-    early[0].send()
+    moving[2].take()
+    moving[2].send()
+    rings[1].take()
+    rings[1].send()
+    moving[0].take()
+    moving[0].send()
+    rings[3].take()
+    moving[2].take()
+    rings[2] = ring(moving[2])
     rings[2].send()
-    early[1] = Moving(swapped.pair(*PAIRS[1]), PAIRS[1], PATHS[1])
-    tiles.take()
-    tiles.send()
-    early[1].send()
+    rings[3].send()
+    rings[1].take()
+    moving[1] = onward(moving[1], rings[1].blocks)
+    moving[1].send()
+    moving[0].take()
+    moving[0].send()
+    rings[2].take()
+    rings[2].send()
     rings[3].take()
     rings[3].send()
-    early[0].take()
-    early[0].send()
-    tiles.take()
-    tiles.send()
+    moving[1].take()
     rings[2].take()
     rings[2].send()
-    early[1].take()
-    early[1].send()
+    moving[1].send()
+    moving[0].take()
+    moving[0].send()
     rings[3].take()
-    rings[3].send()
-    early[0].take()
-    early[0].send()
-    tiles.take()
-    tiles.send()
+    out = times(rings[3].blocks, None, 6 * TILE, SLOTS * TILE)
     rings[2].take()
-    rings[2].send()
-    early[1].take()
-    early[1].send()
-    tiles.take()
-    rings[3].take()
-    value = seq.done(times(rings[3])).reshape(2, TILE, WIDTH)
-    late[1] = Moving(value, PAIRS[3], PATHS[3])
-    early[0].take()
-    early[0].send()
-    late[1].send()
-    rings[2].take()
-    value = seq.done(times(rings[2])).reshape(2, TILE, WIDTH)
-    late[0] = Moving(value, PAIRS[2], PATHS[2])
-    late[0].send()
-    early[1].take()
-    early[1].send()
-    early[0].take()
-    rings[0] = Ring(early[0].value.reshape(2 * TILE, DEPTH))
-    rings[0].send()
-    late[1].take()
-    late[1].send()
-    late[0].take()
-    late[0].send()
-    early[1].take()
-    rings[1] = Ring(early[1].value.reshape(2 * TILE, DEPTH))
-    rings[1].send()
-    rings[0].take()
-    rings[0].send()
-    late[1].take()
-    late[1].send()
-    late[0].take()
-    late[0].send()
-    rings[1].take()
-    rings[1].send()
-    rings[0].take()
-    rings[0].send()
-    late[1].take()
-    late[1].send()
-    rings[1].take()
-    rings[1].send()
-    late[0].take()
-    late[0].send()
-    rings[0].take()
-    out = seq.done(finish(rings[0], None, PAIRS[0][0]))
-    late[1].take()
-    rings[1].take()
-    out = seq.done(finish(rings[1], out, PAIRS[1][0]))
-    late[0].take()
-
-    for part, (low, _) in zip(late, PAIRS[2:]):
-        out = lax.dynamic_update_slice(out, part.value.reshape(2 * TILE, WIDTH), (low * TILE, 0))
+    out = times(rings[2].blocks, out, 4 * TILE, SLOTS * TILE)
+    moving[1].take()
+    moving[0].take()
+    out = lax.dynamic_update_slice(out, moving[0].value.reshape(-1, WIDTH), (0 * TILE, 0))
+    out = lax.dynamic_update_slice(out, moving[1].value.reshape(-1, WIDTH), (2 * TILE, 0))
     return out
 
 

time: 146 us -> 130 us (0.89)
  waiting for transfers between devices: 65.1 us -> 55.1 us
  starting transfers between devices: 43.4 us -> 36.8 us
    ppermute x22, waiting for transfers between devices: 34.1 us -> 20.1 us  [exchange(): return lax.ppermute(value, 'row', pairs)]
    ppermute x22, starting transfers between devices: 33.9 us -> 26.6 us  [exchange(): return lax.ppermute(value, 'row', pairs)]
    ppermute x12, waiting for transfers between devices: 31 us -> 35 us  [turn(): return lax.ppermute(value, AXES, pairs)]
    select_n x20, other arithmetic: 11 us -> 13 us  [choose(): return jnp.where(taken[:, None, None], partner, mine)]
  transfers between devices with their start and end apart: 34 -> 34, of which waited for: 15 -> 15; matrix products, arithmetic and copies ran while one was open for 8% -> 12% of each run, Pallas kernels for 12% -> 14%
where the time goes in v3:
time: 130 us
  waiting for transfers between devices  55.1 us (42%)
  starting transfers between devices  36.8 us (28%)
  Pallas kernels  18.1 us (14%)
  other arithmetic  14.9 us (11%)
  local copies, waits for them, and re-layouts  4.49 us (3%)
    ppermute x12, waiting for transfers between devices, turn(): return lax.ppermute(value, AXES, pairs)  35 us
    ppermute x22, starting transfers between devices, exchange(): return lax.ppermute(value, 'row', pairs)  26.6 us
    ppermute x22, waiting for transfers between devices, exchange(): return lax.ppermute(value, 'row', pairs)  20.1 us
    pallas_call x4, Pallas kernels, product(): pl.pallas_call(functools.partial(product_kernel, first), grid_spec=pltpu....  16.2 us
    select_n x20, other arithmetic, choose(): return jnp.where(taken[:, None, None], partner, mine)  13 us
    ppermute x12, starting transfers between devices, turn(): return lax.ppermute(value, AXES, pairs)  10.2 us
  transfers between devices with their start and end apart: 34, of which 15 were waited for; matrix products, arithmetic and copies ran while one was open for 12% of the time, Pallas kernels for 14%

profile of v3, /device:TPU:0, one launch (start us, length us, event | category | flops | bytes accessed | tf_op | source)
XLA Modules:
  0.0 129.6 jit_solution(5455416243596869295)
XLA Ops:
  0.0 1.8 %shard_map.73 = bf16[1,144,256]{2,1,0:T(8,128)(2,1)} custom-call(s32[1,12]{1,0:T(1,128)} %screen_ref.1, bf16[128,1536]{1,0:T(8,128)(2,1)} %amplitudes_ref.1), custom_call_target="tpu_custom_call" | custom-call | flops 1 | bytes 1 | tf_op jit(solution)/shard_map/pallas_call | solution.py:59
  1.8 1.6 %collective-permute-start = (bf16[1,144,256]{2,1,0:T(8,128)(2,1)}, bf16[1,144,256]{2,1,0:T(8,128)(2,1)S(1)}, u32[]{:S(2)}, u32[]{:S(2)}) collective-permute-start(bf16[1,144,256]{2,1,0:T(8,128)(2,1)} %shard_map.73), channel_id=1, source_target_pairs={{0,8},{4,28},{8,0},{12,20},{16,24},{20,12},{24,16},{28,4},{32,40},... | collective-permute-start | bytes 221192 | tf_op jit(solution)/shard_map/ppermute | solution.py:25
  5.7 1.3 %slice_select_fusion.3 = bf16[2,128,1024]{2,1,0:T(8,128)(2,1)S(1)} fusion(bf16[8,128,1024]{2,1,0:T(8,128)(2,1)} %bitcast.66, bf16[8,128,1024]{2,1,0:T(8,128)(2,1)} %collective-permute-done.1, pred[2]{0:T(512)(128)(4,1)S(1)} %get-tuple-element.279), kind=kLoop, calls=%fused_computation.12 | loop fusion | flops 262144 | bytes 1572866 | tf_op jit(solution)/shard_map/jit(_where)/select_n | solution.py:40
  7.0 1.2 slice_select_fusion.2
  8.3 2.2 %collective-permute-start.2 = (bf16[2,144,256]{2,1,0:T(8,128)(2,1)S(1)}, bf16[2,144,256]{2,1,0:T(8,128)(2,1)S(1)}, u32[]{:S(2)}, u32[]{:S(2)}) collective-permute-start(bf16[2,144,256]{2,1,0:T(8,128)(2,1)S(1)} %pad_maximum_fusion.4), channel_id=1, source_target_pairs={{0,24},{4,12},{8,16},{12,4},{16,8},{20,28},{24,0},{28,20},{32,56},... | collective-permute-start | bytes 442376 | tf_op jit(solution)/shard_map/ppermute | solution.py:25
  10.5 1.6 %collective-permute-start.6 = (bf16[2,128,1024]{2,1,0:T(8,128)(2,1)S(1)}, bf16[2,128,1024]{2,1,0:T(8,128)(2,1)S(1)}, u32[]{:S(2)}, u32[]{:S(2)}) collective-permute-start(bf16[2,128,1024]{2,1,0:T(8,128)(2,1)S(1)} %slice_select_fusion.2), channel_id=1, source_target_pairs={{0,32},{4,100},{8,40},{12,108},{16,48},{20,116},{24,56},{28,124},{... | collective-permute-start | bytes 1572872 | tf_op jit(solution)/shard_map/ppermute | solution.py:25
  12.0 1.2 slice_select_fusion.1
  13.9 1.2 slice_select_fusion
  15.1 2.0 %collective-permute-start.4 = (bf16[256,1024]{1,0:T(8,128)(2,1)S(1)}, bf16[256,1024]{1,0:T(8,128)(2,1)S(1)}, u32[]{:S(2)}, u32[]{:S(2)}) collective-permute-start(bf16[256,1024]{1,0:T(8,128)(2,1)S(1)} %bitcast.55), channel_id=1, source_target_pairs={{0,1},{1,2},{2,3},{3,0},{4,7},{5,4},{6,5},{7,6},{8,9},{9,10},{10,1... | collective-permute-start | bytes 1572872 | tf_op jit(solution)/shard_map/ppermute | solution.py:35
  17.1 1.4 %collective-permute-start.11 = (bf16[2,128,1024]{2,1,0:T(8,128)(2,1)S(1)}, bf16[2,128,1024]{2,1,0:T(8,128)(2,1)S(1)}, u32[]{:S(2)}, u32[]{:S(2)}) collective-permute-start(bf16[2,128,1024]{2,1,0:T(8,128)(2,1)S(1)} %slice_select_fusion), channel_id=1, source_target_pairs={{0,8},{4,28},{8,0},{12,20},{16,24},{20,12},{24,16},{28,4},{32,40},... | collective-permute-start | bytes 1572872 | tf_op jit(solution)/shard_map/ppermute | solution.py:25
  19.8 2.7 %collective-permute-done.5 = bf16[2,128,1024]{2,1,0:T(8,128)(2,1)S(1)} collective-permute-done((bf16[2,128,1024]{2,1,0:T(8,128)(2,1)S(1)}, bf16[2,128,1024]{2,1,0:T(8,128)(2,1)S(1)}, u32[]{:S(2)}, u32[]{:S(2)}) %collective-permute-start.5) | collective-permute-done | bytes 524320 | tf_op jit(solution)/shard_map/ppermute | solution.py:25
  22.5 2.2 %collective-permute-start.10 = (bf16[2,128,1024]{2,1,0:T(8,128)(2,1)S(1)}, bf16[2,128,1024]{2,1,0:T(8,128)(2,1)S(1)}, u32[]{:S(2)}, u32[]{:S(2)}) collective-permute-start(bf16[2,128,1024]{2,1,0:T(8,128)(2,1)S(1)} %broadcast_select_fusion.14), channel_id=1, source_target_pairs={{0,96},{4,36},{8,104},{12,44},{16,112},{20,52},{24,120},{28,60},{3... | collective-permute-start | bytes 1572872 | tf_op jit(solution)/shard_map/ppermute | solution.py:25
  24.8 1.6 %collective-permute-done.4.refs_1_ = bf16[256,1024]{1,0:T(8,128)(2,1)S(1)} collective-permute-done((bf16[256,1024]{1,0:T(8,128)(2,1)S(1)}, bf16[256,1024]{1,0:T(8,128)(2,1)S(1)}, u32[]{:S(2)}, u32[]{:S(2)}) %collective-permute-start.4) | collective-permute-done | bytes 524320 | tf_op jit(solution)/shard_map/ppermute | solution.py:35
  26.4 2.3 %collective-permute-start.7 = (bf16[8,144,256]{2,1,0:T(8,128)(2,1)S(1)}, bf16[8,144,256]{2,1,0:T(8,128)(2,1)S(1)}, u32[]{:S(2)}, u32[]{:S(2)}) collective-permute-start(bf16[8,144,256]{2,1,0:T(8,128)(2,1)S(1)} %pad_maximum_fusion.2), channel_id=1, source_target_pairs={{0,96},{4,36},{8,104},{12,44},{16,112},{20,52},{24,120},{28,60},{3... | collective-permute-start | bytes 1769480 | tf_op jit(solution)/shard_map/ppermute | solution.py:25
  28.7 2.4 %collective-permute-start.8 = (bf16[256,1024]{1,0:T(8,128)(2,1)S(1)}, bf16[256,1024]{1,0:T(8,128)(2,1)}, u32[]{:S(2)}, u32[]{:S(2)}) collective-permute-start(bf16[256,1024]{1,0:T(8,128)(2,1)S(1)} %collective-permute-done.4.refs_1_), channel_id=1, source_target_pairs={{0,1},{1,2},{2,3},{3,0},{4,7},{5,4},{6,5},{7,6},{8,9},{9,10},{10,1... | collective-permute-start | bytes 1572872 | tf_op jit(solution)/shard_map/ppermute | solution.py:35
  31.5 0.9 broadcast_select_fusion.11
  32.4 1.8 %collective-permute-done.10 = bf16[2,128,1024]{2,1,0:T(8,128)(2,1)S(1)} collective-permute-done((bf16[2,128,1024]{2,1,0:T(8,128)(2,1)S(1)}, bf16[2,128,1024]{2,1,0:T(8,128)(2,1)S(1)}, u32[]{:S(2)}, u32[]{:S(2)}) %collective-permute-start.10) | collective-permute-done | bytes 524320 | tf_op jit(solution)/shard_map/ppermute | solution.py:25
  34.3 7.2 %collective-permute-done.9 = bf16[2,128,1024]{2,1,0:T(8,128)(2,1)S(1)} collective-permute-done((bf16[2,128,1024]{2,1,0:T(8,128)(2,1)S(1)}, bf16[2,128,1024]{2,1,0:T(8,128)(2,1)S(1)}, u32[]{:S(2)}, u32[]{:S(2)}) %collective-permute-start.9) | collective-permute-done | bytes 524320 | tf_op jit(solution)/shard_map/ppermute | solution.py:25
  42.0 1.2 collective-permute-start.14
  43.1 1.3 collective-permute-start.17
  44.5 6.7 %collective-permute-done.13 = bf16[2,128,1024]{2,1,0:T(8,128)(2,1)S(1)} collective-permute-done((bf16[2,128,1024]{2,1,0:T(8,128)(2,1)S(1)}, bf16[2,128,1024]{2,1,0:T(8,128)(2,1)S(1)}, u32[]{:S(2)}, u32[]{:S(2)}) %collective-permute-start.13) | collective-permute-done | bytes 524320 | tf_op jit(solution)/shard_map/ppermute | solution.py:25
  51.1 0.9 broadcast_select_fusion.10
  52.7 2.1 %broadcast_select_fusion.7 = bf16[2,128,1024]{2,1,0:T(8,128)(2,1)} fusion(bf16[2,128,1024]{2,1,0:T(8,128)(2,1)} %collective-permute-done.14, bf16[2,128,1024]{2,1,0:T(8,128)(2,1)} %broadcast_select_fusion.11, pred[2]{0:T(512)(128)(4,1)S(1)} %get-tuple-element.268), kind=kLoop, calls=%fused_computation.14 | loop fusion | flops 262144 | bytes 1572866 | tf_op jit(solution)/shard_map/jit(_where)/select_n | solution.py:40
  56.1 1.0 copy-done.1
  57.1 3.5 %shard_map.74 = bf16[256,1536]{1,0:T(8,128)(2,1)S(1)} custom-call(s32[1,32]{1,0:T(1,128)S(1)} %constant_dynamic-slice_fusion.at_ref, s32[64]{0:T(128)S(1)} %reshape.184.place_ref, s32[4]{0:T(128)S(1)} %subtract_and_fusion.base_ref, bf16[256,1024]{1,0:T(8,128)(2,1)S(1)} %bitcast.56, bf16[256,1024]{1,0:T(8,128)(2,1)S(1)} %copy-done.1, ...), custom_call_target="tpu_custom_call" | custom-call | flops 1 | bytes 1 | tf_op jit(solution)/shard_map/pallas_call | solution.py:118
  61.6 1.2 collective-permute-done.16
  62.7 1.3 %collective-permute-start.22 = (bf16[256,1024]{1,0:T(8,128)(2,1)}, bf16[256,1024]{1,0:T(8,128)(2,1)S(1)}, u32[]{:S(2)}, u32[]{:S(2)}) collective-permute-start(bf16[256,1024]{1,0:T(8,128)(2,1)} %collective-permute-done.18.refs_1_), channel_id=1, source_target_pairs={{0,1},{1,2},{2,3},{3,0},{4,7},{5,4},{6,5},{7,6},{8,9},{9,10},{10,1... | collective-permute-start | bytes 1572872 | tf_op jit(solution)/shard_map/ppermute | solution.py:35
  64.1 1.3 %broadcast_select_fusion.6 = bf16[2,128,1024]{2,1,0:T(8,128)(2,1)S(1)} fusion(bf16[2,128,1024]{2,1,0:T(8,128)(2,1)} %collective-permute-done.16, bf16[2,128,1024]{2,1,0:T(8,128)(2,1)} %broadcast_select_fusion.10, pred[2]{0:T(512)(128)(4,1)S(1)} %get-tuple-element.267), kind=kLoop, calls=%fused_computation.13 | loop fusion | flops 262144 | bytes 1572866 | tf_op jit(solution)/shard_map/jit(_where)/select_n | solution.py:40
  66.1 1.3 %broadcast_select_fusion.8 = bf16[2,128,1024]{2,1,0:T(8,128)(2,1)S(1)} fusion(bf16[2,128,1024]{2,1,0:T(8,128)(2,1)} %collective-permute-done.15, bf16[2,128,1024]{2,1,0:T(8,128)(2,1)} %broadcast_select_fusion.7, pred[2]{0:T(512)(128)(4,1)S(1)} %get-tuple-element.269), kind=kLoop, calls=%fused_computation.15 | loop fusion | flops 262144 | bytes 1572866 | tf_op jit(solution)/shard_map/jit(_where)/select_n | solution.py:40
  67.4 4.2 %collective-permute-start.19 = (bf16[2,128,1024]{2,1,0:T(8,128)(2,1)S(1)}, bf16[2,128,1024]{2,1,0:T(8,128)(2,1)S(1)}, u32[]{:S(2)}, u32[]{:S(2)}) collective-permute-start(bf16[2,128,1024]{2,1,0:T(8,128)(2,1)S(1)} %broadcast_select_fusion.8), channel_id=1, source_target_pairs={{0,24},{4,12},{8,16},{12,4},{16,8},{20,28},{24,0},{28,20},{32,56},... | collective-permute-start | bytes 1572872 | tf_op jit(solution)/shard_map/ppermute | solution.py:25
  71.6 1.8 %collective-permute-done.22.refs_2_ = bf16[256,1024]{1,0:T(8,128)(2,1)S(1)} collective-permute-done((bf16[256,1024]{1,0:T(8,128)(2,1)}, bf16[256,1024]{1,0:T(8,128)(2,1)S(1)}, u32[]{:S(2)}, u32[]{:S(2)}) %collective-permute-start.22) | collective-permute-done | bytes 524320 | tf_op jit(solution)/shard_map/ppermute | solution.py:35
  73.5 2.2 %collective-permute-start.24 = (bf16[2,128,1536]{2,1,0:T(8,128)(2,1)S(1)}, bf16[2,128,1536]{2,1,0:T(8,128)(2,1)S(1)}, u32[]{:S(2)}, u32[]{:S(2)}) collective-permute-start(bf16[2,128,1536]{2,1,0:T(8,128)(2,1)S(1)} %broadcast_select_fusion.5), channel_id=1, source_target_pairs={{0,96},{4,36},{8,104},{12,44},{16,112},{20,52},{24,120},{28,60},{3... | collective-permute-start | bytes 2359304 | tf_op jit(solution)/shard_map/ppermute | solution.py:25
  75.7 1.3 %collective-permute-start.25 = (bf16[256,1024]{1,0:T(8,128)(2,1)S(1)}, bf16[256,1024]{1,0:T(8,128)(2,1)S(1)}, u32[]{:S(2)}, u32[]{:S(2)}) collective-permute-start(bf16[256,1024]{1,0:T(8,128)(2,1)S(1)} %collective-permute-done.22.refs_2_), channel_id=1, source_target_pairs={{0,1},{1,2},{2,3},{3,0},{4,7},{5,4},{6,5},{7,6},{8,9},{9,10},{10,1... | collective-permute-start | bytes 1572872 | tf_op jit(solution)/shard_map/ppermute | solution.py:35
  77.0 1.9 %collective-permute-done.20.refs_1_ = bf16[256,1024]{1,0:T(8,128)(2,1)S(1)} collective-permute-done((bf16[256,1024]{1,0:T(8,128)(2,1)S(1)}, bf16[256,1024]{1,0:T(8,128)(2,1)S(1)}, u32[]{:S(2)}, u32[]{:S(2)}) %collective-permute-start.20) | collective-permute-done | bytes 524320 | tf_op jit(solution)/shard_map/ppermute | solution.py:35
  79.1 7.0 %collective-permute-done.25.refs_3_ = bf16[256,1024]{1,0:T(8,128)(2,1)S(1)} collective-permute-done((bf16[256,1024]{1,0:T(8,128)(2,1)S(1)}, bf16[256,1024]{1,0:T(8,128)(2,1)S(1)}, u32[]{:S(2)}, u32[]{:S(2)}) %collective-permute-start.25) | collective-permute-done | bytes 524320 | tf_op jit(solution)/shard_map/ppermute | solution.py:35
  86.1 3.8 %shard_map.75 = bf16[256,1536]{1,0:T(8,128)(2,1)S(1)} custom-call(s32[1,32]{1,0:T(1,128)S(1)} %constant_dynamic-slice_fusion.at_ref, s32[64]{0:T(128)S(1)} %reshape.184.place_ref, s32[4]{0:T(128)S(1)} %subtract_and_fusion.base_ref, bf16[256,1024]{1,0:T(8,128)(2,1)S(1)} %bitcast.58, bf16[256,1024]{1,0:T(8,128)(2,1)} %collective-permute-done.18.refs_1_, ...), custom_call_target="tpu_custom_call" | custom-call | flops 1 | bytes 1 | tf_op jit(solution)/shard_map/pallas_call | solution.py:118
  90.2 1.0 collective-permute-start.28
  91.4 9.1 %collective-permute-done.23.refs_1_ = bf16[256,1024]{1,0:T(8,128)(2,1)S(1)} collective-permute-done((bf16[256,1024]{1,0:T(8,128)(2,1)S(1)}, bf16[256,1024]{1,0:T(8,128)(2,1)S(1)}, u32[]{:S(2)}, u32[]{:S(2)}) %collective-permute-start.23) | collective-permute-done | bytes 524320 | tf_op jit(solution)/shard_map/ppermute | solution.py:35
  100.5 5.6 %collective-permute-done.28.refs_2_ = bf16[256,1024]{1,0:T(8,128)(2,1)S(1)} collective-permute-done((bf16[256,1024]{1,0:T(8,128)(2,1)S(1)}, bf16[256,1024]{1,0:T(8,128)(2,1)S(1)}, u32[]{:S(2)}, u32[]{:S(2)}) %collective-permute-start.28) | collective-permute-done | bytes 524320 | tf_op jit(solution)/shard_map/ppermute | solution.py:35
  106.3 5.5 %collective-permute-done.26.refs_2_ = bf16[256,1024]{1,0:T(8,128)(2,1)S(1)} collective-permute-done((bf16[256,1024]{1,0:T(8,128)(2,1)S(1)}, bf16[256,1024]{1,0:T(8,128)(2,1)S(1)}, u32[]{:S(2)}, u32[]{:S(2)}) %collective-permute-start.26) | collective-permute-done | bytes 524320 | tf_op jit(solution)/shard_map/ppermute | solution.py:35
  111.7 1.5 %collective-permute-start.33 = (bf16[2,128,1536]{2,1,0:T(8,128)(2,1)S(1)}, bf16[2,128,1536]{2,1,0:T(8,128)(2,1)S(1)}, u32[]{:S(2)}, u32[]{:S(2)}) collective-permute-start(bf16[2,128,1536]{2,1,0:T(8,128)(2,1)S(1)} %broadcast_select_fusion.3), channel_id=1, source_target_pairs={{0,96},{4,36},{8,104},{12,44},{16,112},{20,52},{24,120},{28,60},{3... | collective-permute-start | bytes 2359304 | tf_op jit(solution)/shard_map/ppermute | solution.py:25
  113.4 2.6 %collective-permute-start.32 = (bf16[2,128,1536]{2,1,0:T(8,128)(2,1)S(1)}, bf16[2,128,1536]{2,1,0:T(8,128)(2,1)S(1)}, u32[]{:S(2)}, u32[]{:S(2)}) collective-permute-start(bf16[2,128,1536]{2,1,0:T(8,128)(2,1)S(1)} %broadcast_select_fusion.2), channel_id=1, source_target_pairs={{0,24},{4,12},{8,16},{12,4},{16,8},{20,28},{24,0},{28,20},{32,56},... | collective-permute-start | bytes 2359304 | tf_op jit(solution)/shard_map/ppermute | solution.py:25
  116.0 1.3 %collective-permute-done.30.refs_3_ = bf16[256,1024]{1,0:T(8,128)(2,1)S(1)} collective-permute-done((bf16[256,1024]{1,0:T(8,128)(2,1)S(1)}, bf16[256,1024]{1,0:T(8,128)(2,1)S(1)}, u32[]{:S(2)}, u32[]{:S(2)}) %collective-permute-start.30) | collective-permute-done | bytes 524320 | tf_op jit(solution)/shard_map/ppermute | solution.py:35
  117.3 4.4 %shard_map.76.refs_5_ = bf16[1024,1536]{1,0:T(8,128)(2,1)} custom-call(s32[1,32]{1,0:T(1,128)S(1)} %constant_dynamic-slice_fusion.at_ref, s32[64]{0:T(128)S(1)} %reshape.184.place_ref, s32[4]{0:T(128)S(1)} %subtract_and_fusion.base_ref, bf16[256,1024]{1,0:T(8,128)(2,1)S(1)} %bitcast.60, bf16[256,1024]{1,0:T(8,128)(2,1)S(1)} %collective-permute-done.20.refs_1_, ...), custom_call_target="tpu_custom_call" | custom-call | flops 1 | bytes 1 | tf_op jit(solution)/shard_map/pallas_call | solution.py:118
  121.8 1.2 collective-permute-done.29.refs_3_
  123.0 4.4 %shard_map.77 = bf16[1024,1536]{1,0:T(8,128)(2,1)} custom-call(s32[1,32]{1,0:T(1,128)S(1)} %constant_dynamic-slice_fusion.at_ref, s32[64]{0:T(128)S(1)} %reshape.184.place_ref, s32[4]{0:T(128)S(1)} %subtract_and_fusion.base_ref, bf16[256,1024]{1,0:T(8,128)(2,1)S(1)} %bitcast.62, ...), custom_call_target="tpu_custom_call", output_to_operand_aliasing={{}: (8, {})} | custom-call | flops 1 | bytes 1 | tf_op jit(solution)/shard_map/pallas_call | solution.py:118
  127.7 0.9 constant_dynamic-update-slice_fusion.1
  128.7 0.9 constant_dynamic-update-slice_fusion
  (71 shorter events, 10.1 us)
Async XLA Ops:
  0.0 7.0 %copy-start.2 = (bf16[1024,1024]{1,0:T(8,128)(2,1)S(1)}, bf16[1024,1024]{1,0:T(8,128)(2,1)}, u32[]{:S(2)}) copy-start(bf16[1024,1024]{1,0:T(8,128)(2,1)} %param.7) | copy-start | bytes 6291460
  0.0 5.7 %collective-permute-start.1 = (bf16[8,128,1024]{2,1,0:T(8,128)(2,1)}, bf16[8,128,1024]{2,1,0:T(8,128)(2,1)}, u32[]{:S(2)}, u32[]{:S(2)}) collective-permute-start(bf16[8,128,1024]{2,1,0:T(8,128)(2,1)} %bitcast.65), channel_id=1, source_target_pairs={{0,4},{4,0},{8,12},{12,8},{16,20},{20,16},{24,28},{28,24},{32,36},... | collective-permute-start | bytes 6291464 | tf_op jit(solution)/shard_map/ppermute | solution.py:25
  1.8 6.4 %copy-start.3 = (bf16[1,144,256]{2,1,0:T(8,128)(2,1)S(1)}, bf16[1,144,256]{2,1,0:T(8,128)(2,1)}, u32[]{:S(2)}) copy-start(bf16[1,144,256]{2,1,0:T(8,128)(2,1)} %shard_map.73) | copy-start | bytes 221188
  1.8 6.4 %collective-permute-start = (bf16[1,144,256]{2,1,0:T(8,128)(2,1)}, bf16[1,144,256]{2,1,0:T(8,128)(2,1)S(1)}, u32[]{:S(2)}, u32[]{:S(2)}) collective-permute-start(bf16[1,144,256]{2,1,0:T(8,128)(2,1)} %shard_map.73), channel_id=1, source_target_pairs={{0,8},{4,28},{8,0},{12,20},{16,24},{20,12},{24,16},{28,4},{32,40},... | collective-permute-start | bytes 221192 | tf_op jit(solution)/shard_map/ppermute | solution.py:25
  8.3 10.2 %collective-permute-start.2 = (bf16[2,144,256]{2,1,0:T(8,128)(2,1)S(1)}, bf16[2,144,256]{2,1,0:T(8,128)(2,1)S(1)}, u32[]{:S(2)}, u32[]{:S(2)}) collective-permute-start(bf16[2,144,256]{2,1,0:T(8,128)(2,1)S(1)} %pad_maximum_fusion.4), channel_id=1, source_target_pairs={{0,24},{4,12},{8,16},{12,4},{16,8},{20,28},{24,0},{28,20},{32,56},... | collective-permute-start | bytes 442376 | tf_op jit(solution)/shard_map/ppermute | solution.py:25
  10.5 9.2 %collective-permute-start.6 = (bf16[2,128,1024]{2,1,0:T(8,128)(2,1)S(1)}, bf16[2,128,1024]{2,1,0:T(8,128)(2,1)S(1)}, u32[]{:S(2)}, u32[]{:S(2)}) collective-permute-start(bf16[2,128,1024]{2,1,0:T(8,128)(2,1)S(1)} %slice_select_fusion.2), channel_id=1, source_target_pairs={{0,32},{4,100},{8,40},{12,108},{16,48},{20,116},{24,56},{28,124},{... | collective-permute-start | bytes 1572872 | tf_op jit(solution)/shard_map/ppermute | solution.py:25
  13.2 9.3 %collective-permute-start.5 = (bf16[2,128,1024]{2,1,0:T(8,128)(2,1)S(1)}, bf16[2,128,1024]{2,1,0:T(8,128)(2,1)S(1)}, u32[]{:S(2)}, u32[]{:S(2)}) collective-permute-start(bf16[2,128,1024]{2,1,0:T(8,128)(2,1)S(1)} %slice_select_fusion.1), channel_id=1, source_target_pairs={{0,8},{4,28},{8,0},{12,20},{16,24},{20,12},{24,16},{28,4},{32,40},... | collective-permute-start | bytes 1572872 | tf_op jit(solution)/shard_map/ppermute | solution.py:25
  15.1 11.3 %collective-permute-start.4 = (bf16[256,1024]{1,0:T(8,128)(2,1)S(1)}, bf16[256,1024]{1,0:T(8,128)(2,1)S(1)}, u32[]{:S(2)}, u32[]{:S(2)}) collective-permute-start(bf16[256,1024]{1,0:T(8,128)(2,1)S(1)} %bitcast.55), channel_id=1, source_target_pairs={{0,1},{1,2},{2,3},{3,0},{4,7},{5,4},{6,5},{7,6},{8,9},{9,10},{10,1... | collective-permute-start | bytes 1572872 | tf_op jit(solution)/shard_map/ppermute | solution.py:35
  17.1 14.4 %collective-permute-start.11 = (bf16[2,128,1024]{2,1,0:T(8,128)(2,1)S(1)}, bf16[2,128,1024]{2,1,0:T(8,128)(2,1)S(1)}, u32[]{:S(2)}, u32[]{:S(2)}) collective-permute-start(bf16[2,128,1024]{2,1,0:T(8,128)(2,1)S(1)} %slice_select_fusion), channel_id=1, source_target_pairs={{0,8},{4,28},{8,0},{12,20},{16,24},{20,12},{24,16},{28,4},{32,40},... | collective-permute-start | bytes 1572872 | tf_op jit(solution)/shard_map/ppermute | solution.py:25
  18.6 7.8 %collective-permute-start.3 = (bf16[4,144,256]{2,1,0:T(8,128)(2,1)S(1)}, bf16[4,144,256]{2,1,0:T(8,128)(2,1)S(1)}, u32[]{:S(2)}, u32[]{:S(2)}) collective-permute-start(bf16[4,144,256]{2,1,0:T(8,128)(2,1)S(1)} %pad_maximum_fusion.3), channel_id=1, source_target_pairs={{0,32},{4,100},{8,40},{12,108},{16,48},{20,116},{24,56},{28,124},{... | collective-permute-start | bytes 884744 | tf_op jit(solution)/shard_map/ppermute | solution.py:25
  22.5 11.7 %collective-permute-start.10 = (bf16[2,128,1024]{2,1,0:T(8,128)(2,1)S(1)}, bf16[2,128,1024]{2,1,0:T(8,128)(2,1)S(1)}, u32[]{:S(2)}, u32[]{:S(2)}) collective-permute-start(bf16[2,128,1024]{2,1,0:T(8,128)(2,1)S(1)} %broadcast_select_fusion.14), channel_id=1, source_target_pairs={{0,96},{4,36},{8,104},{12,44},{16,112},{20,52},{24,120},{28,60},{3... | collective-permute-start | bytes 1572872 | tf_op jit(solution)/shard_map/ppermute | solution.py:25
  26.4 8.0 %copy-start = (bf16[256,1024]{1,0:T(8,128)(2,1)}, bf16[256,1024]{1,0:T(8,128)(2,1)S(1)}, u32[]{:S(2)}) copy-start(bf16[256,1024]{1,0:T(8,128)(2,1)S(1)} %collective-permute-done.4.refs_1_) | copy-start | bytes 1572868
  26.4 15.2 %collective-permute-start.7 = (bf16[8,144,256]{2,1,0:T(8,128)(2,1)S(1)}, bf16[8,144,256]{2,1,0:T(8,128)(2,1)S(1)}, u32[]{:S(2)}, u32[]{:S(2)}) collective-permute-start(bf16[8,144,256]{2,1,0:T(8,128)(2,1)S(1)} %pad_maximum_fusion.2), channel_id=1, source_target_pairs={{0,96},{4,36},{8,104},{12,44},{16,112},{20,52},{24,120},{28,60},{3... | collective-permute-start | bytes 1769480 | tf_op jit(solution)/shard_map/ppermute | solution.py:25
  28.7 12.9 %collective-permute-start.8 = (bf16[256,1024]{1,0:T(8,128)(2,1)S(1)}, bf16[256,1024]{1,0:T(8,128)(2,1)}, u32[]{:S(2)}, u32[]{:S(2)}) collective-permute-start(bf16[256,1024]{1,0:T(8,128)(2,1)S(1)} %collective-permute-done.4.refs_1_), channel_id=1, source_target_pairs={{0,1},{1,2},{2,3},{3,0},{4,7},{5,4},{6,5},{7,6},{8,9},{9,10},{10,1... | collective-permute-start | bytes 1572872 | tf_op jit(solution)/shard_map/ppermute | solution.py:35
  31.1 10.4 %collective-permute-start.9 = (bf16[2,128,1024]{2,1,0:T(8,128)(2,1)S(1)}, bf16[2,128,1024]{2,1,0:T(8,128)(2,1)S(1)}, u32[]{:S(2)}, u32[]{:S(2)}) collective-permute-start(bf16[2,128,1024]{2,1,0:T(8,128)(2,1)S(1)} %broadcast_select_fusion.15), channel_id=1, source_target_pairs={{0,24},{4,12},{8,16},{12,4},{16,8},{20,28},{24,0},{28,20},{32,56},... | collective-permute-start | bytes 1572872 | tf_op jit(solution)/shard_map/ppermute | solution.py:25
  41.8 10.6 %collective-permute-start.12 = (bf16[16,144,256]{2,1,0:T(8,128)(2,1)S(1)}, bf16[16,144,256]{2,1,0:T(8,128)(2,1)S(1)}, u32[]{:S(2)}, u32[]{:S(2)}) collective-permute-start(bf16[16,144,256]{2,1,0:T(8,128)(2,1)S(1)} %pad_maximum_fusion.1), channel_id=1, source_target_pairs={{0,4},{4,0},{8,12},{12,8},{16,20},{20,16},{24,28},{28,24},{32,36},... | collective-permute-start | bytes 3538952 | tf_op jit(solution)/shard_map/ppermute | solution.py:25
  41.9 9.3 %collective-permute-start.13 = (bf16[2,128,1024]{2,1,0:T(8,128)(2,1)S(1)}, bf16[2,128,1024]{2,1,0:T(8,128)(2,1)S(1)}, u32[]{:S(2)}, u32[]{:S(2)}) collective-permute-start(bf16[2,128,1024]{2,1,0:T(8,128)(2,1)S(1)} %broadcast_select_fusion.12), channel_id=1, source_target_pairs={{0,8},{4,28},{8,0},{12,20},{16,24},{20,12},{24,16},{28,4},{32,40},... | collective-permute-start | bytes 1572872 | tf_op jit(solution)/shard_map/ppermute | solution.py:25
  42.0 10.8 %collective-permute-start.14 = (bf16[2,128,1024]{2,1,0:T(8,128)(2,1)}, bf16[2,128,1024]{2,1,0:T(8,128)(2,1)}, u32[]{:S(2)}, u32[]{:S(2)}) collective-permute-start(bf16[2,128,1024]{2,1,0:T(8,128)(2,1)} %broadcast_select_fusion.11), channel_id=1, source_target_pairs={{0,32},{4,100},{8,40},{12,108},{16,48},{20,116},{24,56},{28,124},{... | collective-permute-start | bytes 1572872 | tf_op jit(solution)/shard_map/ppermute | solution.py:25
  43.1 12.9 %collective-permute-start.17 = (bf16[256,1024]{1,0:T(8,128)(2,1)}, bf16[256,1024]{1,0:T(8,128)(2,1)}, u32[]{:S(2)}, u32[]{:S(2)}) collective-permute-start(bf16[256,1024]{1,0:T(8,128)(2,1)} %collective-permute-done.8.refs_2_), channel_id=1, source_target_pairs={{0,1},{1,2},{2,3},{3,0},{4,7},{5,4},{6,5},{7,6},{8,9},{9,10},{10,1... | collective-permute-start | bytes 1572872 | tf_op jit(solution)/shard_map/ppermute | solution.py:35
  44.4 16.3 %collective-permute-start.18 = (bf16[256,1024]{1,0:T(8,128)(2,1)S(1)}, bf16[256,1024]{1,0:T(8,128)(2,1)}, u32[]{:S(2)}, u32[]{:S(2)}) collective-permute-start(bf16[256,1024]{1,0:T(8,128)(2,1)S(1)} %bitcast.57), channel_id=1, source_target_pairs={{0,1},{1,2},{2,3},{3,0},{4,7},{5,4},{6,5},{7,6},{8,9},{9,10},{10,1... | collective-permute-start | bytes 1572872 | tf_op jit(solution)/shard_map/ppermute | solution.py:35
  52.0 10.7 %collective-permute-start.16 = (bf16[2,128,1024]{2,1,0:T(8,128)(2,1)}, bf16[2,128,1024]{2,1,0:T(8,128)(2,1)}, u32[]{:S(2)}, u32[]{:S(2)}) collective-permute-start(bf16[2,128,1024]{2,1,0:T(8,128)(2,1)} %broadcast_select_fusion.10), channel_id=1, source_target_pairs={{0,24},{4,12},{8,16},{12,4},{16,8},{20,28},{24,0},{28,20},{32,56},... | collective-permute-start | bytes 1572872 | tf_op jit(solution)/shard_map/ppermute | solution.py:25
  54.8 11.2 %collective-permute-start.15 = (bf16[2,128,1024]{2,1,0:T(8,128)(2,1)}, bf16[2,128,1024]{2,1,0:T(8,128)(2,1)}, u32[]{:S(2)}, u32[]{:S(2)}) collective-permute-start(bf16[2,128,1024]{2,1,0:T(8,128)(2,1)} %broadcast_select_fusion.7), channel_id=1, source_target_pairs={{0,96},{4,36},{8,104},{12,44},{16,112},{20,52},{24,120},{28,60},{3... | collective-permute-start | bytes 1572872 | tf_op jit(solution)/shard_map/ppermute | solution.py:25
  56.1 1.0 copy-start.1
  60.7 12.7 %collective-permute-start.21 = (bf16[2,128,1536]{2,1,0:T(8,128)(2,1)S(1)}, bf16[2,128,1536]{2,1,0:T(8,128)(2,1)S(1)}, u32[]{:S(2)}, u32[]{:S(2)}) collective-permute-start(bf16[2,128,1536]{2,1,0:T(8,128)(2,1)S(1)} %bitcast.53), channel_id=1, source_target_pairs={{0,32},{4,100},{8,40},{12,108},{16,48},{20,116},{24,56},{28,124},{... | collective-permute-start | bytes 2359304 | tf_op jit(solution)/shard_map/ppermute | solution.py:25
  62.7 10.6 %collective-permute-start.22 = (bf16[256,1024]{1,0:T(8,128)(2,1)}, bf16[256,1024]{1,0:T(8,128)(2,1)S(1)}, u32[]{:S(2)}, u32[]{:S(2)}) collective-permute-start(bf16[256,1024]{1,0:T(8,128)(2,1)} %collective-permute-done.18.refs_1_), channel_id=1, source_target_pairs={{0,1},{1,2},{2,3},{3,0},{4,7},{5,4},{6,5},{7,6},{8,9},{9,10},{10,1... | collective-permute-start | bytes 1572872 | tf_op jit(solution)/shard_map/ppermute | solution.py:35
  65.4 13.6 %collective-permute-start.20 = (bf16[256,1024]{1,0:T(8,128)(2,1)S(1)}, bf16[256,1024]{1,0:T(8,128)(2,1)S(1)}, u32[]{:S(2)}, u32[]{:S(2)}) collective-permute-start(bf16[256,1024]{1,0:T(8,128)(2,1)S(1)} %bitcast.59), channel_id=1, source_target_pairs={{0,1},{1,2},{2,3},{3,0},{4,7},{5,4},{6,5},{7,6},{8,9},{9,10},{10,1... | collective-permute-start | bytes 1572872 | tf_op jit(solution)/shard_map/ppermute | solution.py:35
  67.4 11.6 %collective-permute-start.19 = (bf16[2,128,1024]{2,1,0:T(8,128)(2,1)S(1)}, bf16[2,128,1024]{2,1,0:T(8,128)(2,1)S(1)}, u32[]{:S(2)}, u32[]{:S(2)}) collective-permute-start(bf16[2,128,1024]{2,1,0:T(8,128)(2,1)S(1)} %broadcast_select_fusion.8), channel_id=1, source_target_pairs={{0,24},{4,12},{8,16},{12,4},{16,8},{20,28},{24,0},{28,20},{32,56},... | collective-permute-start | bytes 1572872 | tf_op jit(solution)/shard_map/ppermute | solution.py:25
  73.5 17.7 %collective-permute-start.24 = (bf16[2,128,1536]{2,1,0:T(8,128)(2,1)S(1)}, bf16[2,128,1536]{2,1,0:T(8,128)(2,1)S(1)}, u32[]{:S(2)}, u32[]{:S(2)}) collective-permute-start(bf16[2,128,1536]{2,1,0:T(8,128)(2,1)S(1)} %broadcast_select_fusion.5), channel_id=1, source_target_pairs={{0,96},{4,36},{8,104},{12,44},{16,112},{20,52},{24,120},{28,60},{3... | collective-permute-start | bytes 2359304 | tf_op jit(solution)/shard_map/ppermute | solution.py:25
  75.7 10.4 %collective-permute-start.25 = (bf16[256,1024]{1,0:T(8,128)(2,1)S(1)}, bf16[256,1024]{1,0:T(8,128)(2,1)S(1)}, u32[]{:S(2)}, u32[]{:S(2)}) collective-permute-start(bf16[256,1024]{1,0:T(8,128)(2,1)S(1)} %collective-permute-done.22.refs_2_), channel_id=1, source_target_pairs={{0,1},{1,2},{2,3},{3,0},{4,7},{5,4},{6,5},{7,6},{8,9},{9,10},{10,1... | collective-permute-start | bytes 1572872 | tf_op jit(solution)/shard_map/ppermute | solution.py:35
  89.9 16.2 %collective-permute-start.27 = (bf16[2,128,1536]{2,1,0:T(8,128)(2,1)S(1)}, bf16[2,128,1536]{2,1,0:T(8,128)(2,1)S(1)}, u32[]{:S(2)}, u32[]{:S(2)}) collective-permute-start(bf16[2,128,1536]{2,1,0:T(8,128)(2,1)S(1)} %bitcast.51), channel_id=1, source_target_pairs={{0,32},{4,100},{8,40},{12,108},{16,48},{20,116},{24,56},{28,124},{... | collective-permute-start | bytes 2359304 | tf_op jit(solution)/shard_map/ppermute | solution.py:25
  90.1 10.4 %collective-permute-start.23 = (bf16[256,1024]{1,0:T(8,128)(2,1)S(1)}, bf16[256,1024]{1,0:T(8,128)(2,1)S(1)}, u32[]{:S(2)}, u32[]{:S(2)}) collective-permute-start(bf16[256,1024]{1,0:T(8,128)(2,1)S(1)} %bitcast.61), channel_id=1, source_target_pairs={{0,1},{1,2},{2,3},{3,0},{4,7},{5,4},{6,5},{7,6},{8,9},{9,10},{10,1... | collective-permute-start | bytes 1572872 | tf_op jit(solution)/shard_map/ppermute | solution.py:35
  90.2 15.9 %collective-permute-start.28 = (bf16[256,1024]{1,0:T(8,128)(2,1)S(1)}, bf16[256,1024]{1,0:T(8,128)(2,1)S(1)}, u32[]{:S(2)}, u32[]{:S(2)}) collective-permute-start(bf16[256,1024]{1,0:T(8,128)(2,1)S(1)} %collective-permute-done.20.refs_1_), channel_id=1, source_target_pairs={{0,1},{1,2},{2,3},{3,0},{4,7},{5,4},{6,5},{7,6},{8,9},{9,10},{10,1... | collective-permute-start | bytes 1572872 | tf_op jit(solution)/shard_map/ppermute | solution.py:35
  91.3 21.9 %collective-permute-start.31 = (bf16[2,128,1536]{2,1,0:T(8,128)(2,1)S(1)}, bf16[2,128,1536]{2,1,0:T(8,128)(2,1)S(1)}, u32[]{:S(2)}, u32[]{:S(2)}) collective-permute-start(bf16[2,128,1536]{2,1,0:T(8,128)(2,1)S(1)} %broadcast_select_fusion.4), channel_id=1, source_target_pairs={{0,8},{4,28},{8,0},{12,20},{16,24},{20,12},{24,16},{28,4},{32,40},... | collective-permute-start | bytes 2359304 | tf_op jit(solution)/shard_map/ppermute | solution.py:25
  100.5 11.2 %collective-permute-start.26 = (bf16[256,1024]{1,0:T(8,128)(2,1)S(1)}, bf16[256,1024]{1,0:T(8,128)(2,1)S(1)}, u32[]{:S(2)}, u32[]{:S(2)}) collective-permute-start(bf16[256,1024]{1,0:T(8,128)(2,1)S(1)} %collective-permute-done.23.refs_1_), channel_id=1, source_target_pairs={{0,1},{1,2},{2,3},{3,0},{4,7},{5,4},{6,5},{7,6},{8,9},{9,10},{10,1... | collective-permute-start | bytes 1572872 | tf_op jit(solution)/shard_map/ppermute | solution.py:35
  106.1 11.2 %collective-permute-start.30 = (bf16[256,1024]{1,0:T(8,128)(2,1)S(1)}, bf16[256,1024]{1,0:T(8,128)(2,1)S(1)}, u32[]{:S(2)}, u32[]{:S(2)}) collective-permute-start(bf16[256,1024]{1,0:T(8,128)(2,1)S(1)} %collective-permute-done.28.refs_2_), channel_id=1, source_target_pairs={{0,1},{1,2},{2,3},{3,0},{4,7},{5,4},{6,5},{7,6},{8,9},{9,10},{10,1... | collective-permute-start | bytes 1572872 | tf_op jit(solution)/shard_map/ppermute | solution.py:35
  111.7 11.2 %collective-permute-start.29 = (bf16[256,1024]{1,0:T(8,128)(2,1)S(1)}, bf16[256,1024]{1,0:T(8,128)(2,1)S(1)}, u32[]{:S(2)}, u32[]{:S(2)}) collective-permute-start(bf16[256,1024]{1,0:T(8,128)(2,1)S(1)} %collective-permute-done.26.refs_2_), channel_id=1, source_target_pairs={{0,1},{1,2},{2,3},{3,0},{4,7},{5,4},{6,5},{7,6},{8,9},{9,10},{10,1... | collective-permute-start | bytes 1572872 | tf_op jit(solution)/shard_map/ppermute | solution.py:35
  111.7 15.7 %collective-permute-start.33 = (bf16[2,128,1536]{2,1,0:T(8,128)(2,1)S(1)}, bf16[2,128,1536]{2,1,0:T(8,128)(2,1)S(1)}, u32[]{:S(2)}, u32[]{:S(2)}) collective-permute-start(bf16[2,128,1536]{2,1,0:T(8,128)(2,1)S(1)} %broadcast_select_fusion.3), channel_id=1, source_target_pairs={{0,96},{4,36},{8,104},{12,44},{16,112},{20,52},{24,120},{28,60},{3... | collective-permute-start | bytes 2359304 | tf_op jit(solution)/shard_map/ppermute | solution.py:25
  113.4 14.2 %collective-permute-start.32 = (bf16[2,128,1536]{2,1,0:T(8,128)(2,1)S(1)}, bf16[2,128,1536]{2,1,0:T(8,128)(2,1)S(1)}, u32[]{:S(2)}, u32[]{:S(2)}) collective-permute-start(bf16[2,128,1536]{2,1,0:T(8,128)(2,1)S(1)} %broadcast_select_fusion.2), channel_id=1, source_target_pairs={{0,24},{4,12},{8,16},{12,4},{16,8},{20,28},{24,0},{28,20},{32,56},... | collective-permute-start | bytes 2359304 | tf_op jit(solution)/shard_map/ppermute | solution.py:25

commit v4 on v3

--- a/solution.py
+++ b/solution.py
@@ -80,7 +80,7 @@
 def product_kernel(first, at_ref, place_ref, base_ref, *refs):
     *sources, tiles_hbm = refs[:5]
     out_hbm, x, tiles, total, out, sems = refs[-6:]
-    rows = total.shape[0]
+    rows = out.shape[0]
     loads = [pltpu.make_async_copy(tiles_hbm, tiles, sems.at[4])]
     loads += [pltpu.make_async_copy(sources[j], x.at[j], sems.at[j]) for j in range(4)]
     for load in loads:
@@ -98,10 +98,10 @@
                 preferred_element_type=jnp.float32,
             )
             for i in range(2):
-                where = pl.ds(pl.multiple_of(place_ref[2 * at + i] * TILE, TILE), TILE)
-                total[:, where] += part[:, i * TILE : (i + 1) * TILE]
-
-    out[...] = total[...].astype(out.dtype)
+                total[place_ref[2 * at + i]] += part[:, i * TILE : (i + 1) * TILE]
+
+    for j in range(WIDTH // TILE):
+        out[:, j * TILE : (j + 1) * TILE] = total[j].astype(out.dtype)
     store = pltpu.make_async_copy(out, out_hbm.at[pl.ds(first, rows)], sems.at[5])
     store.start()
     store.wait()
@@ -125,7 +125,7 @@
             scratch_shapes=[
                 pltpu.VMEM((4, rows, DEPTH), jnp.bfloat16),
                 pltpu.VMEM(tiles.shape, jnp.bfloat16),
-                pltpu.VMEM((rows, WIDTH), jnp.float32),
+                pltpu.VMEM((WIDTH // TILE, rows, TILE), jnp.float32),
                 pltpu.VMEM((rows, WIDTH), jnp.bfloat16),
                 pltpu.SemaphoreType.DMA((6,)),
             ],
@@ -241,9 +241,9 @@
     moving, rings = [None] * 4, [None] * 4
     tiles = Tiles(seq.done(pack(amplitudes, screen)))
     tiles.send()
-    moving[0] = group(0)
     moving[3] = group(3)
     moving[3].send()
+    moving[0] = group(0)
     tiles.take()
     tiles.send()
     moving[1] = group(1)
@@ -252,13 +252,13 @@
     rings[0].send()
     moving[2] = group(2)
     moving[2].send()
+    rings[0].take()
     tiles.take()
     tiles.send()
     moving[3].take()
     moving[3].send()
     moving[1].take()
     moving[1].send()
-    rings[0].take()
     rings[0].send()
     tiles.take()
     tiles.send()
@@ -298,11 +298,11 @@
     rings[2].send()
     rings[3].send()
     rings[1].take()
+    rings[2].take()
     moving[1] = onward(moving[1], rings[1].blocks)
     moving[1].send()
     moving[0].take()
     moving[0].send()
-    rings[2].take()
     rings[2].send()
     rings[3].take()
     rings[3].send()

time: 130 us -> 128 us (0.985)
  waiting for transfers between devices: 55.1 us -> 51.6 us
  starting transfers between devices: 36.8 us -> 39.6 us
  Pallas kernels: 18.1 us -> 16.5 us
    ppermute x12, starting transfers between devices: 10.2 us -> 14.3 us  [turn(): return lax.ppermute(value, AXES, pairs)]
    ppermute x12, waiting for transfers between devices: 35 us -> 30.9 us  [turn(): return lax.ppermute(value, AXES, pairs)]
    pallas_call x4, Pallas kernels: 16.2 us -> 14.6 us  [product(): pl.pallas_call(functools.partial(product_kernel, first), grid_spec=pltpu....]
    ppermute x22, starting transfers between devices: 26.6 us -> 25.3 us  [exchange(): return lax.ppermute(value, 'row', pairs)]
  transfers between devices with their start and end apart: 34 -> 34, of which waited for: 15 -> 16; matrix products, arithmetic and copies ran while one was open for 12% -> 12% of each run, Pallas kernels for 14% -> 13%
where the time goes in v4:
time: 128 us; the launch traced here: 127 us
  waiting for transfers between devices  51.6 us (40%)
  starting transfers between devices  39.6 us (31%)
  Pallas kernels  16.5 us (13%)
  other arithmetic  14.8 us (12%)
  local copies, waits for them, and re-layouts  4.49 us (4%)
    ppermute x12, waiting for transfers between devices, turn(): return lax.ppermute(value, AXES, pairs)  30.9 us
    ppermute x22, starting transfers between devices, exchange(): return lax.ppermute(value, 'row', pairs)  25.3 us
    ppermute x22, waiting for transfers between devices, exchange(): return lax.ppermute(value, 'row', pairs)  20.8 us
    pallas_call x4, Pallas kernels, product(): pl.pallas_call(functools.partial(product_kernel, first), grid_spec=pltpu....  14.6 us
    ppermute x12, starting transfers between devices, turn(): return lax.ppermute(value, AXES, pairs)  14.3 us
    select_n x20, other arithmetic, choose(): return jnp.where(taken[:, None, None], partner, mine)  13 us
  transfers between devices with their start and end apart: 34, of which 16 were waited for; matrix products, arithmetic and copies ran while one was open for 12% of the time, Pallas kernels for 13%

profile of v4, /device:TPU:0, one launch (start us, length us, event | category | flops | bytes accessed | tf_op | source)
XLA Modules:
  0.0 127.3 jit_solution(17341328763344296271)
XLA Ops:
  0.0 1.8 %shard_map.73 = bf16[1,144,256]{2,1,0:T(8,128)(2,1)} custom-call(s32[1,12]{1,0:T(1,128)} %screen_ref.1, bf16[128,1536]{1,0:T(8,128)(2,1)} %amplitudes_ref.1), custom_call_target="tpu_custom_call" | custom-call | flops 1 | bytes 1 | tf_op jit(solution)/shard_map/pallas_call | solution.py:59
  1.8 1.6 %collective-permute-start = (bf16[1,144,256]{2,1,0:T(8,128)(2,1)}, bf16[1,144,256]{2,1,0:T(8,128)(2,1)S(1)}, u32[]{:S(2)}, u32[]{:S(2)}) collective-permute-start(bf16[1,144,256]{2,1,0:T(8,128)(2,1)} %shard_map.73), channel_id=1, source_target_pairs={{0,8},{4,28},{8,0},{12,20},{16,24},{20,12},{24,16},{28,4},{32,40},... | collective-permute-start | bytes 221192 | tf_op jit(solution)/shard_map/ppermute | solution.py:25
  5.6 1.3 %slice_select_fusion.3 = bf16[2,128,1024]{2,1,0:T(8,128)(2,1)S(1)} fusion(bf16[8,128,1024]{2,1,0:T(8,128)(2,1)} %bitcast.66, bf16[8,128,1024]{2,1,0:T(8,128)(2,1)} %collective-permute-done.1, pred[2]{0:T(512)(128)(4,1)S(1)} %get-tuple-element.279), kind=kLoop, calls=%fused_computation.12 | loop fusion | flops 262144 | bytes 1572866 | tf_op jit(solution)/shard_map/jit(_where)/select_n | solution.py:40
  7.0 1.2 slice_select_fusion.2
  8.2 1.2 slice_select_fusion.1
  9.4 2.0 %collective-permute-start.3 = (bf16[256,1024]{1,0:T(8,128)(2,1)S(1)}, bf16[256,1024]{1,0:T(8,128)(2,1)S(1)}, u32[]{:S(2)}, u32[]{:S(2)}) collective-permute-start(bf16[256,1024]{1,0:T(8,128)(2,1)S(1)} %bitcast.55), channel_id=1, source_target_pairs={{0,1},{1,2},{2,3},{3,0},{4,7},{5,4},{6,5},{7,6},{8,9},{9,10},{10,1... | collective-permute-start | bytes 1572872 | tf_op jit(solution)/shard_map/ppermute | solution.py:35
  11.4 1.6 %collective-permute-start.6 = (bf16[2,128,1024]{2,1,0:T(8,128)(2,1)S(1)}, bf16[2,128,1024]{2,1,0:T(8,128)(2,1)S(1)}, u32[]{:S(2)}, u32[]{:S(2)}) collective-permute-start(bf16[2,128,1024]{2,1,0:T(8,128)(2,1)S(1)} %slice_select_fusion.3), channel_id=1, source_target_pairs={{0,32},{4,100},{8,40},{12,108},{16,48},{20,116},{24,56},{28,124},{... | collective-permute-start | bytes 1572872 | tf_op jit(solution)/shard_map/ppermute | solution.py:25
  13.0 2.1 %collective-permute-start.2 = (bf16[2,144,256]{2,1,0:T(8,128)(2,1)S(1)}, bf16[2,144,256]{2,1,0:T(8,128)(2,1)S(1)}, u32[]{:S(2)}, u32[]{:S(2)}) collective-permute-start(bf16[2,144,256]{2,1,0:T(8,128)(2,1)S(1)} %pad_maximum_fusion.4), channel_id=1, source_target_pairs={{0,24},{4,12},{8,16},{12,4},{16,8},{20,28},{24,0},{28,20},{32,56},... | collective-permute-start | bytes 442376 | tf_op jit(solution)/shard_map/ppermute | solution.py:25
  15.7 1.2 slice_select_fusion
  16.9 1.5 %collective-permute-start.11 = (bf16[2,128,1024]{2,1,0:T(8,128)(2,1)S(1)}, bf16[2,128,1024]{2,1,0:T(8,128)(2,1)S(1)}, u32[]{:S(2)}, u32[]{:S(2)}) collective-permute-start(bf16[2,128,1024]{2,1,0:T(8,128)(2,1)S(1)} %slice_select_fusion), channel_id=1, source_target_pairs={{0,8},{4,28},{8,0},{12,20},{16,24},{20,12},{24,16},{28,4},{32,40},... | collective-permute-start | bytes 1572872 | tf_op jit(solution)/shard_map/ppermute | solution.py:25
  18.4 2.3 %collective-permute-done.3.refs_1_ = bf16[256,1024]{1,0:T(8,128)(2,1)S(1)} collective-permute-done((bf16[256,1024]{1,0:T(8,128)(2,1)S(1)}, bf16[256,1024]{1,0:T(8,128)(2,1)S(1)}, u32[]{:S(2)}, u32[]{:S(2)}) %collective-permute-start.3) | collective-permute-done | bytes 524320 | tf_op jit(solution)/shard_map/ppermute | solution.py:35
  20.7 1.7 %collective-permute-start.4 = (bf16[4,144,256]{2,1,0:T(8,128)(2,1)S(1)}, bf16[4,144,256]{2,1,0:T(8,128)(2,1)S(1)}, u32[]{:S(2)}, u32[]{:S(2)}) collective-permute-start(bf16[4,144,256]{2,1,0:T(8,128)(2,1)S(1)} %pad_maximum_fusion.3), channel_id=1, source_target_pairs={{0,32},{4,100},{8,40},{12,108},{16,48},{20,116},{24,56},{28,124},{... | collective-permute-start | bytes 884744 | tf_op jit(solution)/shard_map/ppermute | solution.py:25
  22.5 3.3 %collective-permute-done.5 = bf16[2,128,1024]{2,1,0:T(8,128)(2,1)S(1)} collective-permute-done((bf16[2,128,1024]{2,1,0:T(8,128)(2,1)S(1)}, bf16[2,128,1024]{2,1,0:T(8,128)(2,1)S(1)}, u32[]{:S(2)}, u32[]{:S(2)}) %collective-permute-start.5) | collective-permute-done | bytes 524320 | tf_op jit(solution)/shard_map/ppermute | solution.py:25
  25.8 1.6 %collective-permute-start.10 = (bf16[2,128,1024]{2,1,0:T(8,128)(2,1)S(1)}, bf16[2,128,1024]{2,1,0:T(8,128)(2,1)S(1)}, u32[]{:S(2)}, u32[]{:S(2)}) collective-permute-start(bf16[2,128,1024]{2,1,0:T(8,128)(2,1)S(1)} %broadcast_select_fusion.14), channel_id=1, source_target_pairs={{0,96},{4,36},{8,104},{12,44},{16,112},{20,52},{24,120},{28,60},{3... | collective-permute-start | bytes 1572872 | tf_op jit(solution)/shard_map/ppermute | solution.py:25
  28.5 1.1 collective-permute-start.9
  29.8 1.7 %collective-permute-start.7 = (bf16[8,144,256]{2,1,0:T(8,128)(2,1)S(1)}, bf16[8,144,256]{2,1,0:T(8,128)(2,1)S(1)}, u32[]{:S(2)}, u32[]{:S(2)}) collective-permute-start(bf16[8,144,256]{2,1,0:T(8,128)(2,1)S(1)} %pad_maximum_fusion.2), channel_id=1, source_target_pairs={{0,96},{4,36},{8,104},{12,44},{16,112},{20,52},{24,120},{28,60},{3... | collective-permute-start | bytes 1769480 | tf_op jit(solution)/shard_map/ppermute | solution.py:25
  31.5 1.6 %collective-permute-done.11 = bf16[2,128,1024]{2,1,0:T(8,128)(2,1)S(1)} collective-permute-done((bf16[2,128,1024]{2,1,0:T(8,128)(2,1)S(1)}, bf16[2,128,1024]{2,1,0:T(8,128)(2,1)S(1)}, u32[]{:S(2)}, u32[]{:S(2)}) %collective-permute-start.11) | collective-permute-done | bytes 524320 | tf_op jit(solution)/shard_map/ppermute | solution.py:25
  34.1 2.2 %collective-permute-done.10 = bf16[2,128,1024]{2,1,0:T(8,128)(2,1)S(1)} collective-permute-done((bf16[2,128,1024]{2,1,0:T(8,128)(2,1)S(1)}, bf16[2,128,1024]{2,1,0:T(8,128)(2,1)S(1)}, u32[]{:S(2)}, u32[]{:S(2)}) %collective-permute-start.10) | collective-permute-done | bytes 524320 | tf_op jit(solution)/shard_map/ppermute | solution.py:25
  36.3 2.6 %collective-permute-done.9 = bf16[2,128,1024]{2,1,0:T(8,128)(2,1)S(1)} collective-permute-done((bf16[2,128,1024]{2,1,0:T(8,128)(2,1)S(1)}, bf16[2,128,1024]{2,1,0:T(8,128)(2,1)S(1)}, u32[]{:S(2)}, u32[]{:S(2)}) %collective-permute-start.9) | collective-permute-done | bytes 524320 | tf_op jit(solution)/shard_map/ppermute | solution.py:25
  39.1 3.5 %collective-permute-done.7 = bf16[8,144,256]{2,1,0:T(8,128)(2,1)S(1)} collective-permute-done((bf16[8,144,256]{2,1,0:T(8,128)(2,1)S(1)}, bf16[8,144,256]{2,1,0:T(8,128)(2,1)S(1)}, u32[]{:S(2)}, u32[]{:S(2)}) %collective-permute-start.7) | collective-permute-done | bytes 589856 | tf_op jit(solution)/shard_map/ppermute | solution.py:25
  44.0 1.4 %collective-permute-start.18 = (bf16[256,1024]{1,0:T(8,128)(2,1)S(1)}, bf16[256,1024]{1,0:T(8,128)(2,1)}, u32[]{:S(2)}, u32[]{:S(2)}) collective-permute-start(bf16[256,1024]{1,0:T(8,128)(2,1)S(1)} %bitcast.57), channel_id=1, source_target_pairs={{0,1},{1,2},{2,3},{3,0},{4,7},{5,4},{6,5},{7,6},{8,9},{9,10},{10,1... | collective-permute-start | bytes 1572872 | tf_op jit(solution)/shard_map/ppermute | solution.py:35
  45.4 6.6 %collective-permute-done.13 = bf16[2,128,1024]{2,1,0:T(8,128)(2,1)S(1)} collective-permute-done((bf16[2,128,1024]{2,1,0:T(8,128)(2,1)S(1)}, bf16[2,128,1024]{2,1,0:T(8,128)(2,1)S(1)}, u32[]{:S(2)}, u32[]{:S(2)}) %collective-permute-start.13) | collective-permute-done | bytes 524320 | tf_op jit(solution)/shard_map/ppermute | solution.py:25
  52.9 1.1 collective-permute-start.16
  54.4 2.1 %broadcast_select_fusion.7 = bf16[2,128,1024]{2,1,0:T(8,128)(2,1)} fusion(bf16[2,128,1024]{2,1,0:T(8,128)(2,1)} %collective-permute-done.14, bf16[2,128,1024]{2,1,0:T(8,128)(2,1)} %broadcast_select_fusion.11, pred[2]{0:T(512)(128)(4,1)S(1)} %get-tuple-element.268), kind=kLoop, calls=%fused_computation.14 | loop fusion | flops 262144 | bytes 1572866 | tf_op jit(solution)/shard_map/jit(_where)/select_n | solution.py:40
  56.5 1.2 collective-permute-start.15
  59.5 3.1 %shard_map.74 = bf16[256,1536]{1,0:T(8,128)(2,1)S(1)} custom-call(s32[1,32]{1,0:T(1,128)S(1)} %constant_dynamic-slice_fusion.at_ref, s32[64]{0:T(128)S(1)} %reshape.184.place_ref, s32[4]{0:T(128)S(1)} %subtract_and_fusion.base_ref, bf16[256,1024]{1,0:T(8,128)(2,1)S(1)} %bitcast.56, bf16[256,1024]{1,0:T(8,128)(2,1)S(1)} %copy-done.1, ...), custom_call_target="tpu_custom_call" | custom-call | flops 1 | bytes 1 | tf_op jit(solution)/shard_map/pallas_call | solution.py:118
  63.6 2.6 %collective-permute-start.22 = (bf16[256,1024]{1,0:T(8,128)(2,1)}, bf16[256,1024]{1,0:T(8,128)(2,1)S(1)}, u32[]{:S(2)}, u32[]{:S(2)}) collective-permute-start(bf16[256,1024]{1,0:T(8,128)(2,1)} %collective-permute-done.18.refs_1_), channel_id=1, source_target_pairs={{0,1},{1,2},{2,3},{3,0},{4,7},{5,4},{6,5},{7,6},{8,9},{9,10},{10,1... | collective-permute-start | bytes 1572872 | tf_op jit(solution)/shard_map/ppermute | solution.py:35
  66.2 1.3 %broadcast_select_fusion.6 = bf16[2,128,1024]{2,1,0:T(8,128)(2,1)S(1)} fusion(bf16[2,128,1024]{2,1,0:T(8,128)(2,1)} %collective-permute-done.16, bf16[2,128,1024]{2,1,0:T(8,128)(2,1)} %broadcast_select_fusion.10, pred[2]{0:T(512)(128)(4,1)S(1)} %get-tuple-element.267), kind=kLoop, calls=%fused_computation.13 | loop fusion | flops 262144 | bytes 1572866 | tf_op jit(solution)/shard_map/jit(_where)/select_n | solution.py:40
  67.5 1.8 %collective-permute-start.20 = (bf16[256,1024]{1,0:T(8,128)(2,1)S(1)}, bf16[256,1024]{1,0:T(8,128)(2,1)S(1)}, u32[]{:S(2)}, u32[]{:S(2)}) collective-permute-start(bf16[256,1024]{1,0:T(8,128)(2,1)S(1)} %bitcast.59), channel_id=1, source_target_pairs={{0,1},{1,2},{2,3},{3,0},{4,7},{5,4},{6,5},{7,6},{8,9},{9,10},{10,1... | collective-permute-start | bytes 1572872 | tf_op jit(solution)/shard_map/ppermute | solution.py:35
  69.3 1.3 %broadcast_select_fusion.8 = bf16[2,128,1024]{2,1,0:T(8,128)(2,1)S(1)} fusion(bf16[2,128,1024]{2,1,0:T(8,128)(2,1)} %collective-permute-done.15, bf16[2,128,1024]{2,1,0:T(8,128)(2,1)} %broadcast_select_fusion.7, pred[2]{0:T(512)(128)(4,1)S(1)} %get-tuple-element.269), kind=kLoop, calls=%fused_computation.15 | loop fusion | flops 262144 | bytes 1572866 | tf_op jit(solution)/shard_map/jit(_where)/select_n | solution.py:40
  70.7 2.3 %collective-permute-start.19 = (bf16[2,128,1024]{2,1,0:T(8,128)(2,1)S(1)}, bf16[2,128,1024]{2,1,0:T(8,128)(2,1)S(1)}, u32[]{:S(2)}, u32[]{:S(2)}) collective-permute-start(bf16[2,128,1024]{2,1,0:T(8,128)(2,1)S(1)} %broadcast_select_fusion.8), channel_id=1, source_target_pairs={{0,24},{4,12},{8,16},{12,4},{16,8},{20,28},{24,0},{28,20},{32,56},... | collective-permute-start | bytes 1572872 | tf_op jit(solution)/shard_map/ppermute | solution.py:25
  72.9 1.3 %collective-permute-done.22.refs_2_ = bf16[256,1024]{1,0:T(8,128)(2,1)S(1)} collective-permute-done((bf16[256,1024]{1,0:T(8,128)(2,1)}, bf16[256,1024]{1,0:T(8,128)(2,1)S(1)}, u32[]{:S(2)}, u32[]{:S(2)}) %collective-permute-start.22) | collective-permute-done | bytes 524320 | tf_op jit(solution)/shard_map/ppermute | solution.py:35
  74.2 1.4 %collective-permute-start.24 = (bf16[256,1024]{1,0:T(8,128)(2,1)S(1)}, bf16[256,1024]{1,0:T(8,128)(2,1)S(1)}, u32[]{:S(2)}, u32[]{:S(2)}) collective-permute-start(bf16[256,1024]{1,0:T(8,128)(2,1)S(1)} %collective-permute-done.22.refs_2_), channel_id=1, source_target_pairs={{0,1},{1,2},{2,3},{3,0},{4,7},{5,4},{6,5},{7,6},{8,9},{9,10},{10,1... | collective-permute-start | bytes 1572872 | tf_op jit(solution)/shard_map/ppermute | solution.py:35
  75.8 4.1 %collective-permute-done.20.refs_1_ = bf16[256,1024]{1,0:T(8,128)(2,1)S(1)} collective-permute-done((bf16[256,1024]{1,0:T(8,128)(2,1)S(1)}, bf16[256,1024]{1,0:T(8,128)(2,1)S(1)}, u32[]{:S(2)}, u32[]{:S(2)}) %collective-permute-start.20) | collective-permute-done | bytes 524320 | tf_op jit(solution)/shard_map/ppermute | solution.py:35
  79.9 1.6 %collective-permute-start.25 = (bf16[2,128,1536]{2,1,0:T(8,128)(2,1)S(1)}, bf16[2,128,1536]{2,1,0:T(8,128)(2,1)S(1)}, u32[]{:S(2)}, u32[]{:S(2)}) collective-permute-start(bf16[2,128,1536]{2,1,0:T(8,128)(2,1)S(1)} %broadcast_select_fusion.5), channel_id=1, source_target_pairs={{0,96},{4,36},{8,104},{12,44},{16,112},{20,52},{24,120},{28,60},{3... | collective-permute-start | bytes 2359304 | tf_op jit(solution)/shard_map/ppermute | solution.py:25
  81.5 1.3 collective-permute-start.23
  82.8 2.7 %collective-permute-done.24.refs_3_ = bf16[256,1024]{1,0:T(8,128)(2,1)S(1)} collective-permute-done((bf16[256,1024]{1,0:T(8,128)(2,1)S(1)}, bf16[256,1024]{1,0:T(8,128)(2,1)S(1)}, u32[]{:S(2)}, u32[]{:S(2)}) %collective-permute-start.24) | collective-permute-done | bytes 524320 | tf_op jit(solution)/shard_map/ppermute | solution.py:35
  85.5 3.5 %shard_map.75 = bf16[256,1536]{1,0:T(8,128)(2,1)S(1)} custom-call(s32[1,32]{1,0:T(1,128)S(1)} %constant_dynamic-slice_fusion.at_ref, s32[64]{0:T(128)S(1)} %reshape.184.place_ref, s32[4]{0:T(128)S(1)} %subtract_and_fusion.base_ref, bf16[256,1024]{1,0:T(8,128)(2,1)S(1)} %bitcast.58, bf16[256,1024]{1,0:T(8,128)(2,1)} %collective-permute-done.18.refs_1_, ...), custom_call_target="tpu_custom_call" | custom-call | flops 1 | bytes 1 | tf_op jit(solution)/shard_map/pallas_call | solution.py:118
  89.0 3.2 %collective-permute-done.23.refs_1_ = bf16[256,1024]{1,0:T(8,128)(2,1)S(1)} collective-permute-done((bf16[256,1024]{1,0:T(8,128)(2,1)S(1)}, bf16[256,1024]{1,0:T(8,128)(2,1)S(1)}, u32[]{:S(2)}, u32[]{:S(2)}) %collective-permute-start.23) | collective-permute-done | bytes 524320 | tf_op jit(solution)/shard_map/ppermute | solution.py:35
  92.2 1.6 %collective-permute-start.27 = (bf16[2,128,1536]{2,1,0:T(8,128)(2,1)S(1)}, bf16[2,128,1536]{2,1,0:T(8,128)(2,1)S(1)}, u32[]{:S(2)}, u32[]{:S(2)}) collective-permute-start(bf16[2,128,1536]{2,1,0:T(8,128)(2,1)S(1)} %bitcast.53), channel_id=1, source_target_pairs={{0,32},{4,100},{8,40},{12,108},{16,48},{20,116},{24,56},{28,124},{... | collective-permute-start | bytes 2359304 | tf_op jit(solution)/shard_map/ppermute | solution.py:25
  94.7 1.8 %collective-permute-start.26 = (bf16[256,1024]{1,0:T(8,128)(2,1)S(1)}, bf16[256,1024]{1,0:T(8,128)(2,1)S(1)}, u32[]{:S(2)}, u32[]{:S(2)}) collective-permute-start(bf16[256,1024]{1,0:T(8,128)(2,1)S(1)} %collective-permute-done.23.refs_1_), channel_id=1, source_target_pairs={{0,1},{1,2},{2,3},{3,0},{4,7},{5,4},{6,5},{7,6},{8,9},{9,10},{10,1... | collective-permute-start | bytes 1572872 | tf_op jit(solution)/shard_map/ppermute | solution.py:35
  96.4 7.8 %collective-permute-done.28.refs_2_ = bf16[256,1024]{1,0:T(8,128)(2,1)S(1)} collective-permute-done((bf16[256,1024]{1,0:T(8,128)(2,1)S(1)}, bf16[256,1024]{1,0:T(8,128)(2,1)S(1)}, u32[]{:S(2)}, u32[]{:S(2)}) %collective-permute-start.28) | collective-permute-done | bytes 524320 | tf_op jit(solution)/shard_map/ppermute | solution.py:35
  104.4 5.5 %collective-permute-done.26.refs_2_ = bf16[256,1024]{1,0:T(8,128)(2,1)S(1)} collective-permute-done((bf16[256,1024]{1,0:T(8,128)(2,1)S(1)}, bf16[256,1024]{1,0:T(8,128)(2,1)S(1)}, u32[]{:S(2)}, u32[]{:S(2)}) %collective-permute-start.26) | collective-permute-done | bytes 524320 | tf_op jit(solution)/shard_map/ppermute | solution.py:35
  110.6 2.4 %collective-permute-start.32 = (bf16[2,128,1536]{2,1,0:T(8,128)(2,1)S(1)}, bf16[2,128,1536]{2,1,0:T(8,128)(2,1)S(1)}, u32[]{:S(2)}, u32[]{:S(2)}) collective-permute-start(bf16[2,128,1536]{2,1,0:T(8,128)(2,1)S(1)} %broadcast_select_fusion.2), channel_id=1, source_target_pairs={{0,24},{4,12},{8,16},{12,4},{16,8},{20,28},{24,0},{28,20},{32,56},... | collective-permute-start | bytes 2359304 | tf_op jit(solution)/shard_map/ppermute | solution.py:25
  113.0 2.4 %collective-permute-done.30.refs_3_ = bf16[256,1024]{1,0:T(8,128)(2,1)S(1)} collective-permute-done((bf16[256,1024]{1,0:T(8,128)(2,1)S(1)}, bf16[256,1024]{1,0:T(8,128)(2,1)S(1)}, u32[]{:S(2)}, u32[]{:S(2)}) %collective-permute-start.30) | collective-permute-done | bytes 524320 | tf_op jit(solution)/shard_map/ppermute | solution.py:35
  115.5 4.0 %shard_map.76.refs_5_ = bf16[1024,1536]{1,0:T(8,128)(2,1)} custom-call(s32[1,32]{1,0:T(1,128)S(1)} %constant_dynamic-slice_fusion.at_ref, s32[64]{0:T(128)S(1)} %reshape.184.place_ref, s32[4]{0:T(128)S(1)} %subtract_and_fusion.base_ref, bf16[256,1024]{1,0:T(8,128)(2,1)S(1)} %bitcast.60, bf16[256,1024]{1,0:T(8,128)(2,1)S(1)} %collective-permute-done.20.refs_1_, ...), custom_call_target="tpu_custom_call" | custom-call | flops 1 | bytes 1 | tf_op jit(solution)/shard_map/pallas_call | solution.py:118
  119.5 1.6 %collective-permute-done.29.refs_3_ = bf16[256,1024]{1,0:T(8,128)(2,1)S(1)} collective-permute-done((bf16[256,1024]{1,0:T(8,128)(2,1)S(1)}, bf16[256,1024]{1,0:T(8,128)(2,1)S(1)}, u32[]{:S(2)}, u32[]{:S(2)}) %collective-permute-start.29) | collective-permute-done | bytes 524320 | tf_op jit(solution)/shard_map/ppermute | solution.py:35
  121.1 4.0 %shard_map.77 = bf16[1024,1536]{1,0:T(8,128)(2,1)} custom-call(s32[1,32]{1,0:T(1,128)S(1)} %constant_dynamic-slice_fusion.at_ref, s32[64]{0:T(128)S(1)} %reshape.184.place_ref, s32[4]{0:T(128)S(1)} %subtract_and_fusion.base_ref, bf16[256,1024]{1,0:T(8,128)(2,1)S(1)} %bitcast.62, ...), custom_call_target="tpu_custom_call", output_to_operand_aliasing={{}: (8, {})} | custom-call | flops 1 | bytes 1 | tf_op jit(solution)/shard_map/pallas_call | solution.py:118
  (71 shorter events, 14.9 us)
Async XLA Ops:
  0.0 7.0 %copy-start.2 = (bf16[1024,1024]{1,0:T(8,128)(2,1)S(1)}, bf16[1024,1024]{1,0:T(8,128)(2,1)}, u32[]{:S(2)}) copy-start(bf16[1024,1024]{1,0:T(8,128)(2,1)} %param.7) | copy-start | bytes 6291460
  0.0 5.6 %collective-permute-start.1 = (bf16[8,128,1024]{2,1,0:T(8,128)(2,1)}, bf16[8,128,1024]{2,1,0:T(8,128)(2,1)}, u32[]{:S(2)}, u32[]{:S(2)}) collective-permute-start(bf16[8,128,1024]{2,1,0:T(8,128)(2,1)} %bitcast.65), channel_id=1, source_target_pairs={{0,4},{4,0},{8,12},{12,8},{16,20},{20,16},{24,28},{28,24},{32,36},... | collective-permute-start | bytes 6291464 | tf_op jit(solution)/shard_map/ppermute | solution.py:25
  1.8 6.3 %copy-start.3 = (bf16[1,144,256]{2,1,0:T(8,128)(2,1)S(1)}, bf16[1,144,256]{2,1,0:T(8,128)(2,1)}, u32[]{:S(2)}) copy-start(bf16[1,144,256]{2,1,0:T(8,128)(2,1)} %shard_map.73) | copy-start | bytes 221188
  1.8 6.3 %collective-permute-start = (bf16[1,144,256]{2,1,0:T(8,128)(2,1)}, bf16[1,144,256]{2,1,0:T(8,128)(2,1)S(1)}, u32[]{:S(2)}, u32[]{:S(2)}) collective-permute-start(bf16[1,144,256]{2,1,0:T(8,128)(2,1)} %shard_map.73), channel_id=1, source_target_pairs={{0,8},{4,28},{8,0},{12,20},{16,24},{20,12},{24,16},{28,4},{32,40},... | collective-permute-start | bytes 221192 | tf_op jit(solution)/shard_map/ppermute | solution.py:25
  9.4 11.3 %collective-permute-start.3 = (bf16[256,1024]{1,0:T(8,128)(2,1)S(1)}, bf16[256,1024]{1,0:T(8,128)(2,1)S(1)}, u32[]{:S(2)}, u32[]{:S(2)}) collective-permute-start(bf16[256,1024]{1,0:T(8,128)(2,1)S(1)} %bitcast.55), channel_id=1, source_target_pairs={{0,1},{1,2},{2,3},{3,0},{4,7},{5,4},{6,5},{7,6},{8,9},{9,10},{10,1... | collective-permute-start | bytes 1572872 | tf_op jit(solution)/shard_map/ppermute | solution.py:35
  11.4 11.0 %collective-permute-start.6 = (bf16[2,128,1024]{2,1,0:T(8,128)(2,1)S(1)}, bf16[2,128,1024]{2,1,0:T(8,128)(2,1)S(1)}, u32[]{:S(2)}, u32[]{:S(2)}) collective-permute-start(bf16[2,128,1024]{2,1,0:T(8,128)(2,1)S(1)} %slice_select_fusion.3), channel_id=1, source_target_pairs={{0,32},{4,100},{8,40},{12,108},{16,48},{20,116},{24,56},{28,124},{... | collective-permute-start | bytes 1572872 | tf_op jit(solution)/shard_map/ppermute | solution.py:25
  13.0 7.7 %collective-permute-start.2 = (bf16[2,144,256]{2,1,0:T(8,128)(2,1)S(1)}, bf16[2,144,256]{2,1,0:T(8,128)(2,1)S(1)}, u32[]{:S(2)}, u32[]{:S(2)}) collective-permute-start(bf16[2,144,256]{2,1,0:T(8,128)(2,1)S(1)} %pad_maximum_fusion.4), channel_id=1, source_target_pairs={{0,24},{4,12},{8,16},{12,4},{16,8},{20,28},{24,0},{28,20},{32,56},... | collective-permute-start | bytes 442376 | tf_op jit(solution)/shard_map/ppermute | solution.py:25
  15.1 10.8 %collective-permute-start.5 = (bf16[2,128,1024]{2,1,0:T(8,128)(2,1)S(1)}, bf16[2,128,1024]{2,1,0:T(8,128)(2,1)S(1)}, u32[]{:S(2)}, u32[]{:S(2)}) collective-permute-start(bf16[2,128,1024]{2,1,0:T(8,128)(2,1)S(1)} %slice_select_fusion.1), channel_id=1, source_target_pairs={{0,8},{4,28},{8,0},{12,20},{16,24},{20,12},{24,16},{28,4},{32,40},... | collective-permute-start | bytes 1572872 | tf_op jit(solution)/shard_map/ppermute | solution.py:25
  16.9 16.3 %collective-permute-start.11 = (bf16[2,128,1024]{2,1,0:T(8,128)(2,1)S(1)}, bf16[2,128,1024]{2,1,0:T(8,128)(2,1)S(1)}, u32[]{:S(2)}, u32[]{:S(2)}) collective-permute-start(bf16[2,128,1024]{2,1,0:T(8,128)(2,1)S(1)} %slice_select_fusion), channel_id=1, source_target_pairs={{0,8},{4,28},{8,0},{12,20},{16,24},{20,12},{24,16},{28,4},{32,40},... | collective-permute-start | bytes 1572872 | tf_op jit(solution)/shard_map/ppermute | solution.py:25
  20.7 9.1 %copy-start = (bf16[256,1024]{1,0:T(8,128)(2,1)}, bf16[256,1024]{1,0:T(8,128)(2,1)S(1)}, u32[]{:S(2)}) copy-start(bf16[256,1024]{1,0:T(8,128)(2,1)S(1)} %collective-permute-done.3.refs_1_) | copy-start | bytes 1572868
  20.7 9.0 %collective-permute-start.4 = (bf16[4,144,256]{2,1,0:T(8,128)(2,1)S(1)}, bf16[4,144,256]{2,1,0:T(8,128)(2,1)S(1)}, u32[]{:S(2)}, u32[]{:S(2)}) collective-permute-start(bf16[4,144,256]{2,1,0:T(8,128)(2,1)S(1)} %pad_maximum_fusion.3), channel_id=1, source_target_pairs={{0,32},{4,100},{8,40},{12,108},{16,48},{20,116},{24,56},{28,124},{... | collective-permute-start | bytes 884744 | tf_op jit(solution)/shard_map/ppermute | solution.py:25
  25.8 10.4 %collective-permute-start.10 = (bf16[2,128,1024]{2,1,0:T(8,128)(2,1)S(1)}, bf16[2,128,1024]{2,1,0:T(8,128)(2,1)S(1)}, u32[]{:S(2)}, u32[]{:S(2)}) collective-permute-start(bf16[2,128,1024]{2,1,0:T(8,128)(2,1)S(1)} %broadcast_select_fusion.14), channel_id=1, source_target_pairs={{0,96},{4,36},{8,104},{12,44},{16,112},{20,52},{24,120},{28,60},{3... | collective-permute-start | bytes 1572872 | tf_op jit(solution)/shard_map/ppermute | solution.py:25
  27.5 11.5 %collective-permute-start.8 = (bf16[256,1024]{1,0:T(8,128)(2,1)S(1)}, bf16[256,1024]{1,0:T(8,128)(2,1)}, u32[]{:S(2)}, u32[]{:S(2)}) collective-permute-start(bf16[256,1024]{1,0:T(8,128)(2,1)S(1)} %collective-permute-done.3.refs_1_), channel_id=1, source_target_pairs={{0,1},{1,2},{2,3},{3,0},{4,7},{5,4},{6,5},{7,6},{8,9},{9,10},{10,1... | collective-permute-start | bytes 1572872 | tf_op jit(solution)/shard_map/ppermute | solution.py:35
  28.5 10.4 %collective-permute-start.9 = (bf16[2,128,1024]{2,1,0:T(8,128)(2,1)S(1)}, bf16[2,128,1024]{2,1,0:T(8,128)(2,1)S(1)}, u32[]{:S(2)}, u32[]{:S(2)}) collective-permute-start(bf16[2,128,1024]{2,1,0:T(8,128)(2,1)S(1)} %broadcast_select_fusion.15), channel_id=1, source_target_pairs={{0,24},{4,12},{8,16},{12,4},{16,8},{20,28},{24,0},{28,20},{32,56},... | collective-permute-start | bytes 1572872 | tf_op jit(solution)/shard_map/ppermute | solution.py:25
  29.8 12.8 %collective-permute-start.7 = (bf16[8,144,256]{2,1,0:T(8,128)(2,1)S(1)}, bf16[8,144,256]{2,1,0:T(8,128)(2,1)S(1)}, u32[]{:S(2)}, u32[]{:S(2)}) collective-permute-start(bf16[8,144,256]{2,1,0:T(8,128)(2,1)S(1)} %pad_maximum_fusion.2), channel_id=1, source_target_pairs={{0,96},{4,36},{8,104},{12,44},{16,112},{20,52},{24,120},{28,60},{3... | collective-permute-start | bytes 1769480 | tf_op jit(solution)/shard_map/ppermute | solution.py:25
  42.7 11.4 %collective-permute-start.12 = (bf16[16,144,256]{2,1,0:T(8,128)(2,1)S(1)}, bf16[16,144,256]{2,1,0:T(8,128)(2,1)S(1)}, u32[]{:S(2)}, u32[]{:S(2)}) collective-permute-start(bf16[16,144,256]{2,1,0:T(8,128)(2,1)S(1)} %pad_maximum_fusion.1), channel_id=1, source_target_pairs={{0,4},{4,0},{8,12},{12,8},{16,20},{20,16},{24,28},{28,24},{32,36},... | collective-permute-start | bytes 3538952 | tf_op jit(solution)/shard_map/ppermute | solution.py:25
  42.7 9.3 %collective-permute-start.13 = (bf16[2,128,1024]{2,1,0:T(8,128)(2,1)S(1)}, bf16[2,128,1024]{2,1,0:T(8,128)(2,1)S(1)}, u32[]{:S(2)}, u32[]{:S(2)}) collective-permute-start(bf16[2,128,1024]{2,1,0:T(8,128)(2,1)S(1)} %broadcast_select_fusion.12), channel_id=1, source_target_pairs={{0,8},{4,28},{8,0},{12,20},{16,24},{20,12},{24,16},{28,4},{32,40},... | collective-permute-start | bytes 1572872 | tf_op jit(solution)/shard_map/ppermute | solution.py:25
  43.4 11.0 %collective-permute-start.14 = (bf16[2,128,1024]{2,1,0:T(8,128)(2,1)}, bf16[2,128,1024]{2,1,0:T(8,128)(2,1)}, u32[]{:S(2)}, u32[]{:S(2)}) collective-permute-start(bf16[2,128,1024]{2,1,0:T(8,128)(2,1)} %broadcast_select_fusion.11), channel_id=1, source_target_pairs={{0,32},{4,100},{8,40},{12,108},{16,48},{20,116},{24,56},{28,124},{... | collective-permute-start | bytes 1572872 | tf_op jit(solution)/shard_map/ppermute | solution.py:25
  43.4 15.1 %collective-permute-start.17 = (bf16[256,1024]{1,0:T(8,128)(2,1)}, bf16[256,1024]{1,0:T(8,128)(2,1)}, u32[]{:S(2)}, u32[]{:S(2)}) collective-permute-start(bf16[256,1024]{1,0:T(8,128)(2,1)} %collective-permute-done.8.refs_2_), channel_id=1, source_target_pairs={{0,1},{1,2},{2,3},{3,0},{4,7},{5,4},{6,5},{7,6},{8,9},{9,10},{10,1... | collective-permute-start | bytes 1572872 | tf_op jit(solution)/shard_map/ppermute | solution.py:35
  44.0 18.7 %collective-permute-start.18 = (bf16[256,1024]{1,0:T(8,128)(2,1)S(1)}, bf16[256,1024]{1,0:T(8,128)(2,1)}, u32[]{:S(2)}, u32[]{:S(2)}) collective-permute-start(bf16[256,1024]{1,0:T(8,128)(2,1)S(1)} %bitcast.57), channel_id=1, source_target_pairs={{0,1},{1,2},{2,3},{3,0},{4,7},{5,4},{6,5},{7,6},{8,9},{9,10},{10,1... | collective-permute-start | bytes 1572872 | tf_op jit(solution)/shard_map/ppermute | solution.py:35
  52.9 10.7 %collective-permute-start.16 = (bf16[2,128,1024]{2,1,0:T(8,128)(2,1)}, bf16[2,128,1024]{2,1,0:T(8,128)(2,1)}, u32[]{:S(2)}, u32[]{:S(2)}) collective-permute-start(bf16[2,128,1024]{2,1,0:T(8,128)(2,1)} %broadcast_select_fusion.10), channel_id=1, source_target_pairs={{0,24},{4,12},{8,16},{12,4},{16,8},{20,28},{24,0},{28,20},{32,56},... | collective-permute-start | bytes 1572872 | tf_op jit(solution)/shard_map/ppermute | solution.py:25
  56.5 12.8 %collective-permute-start.15 = (bf16[2,128,1024]{2,1,0:T(8,128)(2,1)}, bf16[2,128,1024]{2,1,0:T(8,128)(2,1)}, u32[]{:S(2)}, u32[]{:S(2)}) collective-permute-start(bf16[2,128,1024]{2,1,0:T(8,128)(2,1)} %broadcast_select_fusion.7), channel_id=1, source_target_pairs={{0,96},{4,36},{8,104},{12,44},{16,112},{20,52},{24,120},{28,60},{3... | collective-permute-start | bytes 1572872 | tf_op jit(solution)/shard_map/ppermute | solution.py:25
  58.5 1.0 copy-start.1
  62.7 13.0 %collective-permute-start.21 = (bf16[2,128,1536]{2,1,0:T(8,128)(2,1)S(1)}, bf16[2,128,1536]{2,1,0:T(8,128)(2,1)S(1)}, u32[]{:S(2)}, u32[]{:S(2)}) collective-permute-start(bf16[2,128,1536]{2,1,0:T(8,128)(2,1)S(1)} %bitcast.51), channel_id=1, source_target_pairs={{0,32},{4,100},{8,40},{12,108},{16,48},{20,116},{24,56},{28,124},{... | collective-permute-start | bytes 2359304 | tf_op jit(solution)/shard_map/ppermute | solution.py:25
  63.6 10.6 %collective-permute-start.22 = (bf16[256,1024]{1,0:T(8,128)(2,1)}, bf16[256,1024]{1,0:T(8,128)(2,1)S(1)}, u32[]{:S(2)}, u32[]{:S(2)}) collective-permute-start(bf16[256,1024]{1,0:T(8,128)(2,1)} %collective-permute-done.18.refs_1_), channel_id=1, source_target_pairs={{0,1},{1,2},{2,3},{3,0},{4,7},{5,4},{6,5},{7,6},{8,9},{9,10},{10,1... | collective-permute-start | bytes 1572872 | tf_op jit(solution)/shard_map/ppermute | solution.py:35
  67.5 12.3 %collective-permute-start.20 = (bf16[256,1024]{1,0:T(8,128)(2,1)S(1)}, bf16[256,1024]{1,0:T(8,128)(2,1)S(1)}, u32[]{:S(2)}, u32[]{:S(2)}) collective-permute-start(bf16[256,1024]{1,0:T(8,128)(2,1)S(1)} %bitcast.59), channel_id=1, source_target_pairs={{0,1},{1,2},{2,3},{3,0},{4,7},{5,4},{6,5},{7,6},{8,9},{9,10},{10,1... | collective-permute-start | bytes 1572872 | tf_op jit(solution)/shard_map/ppermute | solution.py:35
  70.7 10.8 %collective-permute-start.19 = (bf16[2,128,1024]{2,1,0:T(8,128)(2,1)S(1)}, bf16[2,128,1024]{2,1,0:T(8,128)(2,1)S(1)}, u32[]{:S(2)}, u32[]{:S(2)}) collective-permute-start(bf16[2,128,1024]{2,1,0:T(8,128)(2,1)S(1)} %broadcast_select_fusion.8), channel_id=1, source_target_pairs={{0,24},{4,12},{8,16},{12,4},{16,8},{20,28},{24,0},{28,20},{32,56},... | collective-permute-start | bytes 1572872 | tf_op jit(solution)/shard_map/ppermute | solution.py:25
  74.2 11.2 %collective-permute-start.24 = (bf16[256,1024]{1,0:T(8,128)(2,1)S(1)}, bf16[256,1024]{1,0:T(8,128)(2,1)S(1)}, u32[]{:S(2)}, u32[]{:S(2)}) collective-permute-start(bf16[256,1024]{1,0:T(8,128)(2,1)S(1)} %collective-permute-done.22.refs_2_), channel_id=1, source_target_pairs={{0,1},{1,2},{2,3},{3,0},{4,7},{5,4},{6,5},{7,6},{8,9},{9,10},{10,1... | collective-permute-start | bytes 1572872 | tf_op jit(solution)/shard_map/ppermute | solution.py:35
  79.9 14.6 %collective-permute-start.25 = (bf16[2,128,1536]{2,1,0:T(8,128)(2,1)S(1)}, bf16[2,128,1536]{2,1,0:T(8,128)(2,1)S(1)}, u32[]{:S(2)}, u32[]{:S(2)}) collective-permute-start(bf16[2,128,1536]{2,1,0:T(8,128)(2,1)S(1)} %broadcast_select_fusion.5), channel_id=1, source_target_pairs={{0,96},{4,36},{8,104},{12,44},{16,112},{20,52},{24,120},{28,60},{3... | collective-permute-start | bytes 2359304 | tf_op jit(solution)/shard_map/ppermute | solution.py:25
  81.5 10.6 %collective-permute-start.23 = (bf16[256,1024]{1,0:T(8,128)(2,1)S(1)}, bf16[256,1024]{1,0:T(8,128)(2,1)S(1)}, u32[]{:S(2)}, u32[]{:S(2)}) collective-permute-start(bf16[256,1024]{1,0:T(8,128)(2,1)S(1)} %bitcast.61), channel_id=1, source_target_pairs={{0,1},{1,2},{2,3},{3,0},{4,7},{5,4},{6,5},{7,6},{8,9},{9,10},{10,1... | collective-permute-start | bytes 1572872 | tf_op jit(solution)/shard_map/ppermute | solution.py:35
  92.2 12.0 %collective-permute-start.27 = (bf16[2,128,1536]{2,1,0:T(8,128)(2,1)S(1)}, bf16[2,128,1536]{2,1,0:T(8,128)(2,1)S(1)}, u32[]{:S(2)}, u32[]{:S(2)}) collective-permute-start(bf16[2,128,1536]{2,1,0:T(8,128)(2,1)S(1)} %bitcast.53), channel_id=1, source_target_pairs={{0,32},{4,100},{8,40},{12,108},{16,48},{20,116},{24,56},{28,124},{... | collective-permute-start | bytes 2359304 | tf_op jit(solution)/shard_map/ppermute | solution.py:25
  93.8 10.4 %collective-permute-start.28 = (bf16[256,1024]{1,0:T(8,128)(2,1)S(1)}, bf16[256,1024]{1,0:T(8,128)(2,1)S(1)}, u32[]{:S(2)}, u32[]{:S(2)}) collective-permute-start(bf16[256,1024]{1,0:T(8,128)(2,1)S(1)} %collective-permute-done.20.refs_1_), channel_id=1, source_target_pairs={{0,1},{1,2},{2,3},{3,0},{4,7},{5,4},{6,5},{7,6},{8,9},{9,10},{10,1... | collective-permute-start | bytes 1572872 | tf_op jit(solution)/shard_map/ppermute | solution.py:35
  94.6 15.9 %collective-permute-start.31 = (bf16[2,128,1536]{2,1,0:T(8,128)(2,1)S(1)}, bf16[2,128,1536]{2,1,0:T(8,128)(2,1)S(1)}, u32[]{:S(2)}, u32[]{:S(2)}) collective-permute-start(bf16[2,128,1536]{2,1,0:T(8,128)(2,1)S(1)} %broadcast_select_fusion.4), channel_id=1, source_target_pairs={{0,8},{4,28},{8,0},{12,20},{16,24},{20,12},{24,16},{28,4},{32,40},... | collective-permute-start | bytes 2359304 | tf_op jit(solution)/shard_map/ppermute | solution.py:25
  94.7 15.2 %collective-permute-start.26 = (bf16[256,1024]{1,0:T(8,128)(2,1)S(1)}, bf16[256,1024]{1,0:T(8,128)(2,1)S(1)}, u32[]{:S(2)}, u32[]{:S(2)}) collective-permute-start(bf16[256,1024]{1,0:T(8,128)(2,1)S(1)} %collective-permute-done.23.refs_1_), channel_id=1, source_target_pairs={{0,1},{1,2},{2,3},{3,0},{4,7},{5,4},{6,5},{7,6},{8,9},{9,10},{10,1... | collective-permute-start | bytes 1572872 | tf_op jit(solution)/shard_map/ppermute | solution.py:35
  104.2 11.2 %collective-permute-start.30 = (bf16[256,1024]{1,0:T(8,128)(2,1)S(1)}, bf16[256,1024]{1,0:T(8,128)(2,1)S(1)}, u32[]{:S(2)}, u32[]{:S(2)}) collective-permute-start(bf16[256,1024]{1,0:T(8,128)(2,1)S(1)} %collective-permute-done.28.refs_2_), channel_id=1, source_target_pairs={{0,1},{1,2},{2,3},{3,0},{4,7},{5,4},{6,5},{7,6},{8,9},{9,10},{10,1... | collective-permute-start | bytes 1572872 | tf_op jit(solution)/shard_map/ppermute | solution.py:35
  109.8 11.2 %collective-permute-start.29 = (bf16[256,1024]{1,0:T(8,128)(2,1)S(1)}, bf16[256,1024]{1,0:T(8,128)(2,1)S(1)}, u32[]{:S(2)}, u32[]{:S(2)}) collective-permute-start(bf16[256,1024]{1,0:T(8,128)(2,1)S(1)} %collective-permute-done.26.refs_2_), channel_id=1, source_target_pairs={{0,1},{1,2},{2,3},{3,0},{4,7},{5,4},{6,5},{7,6},{8,9},{9,10},{10,1... | collective-permute-start | bytes 1572872 | tf_op jit(solution)/shard_map/ppermute | solution.py:35
  109.8 15.2 %collective-permute-start.33 = (bf16[2,128,1536]{2,1,0:T(8,128)(2,1)S(1)}, bf16[2,128,1536]{2,1,0:T(8,128)(2,1)S(1)}, u32[]{:S(2)}, u32[]{:S(2)}) collective-permute-start(bf16[2,128,1536]{2,1,0:T(8,128)(2,1)S(1)} %broadcast_select_fusion.3), channel_id=1, source_target_pairs={{0,96},{4,36},{8,104},{12,44},{16,112},{20,52},{24,120},{28,60},{3... | collective-permute-start | bytes 2359304 | tf_op jit(solution)/shard_map/ppermute | solution.py:25
  110.6 14.6 %collective-permute-start.32 = (bf16[2,128,1536]{2,1,0:T(8,128)(2,1)S(1)}, bf16[2,128,1536]{2,1,0:T(8,128)(2,1)S(1)}, u32[]{:S(2)}, u32[]{:S(2)}) collective-permute-start(bf16[2,128,1536]{2,1,0:T(8,128)(2,1)S(1)} %broadcast_select_fusion.2), channel_id=1, source_target_pairs={{0,24},{4,12},{8,16},{12,4},{16,8},{20,28},{24,0},{28,20},{32,56},... | collective-permute-start | bytes 2359304 | tf_op jit(solution)/shard_map/ppermute | solution.py:25

commit v5 on v4

--- a/solution.py
+++ b/solution.py
@@ -156,7 +156,7 @@
 PATHS = (
     (Y_A, Y_B, X_A, X_B),
     (X_A, X_B, Y_A, Y_B),
-    (X_A, Y_A, Y_B, X_B),
+    (X_A, Y_A, X_B, Y_B),
     (Y_A, Y_B, X_A, X_B),
 )
 
@@ -277,8 +277,8 @@
     moving[3].send()
     tiles.take()
     moving[2].take()
+    rings[0].take()
     moving[2].send()
-    rings[0].take()
     rings[1].take()
     moving[0] = onward(moving[0], rings[0].blocks)
     moving[0].send()
@@ -292,8 +292,8 @@
     rings[1].send()
     moving[0].take()
     moving[0].send()
+    moving[2].take()
     rings[3].take()
-    moving[2].take()
     rings[2] = ring(moving[2])
     rings[2].send()
     rings[3].send()

time: 128 us -> 127 us (level)
  starting transfers between devices: 39.6 us -> 36 us
  waiting for transfers between devices: 51.6 us -> 54.5 us
    ppermute x22, waiting for transfers between devices: 20.8 us -> 26.8 us  [exchange(): return lax.ppermute(value, 'row', pairs)]
    ppermute x12, starting transfers between devices: 14.3 us -> 10.3 us  [turn(): return lax.ppermute(value, AXES, pairs)]
    ppermute x12, waiting for transfers between devices: 30.9 us -> 27.7 us  [turn(): return lax.ppermute(value, AXES, pairs)]
  transfers between devices with their start and end apart: 34 -> 34, of which waited for: 16 -> 18; matrix products, arithmetic and copies ran while one was open for 12% -> 12% of each run, Pallas kernels for 13% -> 13%
where the time goes in v5:
time: 127 us
  waiting for transfers between devices  54.5 us (43%)
  starting transfers between devices  36 us (28%)
  Pallas kernels  16.5 us (13%)
  other arithmetic  14.8 us (12%)
  local copies, waits for them, and re-layouts  4.49 us (4%)
    ppermute x12, waiting for transfers between devices, turn(): return lax.ppermute(value, AXES, pairs)  27.7 us
    ppermute x22, waiting for transfers between devices, exchange(): return lax.ppermute(value, 'row', pairs)  26.8 us
    ppermute x22, starting transfers between devices, exchange(): return lax.ppermute(value, 'row', pairs)  25.8 us
    pallas_call x4, Pallas kernels, product(): pl.pallas_call(functools.partial(product_kernel, first), grid_spec=pltpu....  14.6 us
    select_n x20, other arithmetic, choose(): return jnp.where(taken[:, None, None], partner, mine)  13 us
    ppermute x12, starting transfers between devices, turn(): return lax.ppermute(value, AXES, pairs)  10.3 us
  transfers between devices with their start and end apart: 34, of which 18 were waited for; matrix products, arithmetic and copies ran while one was open for 12% of the time, Pallas kernels for 13%

profile of v5, /device:TPU:0, one launch (start us, length us, event | category | flops | bytes accessed | tf_op | source)
XLA Modules:
  0.0 126.5 jit_solution(6116722149057352012)
XLA Ops:
  0.0 1.8 %shard_map.73 = bf16[1,144,256]{2,1,0:T(8,128)(2,1)} custom-call(s32[1,12]{1,0:T(1,128)} %screen_ref.1, bf16[128,1536]{1,0:T(8,128)(2,1)} %amplitudes_ref.1), custom_call_target="tpu_custom_call" | custom-call | flops 1 | bytes 1 | tf_op jit(solution)/shard_map/pallas_call | solution.py:59
  1.8 1.6 %collective-permute-start = (bf16[1,144,256]{2,1,0:T(8,128)(2,1)}, bf16[1,144,256]{2,1,0:T(8,128)(2,1)S(1)}, u32[]{:S(2)}, u32[]{:S(2)}) collective-permute-start(bf16[1,144,256]{2,1,0:T(8,128)(2,1)} %shard_map.73), channel_id=1, source_target_pairs={{0,8},{4,28},{8,0},{12,20},{16,24},{20,12},{24,16},{28,4},{32,40},... | collective-permute-start | bytes 221192 | tf_op jit(solution)/shard_map/ppermute | solution.py:25
  5.6 1.3 %slice_select_fusion.3 = bf16[2,128,1024]{2,1,0:T(8,128)(2,1)S(1)} fusion(bf16[8,128,1024]{2,1,0:T(8,128)(2,1)} %bitcast.66, bf16[8,128,1024]{2,1,0:T(8,128)(2,1)} %collective-permute-done.1, pred[2]{0:T(512)(128)(4,1)S(1)} %get-tuple-element.279), kind=kLoop, calls=%fused_computation.12 | loop fusion | flops 262144 | bytes 1572866 | tf_op jit(solution)/shard_map/jit(_where)/select_n | solution.py:40
  7.0 1.2 slice_select_fusion.2
  8.2 1.2 slice_select_fusion.1
  9.4 2.0 %collective-permute-start.3 = (bf16[256,1024]{1,0:T(8,128)(2,1)S(1)}, bf16[256,1024]{1,0:T(8,128)(2,1)S(1)}, u32[]{:S(2)}, u32[]{:S(2)}) collective-permute-start(bf16[256,1024]{1,0:T(8,128)(2,1)S(1)} %bitcast.55), channel_id=1, source_target_pairs={{0,1},{1,2},{2,3},{3,0},{4,7},{5,4},{6,5},{7,6},{8,9},{9,10},{10,1... | collective-permute-start | bytes 1572872 | tf_op jit(solution)/shard_map/ppermute | solution.py:35
  11.4 1.6 %collective-permute-start.6 = (bf16[2,128,1024]{2,1,0:T(8,128)(2,1)S(1)}, bf16[2,128,1024]{2,1,0:T(8,128)(2,1)S(1)}, u32[]{:S(2)}, u32[]{:S(2)}) collective-permute-start(bf16[2,128,1024]{2,1,0:T(8,128)(2,1)S(1)} %slice_select_fusion.3), channel_id=1, source_target_pairs={{0,32},{4,100},{8,40},{12,108},{16,48},{20,116},{24,56},{28,124},{... | collective-permute-start | bytes 1572872 | tf_op jit(solution)/shard_map/ppermute | solution.py:25
  13.0 2.1 %collective-permute-start.2 = (bf16[2,144,256]{2,1,0:T(8,128)(2,1)S(1)}, bf16[2,144,256]{2,1,0:T(8,128)(2,1)S(1)}, u32[]{:S(2)}, u32[]{:S(2)}) collective-permute-start(bf16[2,144,256]{2,1,0:T(8,128)(2,1)S(1)} %pad_maximum_fusion.4), channel_id=1, source_target_pairs={{0,24},{4,12},{8,16},{12,4},{16,8},{20,28},{24,0},{28,20},{32,56},... | collective-permute-start | bytes 442376 | tf_op jit(solution)/shard_map/ppermute | solution.py:25
  15.7 1.2 slice_select_fusion
  16.9 1.5 %collective-permute-start.11 = (bf16[2,128,1024]{2,1,0:T(8,128)(2,1)S(1)}, bf16[2,128,1024]{2,1,0:T(8,128)(2,1)S(1)}, u32[]{:S(2)}, u32[]{:S(2)}) collective-permute-start(bf16[2,128,1024]{2,1,0:T(8,128)(2,1)S(1)} %slice_select_fusion), channel_id=1, source_target_pairs={{0,8},{4,28},{8,0},{12,20},{16,24},{20,12},{24,16},{28,4},{32,40},... | collective-permute-start | bytes 1572872 | tf_op jit(solution)/shard_map/ppermute | solution.py:25
  18.4 2.3 %collective-permute-done.3.refs_1_ = bf16[256,1024]{1,0:T(8,128)(2,1)S(1)} collective-permute-done((bf16[256,1024]{1,0:T(8,128)(2,1)S(1)}, bf16[256,1024]{1,0:T(8,128)(2,1)S(1)}, u32[]{:S(2)}, u32[]{:S(2)}) %collective-permute-start.3) | collective-permute-done | bytes 524320 | tf_op jit(solution)/shard_map/ppermute | solution.py:35
  20.7 1.7 %collective-permute-start.4 = (bf16[4,144,256]{2,1,0:T(8,128)(2,1)S(1)}, bf16[4,144,256]{2,1,0:T(8,128)(2,1)S(1)}, u32[]{:S(2)}, u32[]{:S(2)}) collective-permute-start(bf16[4,144,256]{2,1,0:T(8,128)(2,1)S(1)} %pad_maximum_fusion.3), channel_id=1, source_target_pairs={{0,32},{4,100},{8,40},{12,108},{16,48},{20,116},{24,56},{28,124},{... | collective-permute-start | bytes 884744 | tf_op jit(solution)/shard_map/ppermute | solution.py:25
  22.5 3.3 %collective-permute-done.5 = bf16[2,128,1024]{2,1,0:T(8,128)(2,1)S(1)} collective-permute-done((bf16[2,128,1024]{2,1,0:T(8,128)(2,1)S(1)}, bf16[2,128,1024]{2,1,0:T(8,128)(2,1)S(1)}, u32[]{:S(2)}, u32[]{:S(2)}) %collective-permute-start.5) | collective-permute-done | bytes 524320 | tf_op jit(solution)/shard_map/ppermute | solution.py:25
  25.8 1.6 %collective-permute-start.10 = (bf16[2,128,1024]{2,1,0:T(8,128)(2,1)S(1)}, bf16[2,128,1024]{2,1,0:T(8,128)(2,1)S(1)}, u32[]{:S(2)}, u32[]{:S(2)}) collective-permute-start(bf16[2,128,1024]{2,1,0:T(8,128)(2,1)S(1)} %broadcast_select_fusion.14), channel_id=1, source_target_pairs={{0,96},{4,36},{8,104},{12,44},{16,112},{20,52},{24,120},{28,60},{3... | collective-permute-start | bytes 1572872 | tf_op jit(solution)/shard_map/ppermute | solution.py:25
  28.5 1.1 collective-permute-start.9
  29.8 1.7 %collective-permute-start.7 = (bf16[8,144,256]{2,1,0:T(8,128)(2,1)S(1)}, bf16[8,144,256]{2,1,0:T(8,128)(2,1)S(1)}, u32[]{:S(2)}, u32[]{:S(2)}) collective-permute-start(bf16[8,144,256]{2,1,0:T(8,128)(2,1)S(1)} %pad_maximum_fusion.2), channel_id=1, source_target_pairs={{0,96},{4,36},{8,104},{12,44},{16,112},{20,52},{24,120},{28,60},{3... | collective-permute-start | bytes 1769480 | tf_op jit(solution)/shard_map/ppermute | solution.py:25
  31.5 1.6 %collective-permute-done.11 = bf16[2,128,1024]{2,1,0:T(8,128)(2,1)S(1)} collective-permute-done((bf16[2,128,1024]{2,1,0:T(8,128)(2,1)S(1)}, bf16[2,128,1024]{2,1,0:T(8,128)(2,1)S(1)}, u32[]{:S(2)}, u32[]{:S(2)}) %collective-permute-start.11) | collective-permute-done | bytes 524320 | tf_op jit(solution)/shard_map/ppermute | solution.py:25
  34.1 2.2 %collective-permute-done.10 = bf16[2,128,1024]{2,1,0:T(8,128)(2,1)S(1)} collective-permute-done((bf16[2,128,1024]{2,1,0:T(8,128)(2,1)S(1)}, bf16[2,128,1024]{2,1,0:T(8,128)(2,1)S(1)}, u32[]{:S(2)}, u32[]{:S(2)}) %collective-permute-start.10) | collective-permute-done | bytes 524320 | tf_op jit(solution)/shard_map/ppermute | solution.py:25
  36.3 2.6 %collective-permute-done.9 = bf16[2,128,1024]{2,1,0:T(8,128)(2,1)S(1)} collective-permute-done((bf16[2,128,1024]{2,1,0:T(8,128)(2,1)S(1)}, bf16[2,128,1024]{2,1,0:T(8,128)(2,1)S(1)}, u32[]{:S(2)}, u32[]{:S(2)}) %collective-permute-start.9) | collective-permute-done | bytes 524320 | tf_op jit(solution)/shard_map/ppermute | solution.py:25
  39.1 3.5 %collective-permute-done.7 = bf16[8,144,256]{2,1,0:T(8,128)(2,1)S(1)} collective-permute-done((bf16[8,144,256]{2,1,0:T(8,128)(2,1)S(1)}, bf16[8,144,256]{2,1,0:T(8,128)(2,1)S(1)}, u32[]{:S(2)}, u32[]{:S(2)}) %collective-permute-start.7) | collective-permute-done | bytes 589856 | tf_op jit(solution)/shard_map/ppermute | solution.py:25
  44.0 1.4 %collective-permute-start.18 = (bf16[256,1024]{1,0:T(8,128)(2,1)S(1)}, bf16[256,1024]{1,0:T(8,128)(2,1)}, u32[]{:S(2)}, u32[]{:S(2)}) collective-permute-start(bf16[256,1024]{1,0:T(8,128)(2,1)S(1)} %bitcast.57), channel_id=1, source_target_pairs={{0,1},{1,2},{2,3},{3,0},{4,7},{5,4},{6,5},{7,6},{8,9},{9,10},{10,1... | collective-permute-start | bytes 1572872 | tf_op jit(solution)/shard_map/ppermute | solution.py:35
  45.4 6.6 %collective-permute-done.13 = bf16[2,128,1024]{2,1,0:T(8,128)(2,1)S(1)} collective-permute-done((bf16[2,128,1024]{2,1,0:T(8,128)(2,1)S(1)}, bf16[2,128,1024]{2,1,0:T(8,128)(2,1)S(1)}, u32[]{:S(2)}, u32[]{:S(2)}) %collective-permute-start.13) | collective-permute-done | bytes 524320 | tf_op jit(solution)/shard_map/ppermute | solution.py:25
  52.9 1.1 collective-permute-start.17
  54.4 2.1 %broadcast_select_fusion.7 = bf16[2,128,1024]{2,1,0:T(8,128)(2,1)} fusion(bf16[2,128,1024]{2,1,0:T(8,128)(2,1)} %collective-permute-done.14, bf16[2,128,1024]{2,1,0:T(8,128)(2,1)} %broadcast_select_fusion.11, pred[2]{0:T(512)(128)(4,1)S(1)} %get-tuple-element.268), kind=kLoop, calls=%fused_computation.14 | loop fusion | flops 262144 | bytes 1572866 | tf_op jit(solution)/shard_map/jit(_where)/select_n | solution.py:40
  56.5 2.1 %collective-permute-start.16 = (bf16[2,128,1024]{2,1,0:T(8,128)(2,1)}, bf16[2,128,1024]{2,1,0:T(8,128)(2,1)}, u32[]{:S(2)}, u32[]{:S(2)}) collective-permute-start(bf16[2,128,1024]{2,1,0:T(8,128)(2,1)} %broadcast_select_fusion.7), channel_id=1, source_target_pairs={{0,24},{4,12},{8,16},{12,4},{16,8},{20,28},{24,0},{28,20},{32,56},... | collective-permute-start | bytes 1572872 | tf_op jit(solution)/shard_map/ppermute | solution.py:25
  59.4 1.0 copy-done.1
  60.4 3.1 %shard_map.74 = bf16[256,1536]{1,0:T(8,128)(2,1)S(1)} custom-call(s32[1,32]{1,0:T(1,128)S(1)} %constant_dynamic-slice_fusion.at_ref, s32[64]{0:T(128)S(1)} %reshape.184.place_ref, s32[4]{0:T(128)S(1)} %subtract_and_fusion.base_ref, bf16[256,1024]{1,0:T(8,128)(2,1)S(1)} %bitcast.56, bf16[256,1024]{1,0:T(8,128)(2,1)S(1)} %copy-done.1, ...), custom_call_target="tpu_custom_call" | custom-call | flops 1 | bytes 1 | tf_op jit(solution)/shard_map/pallas_call | solution.py:118
  64.6 1.3 %broadcast_select_fusion.6 = bf16[2,128,1024]{2,1,0:T(8,128)(2,1)S(1)} fusion(bf16[2,128,1024]{2,1,0:T(8,128)(2,1)} %collective-permute-done.17, bf16[2,128,1024]{2,1,0:T(8,128)(2,1)} %broadcast_select_fusion.10, pred[2]{0:T(512)(128)(4,1)S(1)} %get-tuple-element.267), kind=kLoop, calls=%fused_computation.13 | loop fusion | flops 262144 | bytes 1572866 | tf_op jit(solution)/shard_map/jit(_where)/select_n | solution.py:40
  66.0 1.5 %collective-permute-start.22 = (bf16[256,1024]{1,0:T(8,128)(2,1)S(1)}, bf16[256,1024]{1,0:T(8,128)(2,1)S(1)}, u32[]{:S(2)}, u32[]{:S(2)}) collective-permute-start(bf16[256,1024]{1,0:T(8,128)(2,1)S(1)} %bitcast.59), channel_id=1, source_target_pairs={{0,1},{1,2},{2,3},{3,0},{4,7},{5,4},{6,5},{7,6},{8,9},{9,10},{10,1... | collective-permute-start | bytes 1572872 | tf_op jit(solution)/shard_map/ppermute | solution.py:35
  67.4 1.8 %collective-permute-done.16 = bf16[2,128,1024]{2,1,0:T(8,128)(2,1)} collective-permute-done((bf16[2,128,1024]{2,1,0:T(8,128)(2,1)}, bf16[2,128,1024]{2,1,0:T(8,128)(2,1)}, u32[]{:S(2)}, u32[]{:S(2)}) %collective-permute-start.16) | collective-permute-done | bytes 524320 | tf_op jit(solution)/shard_map/ppermute | solution.py:25
  69.3 1.3 %broadcast_select_fusion.8 = bf16[2,128,1024]{2,1,0:T(8,128)(2,1)S(1)} fusion(bf16[2,128,1024]{2,1,0:T(8,128)(2,1)} %collective-permute-done.16, bf16[2,128,1024]{2,1,0:T(8,128)(2,1)} %broadcast_select_fusion.7, pred[2]{0:T(512)(128)(4,1)S(1)} %get-tuple-element.269), kind=kLoop, calls=%fused_computation.15 | loop fusion | flops 262144 | bytes 1572866 | tf_op jit(solution)/shard_map/jit(_where)/select_n | solution.py:40
  70.6 1.6 %collective-permute-start.19 = (bf16[2,128,1024]{2,1,0:T(8,128)(2,1)S(1)}, bf16[2,128,1024]{2,1,0:T(8,128)(2,1)S(1)}, u32[]{:S(2)}, u32[]{:S(2)}) collective-permute-start(bf16[2,128,1024]{2,1,0:T(8,128)(2,1)S(1)} %broadcast_select_fusion.8), channel_id=1, source_target_pairs={{0,96},{4,36},{8,104},{12,44},{16,112},{20,52},{24,120},{28,60},{3... | collective-permute-start | bytes 1572872 | tf_op jit(solution)/shard_map/ppermute | solution.py:25
  72.2 2.1 %collective-permute-done.21.refs_2_ = bf16[256,1024]{1,0:T(8,128)(2,1)S(1)} collective-permute-done((bf16[256,1024]{1,0:T(8,128)(2,1)}, bf16[256,1024]{1,0:T(8,128)(2,1)S(1)}, u32[]{:S(2)}, u32[]{:S(2)}) %collective-permute-start.21) | collective-permute-done | bytes 524320 | tf_op jit(solution)/shard_map/ppermute | solution.py:35
  74.3 4.6 %collective-permute-done.20 = bf16[2,128,1536]{2,1,0:T(8,128)(2,1)S(1)} collective-permute-done((bf16[2,128,1536]{2,1,0:T(8,128)(2,1)S(1)}, bf16[2,128,1536]{2,1,0:T(8,128)(2,1)S(1)}, u32[]{:S(2)}, u32[]{:S(2)}) %collective-permute-start.20) | collective-permute-done | bytes 786464 | tf_op jit(solution)/shard_map/ppermute | solution.py:25
  79.0 1.8 %collective-permute-start.25 = (bf16[2,128,1536]{2,1,0:T(8,128)(2,1)S(1)}, bf16[2,128,1536]{2,1,0:T(8,128)(2,1)S(1)}, u32[]{:S(2)}, u32[]{:S(2)}) collective-permute-start(bf16[2,128,1536]{2,1,0:T(8,128)(2,1)S(1)} %broadcast_select_fusion.5), channel_id=1, source_target_pairs={{0,96},{4,36},{8,104},{12,44},{16,112},{20,52},{24,120},{28,60},{3... | collective-permute-start | bytes 2359304 | tf_op jit(solution)/shard_map/ppermute | solution.py:25
  81.2 2.0 %collective-permute-start.23 = (bf16[256,1024]{1,0:T(8,128)(2,1)S(1)}, bf16[256,1024]{1,0:T(8,128)(2,1)S(1)}, u32[]{:S(2)}, u32[]{:S(2)}) collective-permute-start(bf16[256,1024]{1,0:T(8,128)(2,1)S(1)} %bitcast.61), channel_id=1, source_target_pairs={{0,1},{1,2},{2,3},{3,0},{4,7},{5,4},{6,5},{7,6},{8,9},{9,10},{10,1... | collective-permute-start | bytes 1572872 | tf_op jit(solution)/shard_map/ppermute | solution.py:35
  83.2 2.4 %collective-permute-done.24.refs_3_ = bf16[256,1024]{1,0:T(8,128)(2,1)S(1)} collective-permute-done((bf16[256,1024]{1,0:T(8,128)(2,1)S(1)}, bf16[256,1024]{1,0:T(8,128)(2,1)S(1)}, u32[]{:S(2)}, u32[]{:S(2)}) %collective-permute-start.24) | collective-permute-done | bytes 524320 | tf_op jit(solution)/shard_map/ppermute | solution.py:35
  85.5 3.5 %shard_map.75 = bf16[256,1536]{1,0:T(8,128)(2,1)S(1)} custom-call(s32[1,32]{1,0:T(1,128)S(1)} %constant_dynamic-slice_fusion.at_ref, s32[64]{0:T(128)S(1)} %reshape.184.place_ref, s32[4]{0:T(128)S(1)} %subtract_and_fusion.base_ref, bf16[256,1024]{1,0:T(8,128)(2,1)S(1)} %bitcast.58, bf16[256,1024]{1,0:T(8,128)(2,1)} %collective-permute-done.18.refs_1_, ...), custom_call_target="tpu_custom_call" | custom-call | flops 1 | bytes 1 | tf_op jit(solution)/shard_map/pallas_call | solution.py:118
  89.0 2.8 %collective-permute-done.23.refs_1_ = bf16[256,1024]{1,0:T(8,128)(2,1)S(1)} collective-permute-done((bf16[256,1024]{1,0:T(8,128)(2,1)S(1)}, bf16[256,1024]{1,0:T(8,128)(2,1)S(1)}, u32[]{:S(2)}, u32[]{:S(2)}) %collective-permute-start.23) | collective-permute-done | bytes 524320 | tf_op jit(solution)/shard_map/ppermute | solution.py:35
  91.8 1.3 collective-permute-start.27
  94.2 9.3 %collective-permute-done.28.refs_2_ = bf16[256,1024]{1,0:T(8,128)(2,1)S(1)} collective-permute-done((bf16[256,1024]{1,0:T(8,128)(2,1)S(1)}, bf16[256,1024]{1,0:T(8,128)(2,1)S(1)}, u32[]{:S(2)}, u32[]{:S(2)}) %collective-permute-start.28) | collective-permute-done | bytes 524320 | tf_op jit(solution)/shard_map/ppermute | solution.py:35
  104.0 5.1 %collective-permute-done.26.refs_2_ = bf16[256,1024]{1,0:T(8,128)(2,1)S(1)} collective-permute-done((bf16[256,1024]{1,0:T(8,128)(2,1)S(1)}, bf16[256,1024]{1,0:T(8,128)(2,1)S(1)}, u32[]{:S(2)}, u32[]{:S(2)}) %collective-permute-start.26) | collective-permute-done | bytes 524320 | tf_op jit(solution)/shard_map/ppermute | solution.py:35
  109.1 1.6 %collective-permute-start.33 = (bf16[2,128,1536]{2,1,0:T(8,128)(2,1)S(1)}, bf16[2,128,1536]{2,1,0:T(8,128)(2,1)S(1)}, u32[]{:S(2)}, u32[]{:S(2)}) collective-permute-start(bf16[2,128,1536]{2,1,0:T(8,128)(2,1)S(1)} %broadcast_select_fusion.3), channel_id=1, source_target_pairs={{0,96},{4,36},{8,104},{12,44},{16,112},{20,52},{24,120},{28,60},{3... | collective-permute-start | bytes 2359304 | tf_op jit(solution)/shard_map/ppermute | solution.py:25
  110.8 1.8 %collective-permute-start.32 = (bf16[2,128,1536]{2,1,0:T(8,128)(2,1)S(1)}, bf16[2,128,1536]{2,1,0:T(8,128)(2,1)S(1)}, u32[]{:S(2)}, u32[]{:S(2)}) collective-permute-start(bf16[2,128,1536]{2,1,0:T(8,128)(2,1)S(1)} %broadcast_select_fusion.2), channel_id=1, source_target_pairs={{0,24},{4,12},{8,16},{12,4},{16,8},{20,28},{24,0},{28,20},{32,56},... | collective-permute-start | bytes 2359304 | tf_op jit(solution)/shard_map/ppermute | solution.py:25
  112.7 2.1 %collective-permute-done.30.refs_3_ = bf16[256,1024]{1,0:T(8,128)(2,1)S(1)} collective-permute-done((bf16[256,1024]{1,0:T(8,128)(2,1)S(1)}, bf16[256,1024]{1,0:T(8,128)(2,1)S(1)}, u32[]{:S(2)}, u32[]{:S(2)}) %collective-permute-start.30) | collective-permute-done | bytes 524320 | tf_op jit(solution)/shard_map/ppermute | solution.py:35
  114.7 4.0 %shard_map.76.refs_5_ = bf16[1024,1536]{1,0:T(8,128)(2,1)} custom-call(s32[1,32]{1,0:T(1,128)S(1)} %constant_dynamic-slice_fusion.at_ref, s32[64]{0:T(128)S(1)} %reshape.184.place_ref, s32[4]{0:T(128)S(1)} %subtract_and_fusion.base_ref, bf16[256,1024]{1,0:T(8,128)(2,1)S(1)} %bitcast.60, bf16[256,1024]{1,0:T(8,128)(2,1)S(1)} %collective-permute-done.22.refs_1_, ...), custom_call_target="tpu_custom_call" | custom-call | flops 1 | bytes 1 | tf_op jit(solution)/shard_map/pallas_call | solution.py:118
  118.7 1.6 %collective-permute-done.29.refs_3_ = bf16[256,1024]{1,0:T(8,128)(2,1)S(1)} collective-permute-done((bf16[256,1024]{1,0:T(8,128)(2,1)S(1)}, bf16[256,1024]{1,0:T(8,128)(2,1)S(1)}, u32[]{:S(2)}, u32[]{:S(2)}) %collective-permute-start.29) | collective-permute-done | bytes 524320 | tf_op jit(solution)/shard_map/ppermute | solution.py:35
  120.3 4.0 %shard_map.77 = bf16[1024,1536]{1,0:T(8,128)(2,1)} custom-call(s32[1,32]{1,0:T(1,128)S(1)} %constant_dynamic-slice_fusion.at_ref, s32[64]{0:T(128)S(1)} %reshape.184.place_ref, s32[4]{0:T(128)S(1)} %subtract_and_fusion.base_ref, bf16[256,1024]{1,0:T(8,128)(2,1)S(1)} %bitcast.62, ...), custom_call_target="tpu_custom_call", output_to_operand_aliasing={{}: (8, {})} | custom-call | flops 1 | bytes 1 | tf_op jit(solution)/shard_map/pallas_call | solution.py:118
  (71 shorter events, 14.1 us)
Async XLA Ops:
  0.0 7.0 %copy-start.2 = (bf16[1024,1024]{1,0:T(8,128)(2,1)S(1)}, bf16[1024,1024]{1,0:T(8,128)(2,1)}, u32[]{:S(2)}) copy-start(bf16[1024,1024]{1,0:T(8,128)(2,1)} %param.7) | copy-start | bytes 6291460
  0.0 5.6 %collective-permute-start.1 = (bf16[8,128,1024]{2,1,0:T(8,128)(2,1)}, bf16[8,128,1024]{2,1,0:T(8,128)(2,1)}, u32[]{:S(2)}, u32[]{:S(2)}) collective-permute-start(bf16[8,128,1024]{2,1,0:T(8,128)(2,1)} %bitcast.65), channel_id=1, source_target_pairs={{0,4},{4,0},{8,12},{12,8},{16,20},{20,16},{24,28},{28,24},{32,36},... | collective-permute-start | bytes 6291464 | tf_op jit(solution)/shard_map/ppermute | solution.py:25
  1.8 6.3 %copy-start.3 = (bf16[1,144,256]{2,1,0:T(8,128)(2,1)S(1)}, bf16[1,144,256]{2,1,0:T(8,128)(2,1)}, u32[]{:S(2)}) copy-start(bf16[1,144,256]{2,1,0:T(8,128)(2,1)} %shard_map.73) | copy-start | bytes 221188
  1.8 6.3 %collective-permute-start = (bf16[1,144,256]{2,1,0:T(8,128)(2,1)}, bf16[1,144,256]{2,1,0:T(8,128)(2,1)S(1)}, u32[]{:S(2)}, u32[]{:S(2)}) collective-permute-start(bf16[1,144,256]{2,1,0:T(8,128)(2,1)} %shard_map.73), channel_id=1, source_target_pairs={{0,8},{4,28},{8,0},{12,20},{16,24},{20,12},{24,16},{28,4},{32,40},... | collective-permute-start | bytes 221192 | tf_op jit(solution)/shard_map/ppermute | solution.py:25
  9.4 11.3 %collective-permute-start.3 = (bf16[256,1024]{1,0:T(8,128)(2,1)S(1)}, bf16[256,1024]{1,0:T(8,128)(2,1)S(1)}, u32[]{:S(2)}, u32[]{:S(2)}) collective-permute-start(bf16[256,1024]{1,0:T(8,128)(2,1)S(1)} %bitcast.55), channel_id=1, source_target_pairs={{0,1},{1,2},{2,3},{3,0},{4,7},{5,4},{6,5},{7,6},{8,9},{9,10},{10,1... | collective-permute-start | bytes 1572872 | tf_op jit(solution)/shard_map/ppermute | solution.py:35
  11.4 11.0 %collective-permute-start.6 = (bf16[2,128,1024]{2,1,0:T(8,128)(2,1)S(1)}, bf16[2,128,1024]{2,1,0:T(8,128)(2,1)S(1)}, u32[]{:S(2)}, u32[]{:S(2)}) collective-permute-start(bf16[2,128,1024]{2,1,0:T(8,128)(2,1)S(1)} %slice_select_fusion.3), channel_id=1, source_target_pairs={{0,32},{4,100},{8,40},{12,108},{16,48},{20,116},{24,56},{28,124},{... | collective-permute-start | bytes 1572872 | tf_op jit(solution)/shard_map/ppermute | solution.py:25
  13.0 7.7 %collective-permute-start.2 = (bf16[2,144,256]{2,1,0:T(8,128)(2,1)S(1)}, bf16[2,144,256]{2,1,0:T(8,128)(2,1)S(1)}, u32[]{:S(2)}, u32[]{:S(2)}) collective-permute-start(bf16[2,144,256]{2,1,0:T(8,128)(2,1)S(1)} %pad_maximum_fusion.4), channel_id=1, source_target_pairs={{0,24},{4,12},{8,16},{12,4},{16,8},{20,28},{24,0},{28,20},{32,56},... | collective-permute-start | bytes 442376 | tf_op jit(solution)/shard_map/ppermute | solution.py:25
  15.1 10.8 %collective-permute-start.5 = (bf16[2,128,1024]{2,1,0:T(8,128)(2,1)S(1)}, bf16[2,128,1024]{2,1,0:T(8,128)(2,1)S(1)}, u32[]{:S(2)}, u32[]{:S(2)}) collective-permute-start(bf16[2,128,1024]{2,1,0:T(8,128)(2,1)S(1)} %slice_select_fusion.1), channel_id=1, source_target_pairs={{0,8},{4,28},{8,0},{12,20},{16,24},{20,12},{24,16},{28,4},{32,40},... | collective-permute-start | bytes 1572872 | tf_op jit(solution)/shard_map/ppermute | solution.py:25
  16.9 16.3 %collective-permute-start.11 = (bf16[2,128,1024]{2,1,0:T(8,128)(2,1)S(1)}, bf16[2,128,1024]{2,1,0:T(8,128)(2,1)S(1)}, u32[]{:S(2)}, u32[]{:S(2)}) collective-permute-start(bf16[2,128,1024]{2,1,0:T(8,128)(2,1)S(1)} %slice_select_fusion), channel_id=1, source_target_pairs={{0,8},{4,28},{8,0},{12,20},{16,24},{20,12},{24,16},{28,4},{32,40},... | collective-permute-start | bytes 1572872 | tf_op jit(solution)/shard_map/ppermute | solution.py:25
  20.7 9.1 %copy-start = (bf16[256,1024]{1,0:T(8,128)(2,1)}, bf16[256,1024]{1,0:T(8,128)(2,1)S(1)}, u32[]{:S(2)}) copy-start(bf16[256,1024]{1,0:T(8,128)(2,1)S(1)} %collective-permute-done.3.refs_1_) | copy-start | bytes 1572868
  20.7 9.0 %collective-permute-start.4 = (bf16[4,144,256]{2,1,0:T(8,128)(2,1)S(1)}, bf16[4,144,256]{2,1,0:T(8,128)(2,1)S(1)}, u32[]{:S(2)}, u32[]{:S(2)}) collective-permute-start(bf16[4,144,256]{2,1,0:T(8,128)(2,1)S(1)} %pad_maximum_fusion.3), channel_id=1, source_target_pairs={{0,32},{4,100},{8,40},{12,108},{16,48},{20,116},{24,56},{28,124},{... | collective-permute-start | bytes 884744 | tf_op jit(solution)/shard_map/ppermute | solution.py:25
  25.8 10.4 %collective-permute-start.10 = (bf16[2,128,1024]{2,1,0:T(8,128)(2,1)S(1)}, bf16[2,128,1024]{2,1,0:T(8,128)(2,1)S(1)}, u32[]{:S(2)}, u32[]{:S(2)}) collective-permute-start(bf16[2,128,1024]{2,1,0:T(8,128)(2,1)S(1)} %broadcast_select_fusion.14), channel_id=1, source_target_pairs={{0,96},{4,36},{8,104},{12,44},{16,112},{20,52},{24,120},{28,60},{3... | collective-permute-start | bytes 1572872 | tf_op jit(solution)/shard_map/ppermute | solution.py:25
  27.5 11.5 %collective-permute-start.8 = (bf16[256,1024]{1,0:T(8,128)(2,1)S(1)}, bf16[256,1024]{1,0:T(8,128)(2,1)}, u32[]{:S(2)}, u32[]{:S(2)}) collective-permute-start(bf16[256,1024]{1,0:T(8,128)(2,1)S(1)} %collective-permute-done.3.refs_1_), channel_id=1, source_target_pairs={{0,1},{1,2},{2,3},{3,0},{4,7},{5,4},{6,5},{7,6},{8,9},{9,10},{10,1... | collective-permute-start | bytes 1572872 | tf_op jit(solution)/shard_map/ppermute | solution.py:35
  28.5 10.4 %collective-permute-start.9 = (bf16[2,128,1024]{2,1,0:T(8,128)(2,1)S(1)}, bf16[2,128,1024]{2,1,0:T(8,128)(2,1)S(1)}, u32[]{:S(2)}, u32[]{:S(2)}) collective-permute-start(bf16[2,128,1024]{2,1,0:T(8,128)(2,1)S(1)} %broadcast_select_fusion.15), channel_id=1, source_target_pairs={{0,24},{4,12},{8,16},{12,4},{16,8},{20,28},{24,0},{28,20},{32,56},... | collective-permute-start | bytes 1572872 | tf_op jit(solution)/shard_map/ppermute | solution.py:25
  29.8 12.8 %collective-permute-start.7 = (bf16[8,144,256]{2,1,0:T(8,128)(2,1)S(1)}, bf16[8,144,256]{2,1,0:T(8,128)(2,1)S(1)}, u32[]{:S(2)}, u32[]{:S(2)}) collective-permute-start(bf16[8,144,256]{2,1,0:T(8,128)(2,1)S(1)} %pad_maximum_fusion.2), channel_id=1, source_target_pairs={{0,96},{4,36},{8,104},{12,44},{16,112},{20,52},{24,120},{28,60},{3... | collective-permute-start | bytes 1769480 | tf_op jit(solution)/shard_map/ppermute | solution.py:25
  42.7 11.4 %collective-permute-start.12 = (bf16[16,144,256]{2,1,0:T(8,128)(2,1)S(1)}, bf16[16,144,256]{2,1,0:T(8,128)(2,1)S(1)}, u32[]{:S(2)}, u32[]{:S(2)}) collective-permute-start(bf16[16,144,256]{2,1,0:T(8,128)(2,1)S(1)} %pad_maximum_fusion.1), channel_id=1, source_target_pairs={{0,4},{4,0},{8,12},{12,8},{16,20},{20,16},{24,28},{28,24},{32,36},... | collective-permute-start | bytes 3538952 | tf_op jit(solution)/shard_map/ppermute | solution.py:25
  42.7 9.3 %collective-permute-start.13 = (bf16[2,128,1024]{2,1,0:T(8,128)(2,1)S(1)}, bf16[2,128,1024]{2,1,0:T(8,128)(2,1)S(1)}, u32[]{:S(2)}, u32[]{:S(2)}) collective-permute-start(bf16[2,128,1024]{2,1,0:T(8,128)(2,1)S(1)} %broadcast_select_fusion.12), channel_id=1, source_target_pairs={{0,8},{4,28},{8,0},{12,20},{16,24},{20,12},{24,16},{28,4},{32,40},... | collective-permute-start | bytes 1572872 | tf_op jit(solution)/shard_map/ppermute | solution.py:25
  43.4 11.0 %collective-permute-start.14 = (bf16[2,128,1024]{2,1,0:T(8,128)(2,1)}, bf16[2,128,1024]{2,1,0:T(8,128)(2,1)}, u32[]{:S(2)}, u32[]{:S(2)}) collective-permute-start(bf16[2,128,1024]{2,1,0:T(8,128)(2,1)} %broadcast_select_fusion.11), channel_id=1, source_target_pairs={{0,32},{4,100},{8,40},{12,108},{16,48},{20,116},{24,56},{28,124},{... | collective-permute-start | bytes 1572872 | tf_op jit(solution)/shard_map/ppermute | solution.py:25
  43.4 13.1 %collective-permute-start.15 = (bf16[256,1024]{1,0:T(8,128)(2,1)}, bf16[256,1024]{1,0:T(8,128)(2,1)}, u32[]{:S(2)}, u32[]{:S(2)}) collective-permute-start(bf16[256,1024]{1,0:T(8,128)(2,1)} %collective-permute-done.8.refs_2_), channel_id=1, source_target_pairs={{0,1},{1,2},{2,3},{3,0},{4,7},{5,4},{6,5},{7,6},{8,9},{9,10},{10,1... | collective-permute-start | bytes 1572872 | tf_op jit(solution)/shard_map/ppermute | solution.py:35
  44.0 19.6 %collective-permute-start.18 = (bf16[256,1024]{1,0:T(8,128)(2,1)S(1)}, bf16[256,1024]{1,0:T(8,128)(2,1)}, u32[]{:S(2)}, u32[]{:S(2)}) collective-permute-start(bf16[256,1024]{1,0:T(8,128)(2,1)S(1)} %bitcast.57), channel_id=1, source_target_pairs={{0,1},{1,2},{2,3},{3,0},{4,7},{5,4},{6,5},{7,6},{8,9},{9,10},{10,1... | collective-permute-start | bytes 1572872 | tf_op jit(solution)/shard_map/ppermute | solution.py:35
  52.9 10.7 %collective-permute-start.17 = (bf16[2,128,1024]{2,1,0:T(8,128)(2,1)}, bf16[2,128,1024]{2,1,0:T(8,128)(2,1)}, u32[]{:S(2)}, u32[]{:S(2)}) collective-permute-start(bf16[2,128,1024]{2,1,0:T(8,128)(2,1)} %broadcast_select_fusion.10), channel_id=1, source_target_pairs={{0,24},{4,12},{8,16},{12,4},{16,8},{20,28},{24,0},{28,20},{32,56},... | collective-permute-start | bytes 1572872 | tf_op jit(solution)/shard_map/ppermute | solution.py:25
  56.5 12.7 %collective-permute-start.16 = (bf16[2,128,1024]{2,1,0:T(8,128)(2,1)}, bf16[2,128,1024]{2,1,0:T(8,128)(2,1)}, u32[]{:S(2)}, u32[]{:S(2)}) collective-permute-start(bf16[2,128,1024]{2,1,0:T(8,128)(2,1)} %broadcast_select_fusion.7), channel_id=1, source_target_pairs={{0,24},{4,12},{8,16},{12,4},{16,8},{20,28},{24,0},{28,20},{32,56},... | collective-permute-start | bytes 1572872 | tf_op jit(solution)/shard_map/ppermute | solution.py:25
  59.3 1.0 copy-start.1
  63.5 15.3 %collective-permute-start.20 = (bf16[2,128,1536]{2,1,0:T(8,128)(2,1)S(1)}, bf16[2,128,1536]{2,1,0:T(8,128)(2,1)S(1)}, u32[]{:S(2)}, u32[]{:S(2)}) collective-permute-start(bf16[2,128,1536]{2,1,0:T(8,128)(2,1)S(1)} %bitcast.51), channel_id=1, source_target_pairs={{0,32},{4,100},{8,40},{12,108},{16,48},{20,116},{24,56},{28,124},{... | collective-permute-start | bytes 2359304 | tf_op jit(solution)/shard_map/ppermute | solution.py:25
  63.6 10.7 %collective-permute-start.21 = (bf16[256,1024]{1,0:T(8,128)(2,1)}, bf16[256,1024]{1,0:T(8,128)(2,1)S(1)}, u32[]{:S(2)}, u32[]{:S(2)}) collective-permute-start(bf16[256,1024]{1,0:T(8,128)(2,1)} %collective-permute-done.18.refs_1_), channel_id=1, source_target_pairs={{0,1},{1,2},{2,3},{3,0},{4,7},{5,4},{6,5},{7,6},{8,9},{9,10},{10,1... | collective-permute-start | bytes 1572872 | tf_op jit(solution)/shard_map/ppermute | solution.py:35
  66.0 15.2 %collective-permute-start.22 = (bf16[256,1024]{1,0:T(8,128)(2,1)S(1)}, bf16[256,1024]{1,0:T(8,128)(2,1)S(1)}, u32[]{:S(2)}, u32[]{:S(2)}) collective-permute-start(bf16[256,1024]{1,0:T(8,128)(2,1)S(1)} %bitcast.59), channel_id=1, source_target_pairs={{0,1},{1,2},{2,3},{3,0},{4,7},{5,4},{6,5},{7,6},{8,9},{9,10},{10,1... | collective-permute-start | bytes 1572872 | tf_op jit(solution)/shard_map/ppermute | solution.py:35
  70.6 10.5 %collective-permute-start.19 = (bf16[2,128,1024]{2,1,0:T(8,128)(2,1)S(1)}, bf16[2,128,1024]{2,1,0:T(8,128)(2,1)S(1)}, u32[]{:S(2)}, u32[]{:S(2)}) collective-permute-start(bf16[2,128,1024]{2,1,0:T(8,128)(2,1)S(1)} %broadcast_select_fusion.8), channel_id=1, source_target_pairs={{0,96},{4,36},{8,104},{12,44},{16,112},{20,52},{24,120},{28,60},{3... | collective-permute-start | bytes 1572872 | tf_op jit(solution)/shard_map/ppermute | solution.py:25
  74.3 11.2 %collective-permute-start.24 = (bf16[256,1024]{1,0:T(8,128)(2,1)S(1)}, bf16[256,1024]{1,0:T(8,128)(2,1)S(1)}, u32[]{:S(2)}, u32[]{:S(2)}) collective-permute-start(bf16[256,1024]{1,0:T(8,128)(2,1)S(1)} %collective-permute-done.21.refs_2_), channel_id=1, source_target_pairs={{0,1},{1,2},{2,3},{3,0},{4,7},{5,4},{6,5},{7,6},{8,9},{9,10},{10,1... | collective-permute-start | bytes 1572872 | tf_op jit(solution)/shard_map/ppermute | solution.py:35
  79.0 14.1 %collective-permute-start.25 = (bf16[2,128,1536]{2,1,0:T(8,128)(2,1)S(1)}, bf16[2,128,1536]{2,1,0:T(8,128)(2,1)S(1)}, u32[]{:S(2)}, u32[]{:S(2)}) collective-permute-start(bf16[2,128,1536]{2,1,0:T(8,128)(2,1)S(1)} %broadcast_select_fusion.5), channel_id=1, source_target_pairs={{0,96},{4,36},{8,104},{12,44},{16,112},{20,52},{24,120},{28,60},{3... | collective-permute-start | bytes 2359304 | tf_op jit(solution)/shard_map/ppermute | solution.py:25
  81.2 10.6 %collective-permute-start.23 = (bf16[256,1024]{1,0:T(8,128)(2,1)S(1)}, bf16[256,1024]{1,0:T(8,128)(2,1)S(1)}, u32[]{:S(2)}, u32[]{:S(2)}) collective-permute-start(bf16[256,1024]{1,0:T(8,128)(2,1)S(1)} %bitcast.61), channel_id=1, source_target_pairs={{0,1},{1,2},{2,3},{3,0},{4,7},{5,4},{6,5},{7,6},{8,9},{9,10},{10,1... | collective-permute-start | bytes 1572872 | tf_op jit(solution)/shard_map/ppermute | solution.py:35
  91.8 12.0 %collective-permute-start.27 = (bf16[2,128,1536]{2,1,0:T(8,128)(2,1)S(1)}, bf16[2,128,1536]{2,1,0:T(8,128)(2,1)S(1)}, u32[]{:S(2)}, u32[]{:S(2)}) collective-permute-start(bf16[2,128,1536]{2,1,0:T(8,128)(2,1)S(1)} %bitcast.53), channel_id=1, source_target_pairs={{0,32},{4,100},{8,40},{12,108},{16,48},{20,116},{24,56},{28,124},{... | collective-permute-start | bytes 2359304 | tf_op jit(solution)/shard_map/ppermute | solution.py:25
  93.1 10.4 %collective-permute-start.28 = (bf16[256,1024]{1,0:T(8,128)(2,1)S(1)}, bf16[256,1024]{1,0:T(8,128)(2,1)S(1)}, u32[]{:S(2)}, u32[]{:S(2)}) collective-permute-start(bf16[256,1024]{1,0:T(8,128)(2,1)S(1)} %collective-permute-done.22.refs_1_), channel_id=1, source_target_pairs={{0,1},{1,2},{2,3},{3,0},{4,7},{5,4},{6,5},{7,6},{8,9},{9,10},{10,1... | collective-permute-start | bytes 1572872 | tf_op jit(solution)/shard_map/ppermute | solution.py:35
  93.2 17.4 %collective-permute-start.31 = (bf16[2,128,1536]{2,1,0:T(8,128)(2,1)S(1)}, bf16[2,128,1536]{2,1,0:T(8,128)(2,1)S(1)}, u32[]{:S(2)}, u32[]{:S(2)}) collective-permute-start(bf16[2,128,1536]{2,1,0:T(8,128)(2,1)S(1)} %broadcast_select_fusion.4), channel_id=1, source_target_pairs={{0,8},{4,28},{8,0},{12,20},{16,24},{20,12},{24,16},{28,4},{32,40},... | collective-permute-start | bytes 2359304 | tf_op jit(solution)/shard_map/ppermute | solution.py:25
  93.3 15.8 %collective-permute-start.26 = (bf16[256,1024]{1,0:T(8,128)(2,1)S(1)}, bf16[256,1024]{1,0:T(8,128)(2,1)S(1)}, u32[]{:S(2)}, u32[]{:S(2)}) collective-permute-start(bf16[256,1024]{1,0:T(8,128)(2,1)S(1)} %collective-permute-done.23.refs_1_), channel_id=1, source_target_pairs={{0,1},{1,2},{2,3},{3,0},{4,7},{5,4},{6,5},{7,6},{8,9},{9,10},{10,1... | collective-permute-start | bytes 1572872 | tf_op jit(solution)/shard_map/ppermute | solution.py:35
  103.5 11.2 %collective-permute-start.30 = (bf16[256,1024]{1,0:T(8,128)(2,1)S(1)}, bf16[256,1024]{1,0:T(8,128)(2,1)S(1)}, u32[]{:S(2)}, u32[]{:S(2)}) collective-permute-start(bf16[256,1024]{1,0:T(8,128)(2,1)S(1)} %collective-permute-done.28.refs_2_), channel_id=1, source_target_pairs={{0,1},{1,2},{2,3},{3,0},{4,7},{5,4},{6,5},{7,6},{8,9},{9,10},{10,1... | collective-permute-start | bytes 1572872 | tf_op jit(solution)/shard_map/ppermute | solution.py:35
  109.1 11.2 %collective-permute-start.29 = (bf16[256,1024]{1,0:T(8,128)(2,1)S(1)}, bf16[256,1024]{1,0:T(8,128)(2,1)S(1)}, u32[]{:S(2)}, u32[]{:S(2)}) collective-permute-start(bf16[256,1024]{1,0:T(8,128)(2,1)S(1)} %collective-permute-done.26.refs_2_), channel_id=1, source_target_pairs={{0,1},{1,2},{2,3},{3,0},{4,7},{5,4},{6,5},{7,6},{8,9},{9,10},{10,1... | collective-permute-start | bytes 1572872 | tf_op jit(solution)/shard_map/ppermute | solution.py:35
  109.1 15.2 %collective-permute-start.33 = (bf16[2,128,1536]{2,1,0:T(8,128)(2,1)S(1)}, bf16[2,128,1536]{2,1,0:T(8,128)(2,1)S(1)}, u32[]{:S(2)}, u32[]{:S(2)}) collective-permute-start(bf16[2,128,1536]{2,1,0:T(8,128)(2,1)S(1)} %broadcast_select_fusion.3), channel_id=1, source_target_pairs={{0,96},{4,36},{8,104},{12,44},{16,112},{20,52},{24,120},{28,60},{3... | collective-permute-start | bytes 2359304 | tf_op jit(solution)/shard_map/ppermute | solution.py:25
  110.8 13.7 %collective-permute-start.32 = (bf16[2,128,1536]{2,1,0:T(8,128)(2,1)S(1)}, bf16[2,128,1536]{2,1,0:T(8,128)(2,1)S(1)}, u32[]{:S(2)}, u32[]{:S(2)}) collective-permute-start(bf16[2,128,1536]{2,1,0:T(8,128)(2,1)S(1)} %broadcast_select_fusion.2), channel_id=1, source_target_pairs={{0,24},{4,12},{8,16},{12,4},{16,8},{20,28},{24,0},{28,20},{32,56},... | collective-permute-start | bytes 2359304 | tf_op jit(solution)/shard_map/ppermute | solution.py:25
